TPU v7x, 256 devices: a whole 4x4x8 slice. The times are simulated.
256 devices in a mesh: dp: 16 (over x, z_hi, core), mp: 16 (over y, z_lo).
Axes of the slice: x: 4, y: 4, z: 8 (z_hi: 2, z_lo: 4; z = z_hi * 4 + z_lo), core: 2. Of those that a mesh axis runs over, the one named last changes fastest.
Arguments:
- weight_gate: bfloat16 [8192, 16384], P(('dp', 'mp')), may hold values from -6 to 6
- weight_up: bfloat16 [8192, 16384], P(('dp', 'mp')), may hold values from -6 to 6
- grad_gate: bfloat16 [8192, 16384], P(('dp', 'mp')), may hold values from -6 to 6
- grad_up: bfloat16 [8192, 16384], P(('dp', 'mp')), may hold values from -6 to 6
- moment_gate: bfloat16 [8192, 16384], P(('dp', 'mp')), may hold values from -4 to 4
- moment_up: bfloat16 [8192, 16384], P(('dp', 'mp')), may hold values from -4 to 4
- second_gate: bfloat16 [8192, 16384], P(('dp', 'mp')), may hold values from 0.0099487305 to 1
- second_up: bfloat16 [8192, 16384], P(('dp', 'mp')), may hold values from 0.0099487305 to 1
- layer_input: bfloat16 [4, 512, 8192], P(None, ('dp', 'mp')), may hold values from -6 to 6
- queries: bfloat16 [4, 512, 8192], P(None, ('dp', 'mp')), may hold values from -160 to 160
- fresh_keys: bfloat16 [4, 512, 1024], P(None, ('dp', 'mp')), may hold values from -16 to 16
- fresh_values: bfloat16 [4, 512, 1024], P(None, ('dp', 'mp')), may hold values from -16 to 16
- cached_keys: bfloat16 [512, 128, 1024], P(('dp', 'mp')), may hold values from -6 to 6
- cached_values: bfloat16 [512, 128, 1024], P(('dp', 'mp')), may hold values from -16 to 16
- lengths: int32 [512], P(('dp', 'mp')), may hold values from 2 to 128, as said below
- norm_gain: bfloat16 [8192], replicated, may hold values from 0.099609375 to 1.8984375
Outputs:
- gate_new: bfloat16 [8192, 16384], P('dp', 'mp')
- up_new: bfloat16 [8192, 16384], P('dp', 'mp')
- hidden: bfloat16 [4, 512, 16384], P(None, 'dp', 'mp')
Inputs may be any that keep to these rules, and one draw needn't show every extreme that they name: `lengths`: every row has at least 2 cached positions and some row has exactly 128.
All inputs are finite; a program needn't handle non-finite values.
Results may differ from a plain program's by a relative error of at most 0.035.
Values may be sent and summed in bfloat16 or wider, within the bound.
No kernel may reach another device: no remote copies, remote signals or barrier semaphores. Data moves between devices by JAX's collectives and lax.ppermute only.
A program may use at most 128 MiB of HBM per device.

v0:
```python
import jax
import jax.numpy as jnp
from jax import lax
from jax.sharding import PartitionSpec as P

D = 8192
HD = 128
KVH = 8
GROUP = 8
CTX = 128
STEPS = 4


beta_one = 0.9
beta_two = 0.95
learn_rate = 0.15
weight_decay = 0.1
adam_eps = 1e-08
first_fix = 1.0 - 0.9**10
second_fix = 1.0 - 0.95**10


def adamw_step(weight, gradient, moment, second):
    weight_f = weight.astype(jnp.float32)
    grad_f = gradient.astype(jnp.float32)
    moment_next = beta_one * moment.astype(jnp.float32) + (1.0 - beta_one) * grad_f
    second_next = beta_two * second.astype(jnp.float32) + (1.0 - beta_two) * grad_f * grad_f
    update = moment_next / first_fix / (jnp.sqrt(second_next / second_fix) + adam_eps)
    return (weight_f - learn_rate * (update + weight_decay * weight_f)).astype(jnp.bfloat16)


def attend(query_row, fresh_k, fresh_v, cache_k, cache_v, length_row):
    row_count = query_row.shape[0]
    fresh_count = fresh_k.shape[0]
    scaled = query_row.astype(jnp.float32).reshape(row_count, KVH, GROUP, HD) * HD ** (-0.5)
    keys_old = cache_k.astype(jnp.float32).reshape(row_count, CTX, KVH, HD)
    values_old = cache_v.astype(jnp.float32).reshape(row_count, CTX, KVH, HD)
    keys_new = fresh_k.astype(jnp.float32).reshape(fresh_count, row_count, KVH, HD)
    values_new = fresh_v.astype(jnp.float32).reshape(fresh_count, row_count, KVH, HD)
    scores_old = jnp.einsum("rgjd,rpgd->rgjp", scaled, keys_old)
    visible = jnp.arange(CTX)[None, :] < length_row[:, None]
    scores_old = jnp.where(visible[:, None, None, :], scores_old, jnp.float32(-1e30))
    scores_new = jnp.einsum("rgjd,srgd->rgjs", scaled, keys_new)
    peak_score = jnp.maximum(jnp.max(scores_old, axis=-1), jnp.max(scores_new, axis=-1))[..., None]
    exp_old = jnp.exp(scores_old - peak_score)
    exp_new = jnp.exp(scores_new - peak_score)
    totals = jnp.sum(exp_old, axis=-1, keepdims=True) + jnp.sum(exp_new, axis=-1, keepdims=True)
    probs_old = lax.optimization_barrier((exp_old / totals).astype(jnp.bfloat16)).astype(
        jnp.float32
    )
    probs_new = lax.optimization_barrier((exp_new / totals).astype(jnp.bfloat16)).astype(
        jnp.float32
    )
    attended = jnp.einsum("rgjp,rpgd->rgjd", probs_old, values_old) + jnp.einsum(
        "rgjs,srgd->rgjd", probs_new, values_new
    )
    return attended.reshape(row_count, KVH * GROUP * HD)


def rms_normed(residual_in, attended, norm_scale):
    summed_in = residual_in.astype(jnp.float32) + attended
    factor = lax.rsqrt(jnp.mean(summed_in * summed_in, axis=-1, keepdims=True) + 1e-06)
    return (summed_in * factor * norm_scale).astype(jnp.bfloat16)


def local(
    weight_gate,
    weight_up,
    grad_gate,
    grad_up,
    moment_gate,
    moment_up,
    second_gate,
    second_up,
    layer_input,
    queries,
    fresh_keys,
    fresh_values,
    cached_keys,
    cached_values,
    lengths,
    norm_gain,
):
    gate_step = adamw_step(weight_gate, grad_gate, moment_gate, second_gate)
    up_step = adamw_step(weight_up, grad_up, moment_up, second_up)
    gate_new, up_new = (
        lax.all_to_all(gate_step, "mp", split_axis=1, concat_axis=0, tiled=True),
        lax.all_to_all(up_step, "mp", split_axis=1, concat_axis=0, tiled=True),
    )
    width_cols = gate_new.shape[1]
    joined = jnp.concatenate([gate_new, up_new], axis=1)
    norm_scale = norm_gain.astype(jnp.float32)
    outputs = []
    for step_idx in range(STEPS):
        attended = attend(
            queries[step_idx],
            fresh_keys[: step_idx + 1],
            fresh_values[: step_idx + 1],
            cached_keys,
            cached_values,
            lengths,
        )
        normed = rms_normed(layer_input[step_idx], attended, norm_scale)
        grouped = lax.all_gather(normed, "mp", axis=0, tiled=True)
        spread = lax.all_to_all(grouped, "dp", split_axis=1, concat_axis=0, tiled=True)
        summed = lax.psum_scatter(
            (jnp.dot(spread, joined, preferred_element_type=jnp.float32) * D ** (-0.5)).astype(
                jnp.bfloat16
            ),
            "dp",
            scatter_dimension=0,
            tiled=True,
        ).astype(jnp.float32)
        outputs.append(
            (jax.nn.silu(summed[:, :width_cols]) * summed[:, width_cols:]).astype(jnp.bfloat16)
        )
    return (gate_new, up_new, jnp.stack(outputs))


def solution(mesh):
    in_specs = (
        P(("dp", "mp"), None),
        P(("dp", "mp"), None),
        P(("dp", "mp"), None),
        P(("dp", "mp"), None),
        P(("dp", "mp"), None),
        P(("dp", "mp"), None),
        P(("dp", "mp"), None),
        P(("dp", "mp"), None),
        P(None, ("dp", "mp"), None),
        P(None, ("dp", "mp"), None),
        P(None, ("dp", "mp"), None),
        P(None, ("dp", "mp"), None),
        P(("dp", "mp"), None, None),
        P(("dp", "mp"), None, None),
        P(("dp", "mp")),
        P(),
    )
    out_specs = (P("dp", "mp"), P("dp", "mp"), P(None, "dp", "mp"))
    return jax.shard_map(local, mesh=mesh, in_specs=in_specs, out_specs=out_specs, check_vma=False)
```

profile of v0, /device:TPU:32, one launch (start us, length us, event | category | flops | bytes accessed | tf_op | source)
XLA Modules:
  0.0 524.2 jit_solution(5096444039216901043)
XLA Ops:
  7.2 1.0 multiply_bitcast_fusion.3
  8.3 0.7 iota_compare_fusion
  9.0 0.7 slice.80
  9.7 0.2 fusion.114
  9.9 0.4 fusion.113
  10.4 0.2 fusion.93
  10.6 0.1 divide_convert_fusion.1
  10.8 0.7 reshape.236
  11.5 0.4 fusion.115
  12.0 0.2 fusion.116
  12.1 0.2 fusion.94
  12.4 0.1 divide_convert_fusion
  12.6 0.4 fusion.111
  13.1 0.2 fusion.112
  13.2 0.2 fusion.92
  13.8 0.2 fusion.22
  14.0 0.3 fusion.20
  14.3 0.3 fusion.24
  14.6 0.4 fusion.110
  15.0 0.1 fusion.76
  15.2 0.2 fusion.91
  15.4 0.1 divide_convert_fusion.3
  15.5 0.3 fusion.65
  15.9 0.3 fusion.60
  16.2 0.3 fusion.70
  16.5 0.3 fusion.75
  16.8 0.3 fusion.98
  17.1 42.8 %all-gather = bf16[16,2,8192]{2,1,0:T(2,128)(2,1)S(1)} all-gather(bf16[1,2,8192]{2,1,0:T(2,128)(2,1)S(1)} %get-tuple-element.3), channel_id=1, replica_groups=mesh['dp'=16,'mp'=16] {'mp'}, dimensions={0}, use_global_device_ids=true | all-gather | bytes 557056 | tf_op jit(solution)/shard_map/all_gather | solution.py:104
  59.9 0.4 all_to_all.92
  60.3 1.1 copy.71
  61.4 9.7 %all-to-all-start.2 = ((bf16[32,16,512]{2,0,1:T(8,128)(2,1)}), bf16[32,16,512]{2,0,1:T(8,128)(2,1)S(1)}, u32[]{:S(2)}, u32[]{:S(2)}) async-start(bf16[32,16,512]{2,0,1:T(8,128)(2,1)} %copy.71), calls=%async_computation.2 | async-start | bytes 1048576 | tf_op jit(solution)/shard_map/all_to_all | solution.py:105
  71.0 3.7 fusion.2
  74.8 1.1 copy.238
  75.8 11.8 %all-to-all-done.2 = bf16[32,16,512]{2,0,1:T(8,128)(2,1)S(1)} async-done(((bf16[32,16,512]{2,0,1:T(8,128)(2,1)}), bf16[32,16,512]{2,0,1:T(8,128)(2,1)S(1)}, u32[]{:S(2)}, u32[]{:S(2)}) %all-to-all-start.2) | async-done | bytes 524320 | tf_op jit(solution)/shard_map/all_to_all | solution.py:105
  87.7 7.0 %all-to-all-start = ((bf16[32,16,1024]{2,0,1:T(8,128)(2,1)}), bf16[32,16,1024]{2,0,1:T(8,128)(2,1)S(1)}, u32[]{:S(2)}, u32[]{:S(2)}) async-start(bf16[32,16,1024]{2,0,1:T(8,128)(2,1)} %bitcast.281), calls=%async_computation | async-start | bytes 2097152 | tf_op jit(solution)/shard_map/all_to_all | solution.py:87
  94.7 4.0 fusion.8
  98.7 1.1 copy.237
  99.8 18.7 %all-to-all-done = bf16[32,16,1024]{2,0,1:T(8,128)(2,1)S(1)} async-done(((bf16[32,16,1024]{2,0,1:T(8,128)(2,1)}), bf16[32,16,1024]{2,0,1:T(8,128)(2,1)S(1)}, u32[]{:S(2)}, u32[]{:S(2)}) %all-to-all-start) | async-done | bytes 1048608 | tf_op jit(solution)/shard_map/all_to_all | solution.py:87
  118.5 33.4 %all_to_all.114 = bf16[32,16,1024]{2,0,1:T(8,128)(2,1)S(1)} all-to-all(bf16[32,16,1024]{2,0,1:T(8,128)(2,1)} %bitcast.295), channel_id=1, replica_groups=mesh['dp'=16,'mp'=16] {'mp'}, dimensions={1} | all-to-all | bytes 2097152 | tf_op jit(solution)/shard_map/all_to_all | solution.py:88
  151.9 2.6 multiply_convert_fusion.3
  154.6 44.2 %all-gather.1 = bf16[16,2,8192]{2,1,0:T(2,128)(2,1)S(1)} all-gather(bf16[1,2,8192]{2,1,0:T(2,128)(2,1)S(1)} %get-tuple-element.4), channel_id=1, replica_groups=mesh['dp'=16,'mp'=16] {'mp'}, dimensions={0}, use_global_device_ids=true | all-gather | bytes 557056 | tf_op jit(solution)/shard_map/all_gather | solution.py:104
  198.8 1.2 all_to_all.96
  199.9 1.3 copy.76
  201.3 23.6 %all_to_all.115 = bf16[32,16,512]{2,0,1:T(8,128)(2,1)S(1)} all-to-all(bf16[32,16,512]{2,0,1:T(8,128)(2,1)S(1)} %copy.76), channel_id=1, replica_groups=mesh['dp'=16,'mp'=16] {'dp'}, dimensions={1} | all-to-all | bytes 1048576 | tf_op jit(solution)/shard_map/all_to_all | solution.py:105
  224.9 2.6 multiply_convert_fusion.2
  227.5 43.0 %all-gather.2 = bf16[16,2,8192]{2,1,0:T(2,128)(2,1)S(1)} all-gather(bf16[1,2,8192]{2,1,0:T(2,128)(2,1)S(1)} %get-tuple-element.5), channel_id=1, replica_groups=mesh['dp'=16,'mp'=16] {'mp'}, dimensions={0}, use_global_device_ids=true | all-gather | bytes 557056 | tf_op jit(solution)/shard_map/all_gather | solution.py:104
  270.6 1.2 all_to_all.100
  271.7 1.3 copy.81
  273.1 27.1 %all_to_all.116 = bf16[32,16,512]{2,0,1:T(8,128)(2,1)S(1)} all-to-all(bf16[32,16,512]{2,0,1:T(8,128)(2,1)S(1)} %copy.81), channel_id=1, replica_groups=mesh['dp'=16,'mp'=16] {'dp'}, dimensions={1} | all-to-all | bytes 1048576 | tf_op jit(solution)/shard_map/all_to_all | solution.py:105
  300.1 2.6 multiply_convert_fusion.1
  302.8 50.2 %all-gather.3 = bf16[16,2,8192]{2,1,0:T(2,128)(2,1)S(1)} all-gather(bf16[1,2,8192]{2,1,0:T(2,128)(2,1)S(1)} %get-tuple-element.6), channel_id=1, replica_groups=mesh['dp'=16,'mp'=16] {'mp'}, dimensions={0}, use_global_device_ids=true | all-gather | bytes 557056 | tf_op jit(solution)/shard_map/all_gather | solution.py:104
  353.0 1.2 all_to_all.104
  354.1 1.4 copy.86
  355.5 24.3 %all_to_all.117 = bf16[32,16,512]{2,0,1:T(8,128)(2,1)S(1)} all-to-all(bf16[32,16,512]{2,0,1:T(8,128)(2,1)S(1)} %copy.86), channel_id=1, replica_groups=mesh['dp'=16,'mp'=16] {'dp'}, dimensions={1} | all-to-all | bytes 1048576 | tf_op jit(solution)/shard_map/all_to_all | solution.py:105
  379.8 2.6 multiply_convert_fusion
  382.5 0.9 convert_element_type.221
  383.5 0.9 convert_element_type.232
  384.4 42.0 %reduce-scatter.9.cloned.1.call-done = bf16[32,2048]{1,0:T(8,128)(2,1)} async-done(((bf16[512,2048]{1,0:T(8,128)(2,1)}), bf16[32,2048]{1,0:T(8,128)(2,1)}) %reduce-scatter.9.cloned.1.call-update) | async-done | bytes 131088 | tf_op jit(solution)/shard_map/reduce_scatter | solution.py:106
  426.4 0.9 convert_element_type.243
  427.5 86.5 %reduce-scatter.11.cloned.1.call-done = bf16[32,2048]{1,0:T(8,128)(2,1)} async-done(((bf16[512,2048]{1,0:T(8,128)(2,1)}), bf16[32,2048]{1,0:T(8,128)(2,1)}) %reduce-scatter.11.cloned.1.call-update) | async-done | bytes 131088 | tf_op jit(solution)/shard_map/reduce_scatter | solution.py:106
  514.0 0.9 convert_element_type.254
  515.0 0.7 pad_maximum_fusion.1
  515.7 1.0 copy.242
  516.7 1.0 copy.243
  (62 shorter events, 1.1 us)
Async XLA Ops:
  7.2 2.7 copy-start
  7.2 5.9 %slice-start = ((bf16[4,2,1024]{2,1,0:T(2,128)(2,1)}), bf16[2,2,1024]{2,1,0:T(2,128)(2,1)S(1)}, s32[]{:S(2)}) async-start(bf16[4,2,1024]{2,1,0:T(2,128)(2,1)} %param.26), calls=%async_computation.14 | async-start | bytes 16384 | tf_op jit(solution)/shard_map/slice | solution.py:97
  7.2 5.3 %copy-start.4 = (bf16[4,2,1024]{2,1,0:T(2,128)(2,1)S(1)}, bf16[4,2,1024]{2,1,0:T(2,128)(2,1)}, u32[]{:S(2)}) copy-start(bf16[4,2,1024]{2,1,0:T(2,128)(2,1)} %param.27) | copy-start | bytes 49156
  7.2 6.5 %slice-start.2 = ((bf16[4,2,1024]{2,1,0:T(2,128)(2,1)}), bf16[3,2,1024]{2,1,0:T(2,128)(2,1)S(1)}, s32[]{:S(2)}) async-start(bf16[4,2,1024]{2,1,0:T(2,128)(2,1)} %param.27), calls=%async_computation.16 | async-start | bytes 24576 | tf_op jit(solution)/shard_map/slice | solution.py:98
  7.2 6.4 %copy-start.3 = (bf16[4,2,8192]{2,1,0:T(2,128)(2,1)S(1)}, bf16[4,2,8192]{2,1,0:T(2,128)(2,1)}, u32[]{:S(2)}) copy-start(bf16[4,2,8192]{2,1,0:T(2,128)(2,1)} %param.24) | copy-start | bytes 393220
  7.2 6.6 %copy-start.1 = (bf16[2,128,1024]{2,1,0:T(8,128)(2,1)S(1)}, bf16[2,128,1024]{2,1,0:T(8,128)(2,1)}, u32[]{:S(2)}) copy-start(bf16[2,128,1024]{2,1,0:T(8,128)(2,1)} %param.29) | copy-start | bytes 1572868
  12.0 2.6 slice-start.3
  12.5 2.5 slice-start.1
  12.6 3.0 copy-start.5
  16.8 54.2 %copy-start.2 = (bf16[32,16384]{1,0:T(8,128)(2,1)S(1)}, bf16[32,16384]{1,0:T(8,128)(2,1)}, u32[]{:S(2)}) copy-start(bf16[32,16384]{1,0:T(8,128)(2,1)} %param.16) | copy-start | bytes 3145732
  61.4 26.3 %all-to-all-start.2 = ((bf16[32,16,512]{2,0,1:T(8,128)(2,1)}), bf16[32,16,512]{2,0,1:T(8,128)(2,1)S(1)}, u32[]{:S(2)}, u32[]{:S(2)}) async-start(bf16[32,16,512]{2,0,1:T(8,128)(2,1)} %copy.71), calls=%async_computation.2 | async-start | bytes 1048576 | tf_op jit(solution)/shard_map/all_to_all | solution.py:105
  87.7 30.8 %all-to-all-start = ((bf16[32,16,1024]{2,0,1:T(8,128)(2,1)}), bf16[32,16,1024]{2,0,1:T(8,128)(2,1)S(1)}, u32[]{:S(2)}, u32[]{:S(2)}) async-start(bf16[32,16,1024]{2,0,1:T(8,128)(2,1)} %bitcast.281), calls=%async_computation | async-start | bytes 2097152 | tf_op jit(solution)/shard_map/all_to_all | solution.py:87
  94.6 287.9 %reduce-scatter.5.cloned.1.call-start = ((), (), s32[]{:S(2)}) async-start(), calls=%async_computation.10 | async-start | bytes 2228224 | tf_op jit(solution)/shard_map/reduce_scatter | solution.py:106
  154.5 228.9 %reduce-scatter.7.cloned.1.call-start = ((), (), s32[]{:S(2)}) async-start(), calls=%async_computation.11 | async-start | bytes 2228224 | tf_op jit(solution)/shard_map/reduce_scatter | solution.py:106
  227.5 198.9 %reduce-scatter.9.cloned.1.call-start = ((), (), s32[]{:S(2)}) async-start(), calls=%async_computation.12 | async-start | bytes 2228224 | tf_op jit(solution)/shard_map/reduce_scatter | solution.py:106
  302.7 211.3 %reduce-scatter.11.cloned.1.call-start = ((), (), s32[]{:S(2)}) async-start(), calls=%async_computation.13 | async-start | bytes 2228224 | tf_op jit(solution)/shard_map/reduce_scatter | solution.py:106
Sparse Core Ops, SparseCore 0:
  154.7 88.9 reduce-scatter.4
  247.9 91.2 reduce-scatter.6
  343.4 82.9 reduce-scatter.8
  430.5 83.4 reduce-scatter.10
where the time goes:
time: 527 us; the launch traced here: 524 us
  blocking collectives  289 us (55%)
  waiting for transfers between devices  159 us (30%)
  starting transfers between devices  16.8 us (3%)
  other arithmetic  16 us (3%)
  matrix products  14.8 us (3%)
  local copies, waits for them, and re-layouts  14.6 us (3%)
  between operations  14.2 us (3%)
    all_gather x4, blocking collectives, local(): grouped = lax.all_gather(normed, 'mp', axis=0, tiled=True)  180 us
    reduce_scatter x4, waiting for transfers between devices, local(): lax.psum_scatter((jnp.dot(spread, joined, preferred_element_type=jnp.floa...  129 us
    all_to_all x3, blocking collectives, local(): lax.all_to_all(grouped, 'dp', split_axis=1, concat_axis=0, tiled=True)  75 us
    all_to_all x1, blocking collectives, local(): lax.all_to_all(up_step, 'mp', split_axis=1, concat_axis=0, tiled=True)  33.4 us
    all_to_all x1, waiting for transfers between devices, local(): lax.all_to_all(gate_step, 'mp', split_axis=1, concat_axis=0, tiled=True)  18.7 us
    all_to_all x1, waiting for transfers between devices, local(): lax.all_to_all(grouped, 'dp', split_axis=1, concat_axis=0, tiled=True)  11.8 us
  transfers between devices with their start and end apart: 6, of which 4 were waited for; matrix products, arithmetic and copies ran while one was open for 5% of the time, Pallas kernels for 0%

commit v1 on v0

v1 whole, which is shorter than its diff:
```python
import functools

import jax
import jax.numpy as jnp
from jax import lax
from jax.experimental import pallas as pl
from jax.experimental.pallas import tpu as pltpu
from jax.sharding import PartitionSpec as P

D = 8192
HD = 128
KVH = 8
GROUP = 8
CTX = 128
STEPS = 4
ROWS_HERE = 2

GRAY = (0, 1, 3, 2)

beta_one = 0.9
beta_two = 0.95
learn_rate = 0.15
weight_decay = 0.1
adam_eps = 1e-08
first_fix = 1.0 - 0.9**10
second_fix = 1.0 - 0.95**10


def dp_swap(flip_x, flip_z, flip_core):
    pairs = []
    for dp in range(16):
        x, z_hi, core = dp // 4, dp // 2 % 2, dp % 2
        x_to = GRAY[GRAY[x] ^ flip_x]
        pairs.append((dp, x_to * 4 + (z_hi ^ flip_z) * 2 + (core ^ flip_core)))
    return pairs


def mp_swap(flip_y, flip_z):
    pairs = []
    for mp in range(16):
        y, z_lo = mp // 4, mp % 4
        pairs.append((mp, GRAY[GRAY[y] ^ flip_y] * 4 + (z_lo ^ flip_z)))
    return pairs


def adam_kernel(weight_ref, grad_ref, moment_ref, second_ref, out_ref):
    width = out_ref.shape[2]
    for part in range(out_ref.shape[0]):
        cols = slice(part * width, (part + 1) * width)
        weight_f = weight_ref[:, cols].astype(jnp.float32)
        grad_f = grad_ref[:, cols].astype(jnp.float32)
        moment_next = (
            beta_one * moment_ref[:, cols].astype(jnp.float32) + (1.0 - beta_one) * grad_f
        )
        second_next = (
            beta_two * second_ref[:, cols].astype(jnp.float32)
            + (1.0 - beta_two) * grad_f * grad_f
        )
        update = moment_next / first_fix / (jnp.sqrt(second_next / second_fix) + adam_eps)
        new = weight_f - learn_rate * (update + weight_decay * weight_f)
        out_ref[part] = new.astype(jnp.bfloat16)


def adam_blocks(weight, gradient, moment, second):
    rows, cols = weight.shape
    width = cols // 16
    per_step = 2
    spec = pl.BlockSpec((rows, per_step * width), lambda i: (0, i))
    return pl.pallas_call(
        adam_kernel,
        grid=(16 // per_step,),
        in_specs=[spec] * 4,
        out_specs=pl.BlockSpec((per_step, rows, width), lambda i: (i, 0, 0)),
        out_shape=jax.ShapeDtypeStruct((16, rows, width), jnp.bfloat16),
        cost_estimate=pl.CostEstimate(
            flops=20 * rows * cols, bytes_accessed=10 * rows * cols, transcendentals=2 * rows * cols
        ),
        name="adam",
    )(weight, gradient, moment, second)


def attend_all(queries, fresh_keys, fresh_values, cached_keys, cached_values, lengths):
    q = queries.reshape(STEPS, ROWS_HERE, KVH, GROUP, HD)
    keys_old = cached_keys.reshape(ROWS_HERE, CTX, KVH, HD)
    values_old = cached_values.reshape(ROWS_HERE, CTX, KVH, HD)
    keys_new = fresh_keys.reshape(STEPS, ROWS_HERE, KVH, HD)
    values_new = fresh_values.reshape(STEPS, ROWS_HERE, KVH, HD)
    scale = HD ** (-0.5)
    scores_old = scale * jnp.einsum(
        "srgjd,rpgd->rgsjp", q, keys_old, preferred_element_type=jnp.float32
    )
    scores_new = scale * jnp.einsum(
        "srgjd,trgd->rgsjt", q, keys_new, preferred_element_type=jnp.float32
    )
    visible = jnp.arange(CTX)[None, :] < lengths[:, None]
    scores_old = jnp.where(visible[:, None, None, None, :], scores_old, jnp.float32(-1e30))
    causal = jnp.arange(STEPS)[None, :] <= jnp.arange(STEPS)[:, None]
    scores_new = jnp.where(causal[None, None, :, None, :], scores_new, jnp.float32(-1e30))
    peak = jnp.maximum(jnp.max(scores_old, axis=-1), jnp.max(scores_new, axis=-1))[..., None]
    exp_old = jnp.exp(scores_old - peak)
    exp_new = jnp.exp(scores_new - peak)
    totals = jnp.sum(exp_old, axis=-1, keepdims=True) + jnp.sum(exp_new, axis=-1, keepdims=True)
    probs_old = (exp_old / totals).astype(jnp.bfloat16)
    probs_new = (exp_new / totals).astype(jnp.bfloat16)
    attended = jnp.einsum(
        "rgsjp,rpgd->srgjd", probs_old, values_old, preferred_element_type=jnp.float32
    ) + jnp.einsum("rgsjt,trgd->srgjd", probs_new, values_new, preferred_element_type=jnp.float32)
    return attended.reshape(STEPS, ROWS_HERE, D)


def product_kernel(chip_ref, *refs):
    row_refs = refs[:4]
    own_ref, other_ref, send_a, keep_a, send_b, keep_b = refs[4:]
    half = own_ref.shape[1] // 2
    depth = own_ref.shape[0]
    gray_here, z_here = chip_ref[0], chip_ref[1]
    for flip in (3, 1, 2, 0):
        gray = gray_here ^ flip
        x = gray ^ (gray >> 1)
        rows = jnp.concatenate(
            [ref[x * 2 + (z_here ^ flip_z)] for flip_z in range(2) for ref in row_refs], axis=0
        )
        total = jnp.dot(rows[:, :depth], own_ref[...], preferred_element_type=jnp.float32)
        total += jnp.dot(rows[:, depth:], other_ref[...], preferred_element_type=jnp.float32)
        term = (total * D ** (-0.5)).astype(jnp.bfloat16).reshape(2, 128, 2 * half)
        (send_a if flip & 1 else keep_a)[flip >> 1] = term[:, :, :half]
        (send_b if flip & 2 else keep_b)[flip & 1] = term[:, :, half:]


def products(chip, row_parts, own, other):
    half = own.shape[1] // 2
    out = jax.ShapeDtypeStruct((2, 2, 128, half), jnp.bfloat16)
    vmem = pl.BlockSpec(memory_space=pltpu.VMEM)
    return pl.pallas_call(
        product_kernel,
        in_specs=[pl.BlockSpec(memory_space=pltpu.SMEM)] + [vmem] * 6,
        out_specs=[vmem] * 4,
        out_shape=[out] * 4,
        compiler_params=pltpu.CompilerParams(vmem_limit_bytes=32 * 2**20),
        cost_estimate=pl.CostEstimate(
            flops=2 * 1024 * 1024 * 1024, bytes_accessed=6 * 2**20, transcendentals=0
        ),
        name="products",
    )(chip, *row_parts, own, other)


def add(kept, arrived):
    return kept.astype(jnp.float32) + arrived.astype(jnp.float32)


def scatter_sums(parts):
    send_a, keep_a, send_b, keep_b = parts
    got_a = lax.ppermute(send_a, "dp", dp_swap(1, 0, 0))
    got_b = lax.ppermute(send_b, "dp", dp_swap(2, 0, 0))
    sum_a = add(keep_a, got_a)
    sum_b = add(keep_b, got_b)
    got_a = lax.ppermute(sum_a[1].astype(jnp.bfloat16), "dp", dp_swap(2, 0, 0))
    got_b = lax.ppermute(sum_b[1].astype(jnp.bfloat16), "dp", dp_swap(1, 0, 0))
    sum_a = add(sum_a[0], got_a)
    sum_b = add(sum_b[0], got_b)
    both = jnp.concatenate([sum_a, sum_b], axis=-1)
    got = lax.ppermute(both[1].astype(jnp.bfloat16), "dp", dp_swap(0, 1, 0))
    return add(both[0], got)


def local(
    weight_gate,
    weight_up,
    grad_gate,
    grad_up,
    moment_gate,
    moment_up,
    second_gate,
    second_up,
    layer_input,
    queries,
    fresh_keys,
    fresh_values,
    cached_keys,
    cached_values,
    lengths,
    norm_gain,
):
    dp = lax.axis_index("dp")
    mp = lax.axis_index("mp")
    x, z_hi, core = dp // 4, dp // 2 % 2, dp % 2
    y, z_lo = mp // 4, mp % 4
    chip = jnp.stack([x ^ (x >> 1), z_hi]).astype(jnp.int32)

    attended = attend_all(
        queries, fresh_keys, fresh_values, cached_keys, cached_values, lengths
    )
    summed_in = layer_input.astype(jnp.float32) + attended
    factor = lax.rsqrt(jnp.mean(summed_in * summed_in, axis=-1, keepdims=True) + 1e-06)
    normed = (summed_in * factor * norm_gain.astype(jnp.float32)).astype(jnp.bfloat16)
    halves = normed.reshape(8, 8, 2, 512).transpose(1, 2, 0, 3)
    halves = jnp.where(core == 0, halves, halves[:, ::-1])
    blocks = halves.transpose(0, 2, 1, 3).reshape(8, 8, 1024)
    gate_step = adam_blocks(weight_gate, grad_gate, moment_gate, second_gate)
    up_step = adam_blocks(weight_up, grad_up, moment_up, second_up)

    groups = [[2 * chip_at + kind for chip_at in range(8)] for kind in range(2)]
    spread = lax.all_to_all(
        blocks, "dp", split_axis=0, concat_axis=0, axis_index_groups=groups, tiled=True
    )
    along_z = [spread] + [lax.ppermute(spread, "mp", mp_swap(0, k)) for k in (1, 2, 3)]
    column = jnp.concatenate(along_z, axis=1)
    row_parts = [column] + [lax.ppermute(column, "mp", mp_swap(k, 0)) for k in (1, 2, 3)]

    news, totals = [], []
    for step in (gate_step, up_step):
        new = lax.all_to_all(step, "mp", split_axis=0, concat_axis=0, tiled=True)
        new = new.reshape(512, 1024)
        other = lax.ppermute(new, "dp", dp_swap(0, 0, 1))
        news.append(new)
        totals.append(scatter_sums(products(chip, row_parts, new, other)))
    gate_total, up_total = totals
    hidden = (jax.nn.silu(gate_total) * up_total).astype(jnp.bfloat16)

    at = jnp.arange(128)
    y_flip, z_flip, step_at, row_at = at // 32, at // 8 % 4, at // 2 % 4, at % 2
    gray_from = (y ^ (y >> 1)) ^ y_flip
    y_from = gray_from ^ (gray_from >> 1)
    target = step_at * 32 + (y_from * 4 + (z_lo ^ z_flip)) * 2 + row_at
    placed = (at[:, None] == target[None, :]).astype(jnp.bfloat16)
    hidden = jnp.dot(placed, hidden, preferred_element_type=jnp.float32).astype(jnp.bfloat16)
    return news[0], news[1], hidden.reshape(STEPS, 32, 1024)


def solution(mesh):
    rows = P(("dp", "mp"), None)
    steps = P(None, ("dp", "mp"), None)
    cache = P(("dp", "mp"), None, None)
    in_specs = (rows,) * 8 + (steps,) * 4 + (cache,) * 2 + (P(("dp", "mp")), P())
    out_specs = (P("dp", "mp"), P("dp", "mp"), P(None, "dp", "mp"))
    return jax.shard_map(local, mesh=mesh, in_specs=in_specs, out_specs=out_specs, check_vma=False)
```

time: 527 us -> 197 us (0.37)
  blocking collectives: 289 us -> 0 us
  waiting for transfers between devices: 159 us -> 110 us
  starting transfers between devices: 16.8 us -> 47.6 us
  Pallas kernels: 0 us -> 21.3 us
  between operations: 14.2 us -> 1 us
  other arithmetic: 16 us -> 3.52 us
  matrix products: 14.8 us -> 4.03 us
  local copies, waits for them, and re-layouts: 14.6 us -> 7.97 us
    all_gather x4 -> x0, blocking collectives: 180 us -> none  [local(): grouped = lax.all_gather(normed, 'mp', axis=0, tiled=True)]
    reduce_scatter x4 -> x0, waiting for transfers between devices: 129 us -> none  [local(): lax.psum_scatter((jnp.dot(spread, joined, preferred_element_type=jnp.floa...]
    all_to_all x4 -> x0, blocking collectives: 108 us -> none  [the longest x3 75 us: local(): lax.all_to_all(grouped, 'dp', split_axis=1, concat_axis=0, tiled=True)]
    ppermute x0 -> x18, waiting for transfers between devices: none -> 90.8 us  [the longest x3 31 us: local(): lax.ppermute(spread, 'mp', mp_swap(0, k))]
    ppermute x0 -> x18, starting transfers between devices: none -> 23.2 us  [the longest x2 7.69 us: scatter_sums(): got = lax.ppermute(both[1].astype(jnp.bfloat16), 'dp', dp_swap(0, 1, 0))]
    pallas_call x0 -> x4, Pallas kernels: none -> 21.3 us  [the longest x2 13.5 us: adam_blocks(): pl.pallas_call(adam_kernel, grid=(16 // per_step,), in_specs=[spec] * 4,...]
    all_to_all x2 -> x3, waiting for transfers between devices: 30.5 us -> 19.4 us  [the longest x2 15.4 us: local(): new = lax.all_to_all(step, 'mp', split_axis=0, concat_axis=0, tiled=True)]
    all_to_all x10 -> x0, local copies, waits for them, and re-layouts: 11.1 us -> none  [the longest x8 8.95 us: local(): lax.all_to_all(grouped, 'dp', split_axis=1, concat_axis=0, tiled=True)]
  transfers between devices with their start and end apart: 6 -> 21, of which waited for: 4 -> 13; matrix products, arithmetic and copies ran while one was open for 5% -> 1% of each run, Pallas kernels for 0% -> 11%
where the time goes in v1:
time: 197 us; the launch traced here: 196 us
  waiting for transfers between devices  110 us (56%)
  starting transfers between devices  47.6 us (24%)
  Pallas kernels  21.3 us (11%)
  local copies, waits for them, and re-layouts  7.97 us (4%)
  matrix products  4.03 us (2%)
  other arithmetic  3.52 us (2%)
    ppermute x3, waiting for transfers between devices, local(): lax.ppermute(spread, 'mp', mp_swap(0, k))  31 us
    ppermute x3, waiting for transfers between devices, local(): lax.ppermute(column, 'mp', mp_swap(k, 0))  23.7 us
    all_to_all x2, waiting for transfers between devices, local(): new = lax.all_to_all(step, 'mp', split_axis=0, concat_axis=0, tiled=True)  15.4 us
    ppermute x2, waiting for transfers between devices, scatter_sums(): got = lax.ppermute(both[1].astype(jnp.bfloat16), 'dp', dp_swap(0, 1, 0))  14.7 us
    all_to_all x2, starting transfers between devices, local(): new = lax.all_to_all(step, 'mp', split_axis=0, concat_axis=0, tiled=True)  14.4 us
    pallas_call x2, Pallas kernels, adam_blocks(): pl.pallas_call(adam_kernel, grid=(16 // per_step,), in_specs=[spec] * 4,...  13.5 us
    ppermute x2, waiting for transfers between devices, scatter_sums(): got_b = lax.ppermute(send_b, 'dp', dp_swap(2, 0, 0))  10.9 us
    all_to_all x1, starting transfers between devices, local(): lax.all_to_all(blocks, 'dp', split_axis=0, concat_axis=0, axis_index_grou...  10 us
  transfers between devices with their start and end apart: 21, of which 13 were waited for; matrix products, arithmetic and copies ran while one was open for 1% of the time, Pallas kernels for 11%

profile of v1, /device:TPU:32, one launch (start us, length us, event | category | flops | bytes accessed | tf_op | source)
XLA Modules:
  0.0 195.6 jit_solution(17231310363463384128)
XLA Ops:
  0.7 1.0 reshape.164
  1.7 1.1 copy.46
  2.9 0.6 copy-done.7
  3.6 0.5 fusion.51
  4.1 0.7 fusion.52
  4.8 0.3 fusion.26
  5.1 0.1 fusion.31
  5.3 0.6 copy-done.6
  5.9 0.1 copy.47
  6.0 0.3 fusion.32
  6.3 0.3 fusion
  6.7 0.1 reshape.169
  6.8 0.7 copy-done.2
  7.6 0.3 multiply_reduce_fusion
  7.8 0.4 copy-done.4
  8.3 0.2 multiply_convert_fusion
  8.5 0.1 reshape.170
  8.7 0.7 reverse_select_fusion
  9.4 10.0 %all-to-all-start.2 = ((bf16[8,8,1024]{2,1,0:T(8,128)(2,1)}), bf16[8,8,1024]{2,1,0:T(8,128)(2,1)S(1)}, u32[]{:S(2)}, u32[]{:S(2)}) async-start(bf16[8,8,1024]{2,1,0:T(8,128)(2,1)} %bitcast.11), calls=%async_computation.2 | async-start | bytes 262144 | tf_op jit(solution)/shard_map/all_to_all | solution.py:203
  19.4 6.8 %adam.2 = bf16[16,32,1024]{2,1,0:T(8,128)(2,1)} custom-call(bf16[32,16384]{1,0:T(8,128)(2,1)} %weight_ref.2, bf16[32,16384]{1,0:T(8,128)(2,1)} %grad_ref.2, bf16[32,16384]{1,0:T(8,128)(2,1)} %moment_ref.2, bf16[32,16384]{1,0:T(8,128)(2,1)} %second_ref.2), custom_call_target="tpu_custom_call" | custom-call | flops 10485760 | bytes 5242880 | tf_op jit(solution)/shard_map/adam/pallas_call | solution.py:69
  26.2 4.0 %all-to-all-done.2 = bf16[8,8,1024]{2,1,0:T(8,128)(2,1)S(1)} async-done(((bf16[8,8,1024]{2,1,0:T(8,128)(2,1)}), bf16[8,8,1024]{2,1,0:T(8,128)(2,1)S(1)}, u32[]{:S(2)}, u32[]{:S(2)}) %all-to-all-start.2) | async-done | bytes 131104 | tf_op jit(solution)/shard_map/all_to_all | solution.py:203
  30.2 6.7 %all-to-all-start = ((bf16[16,32,1024]{2,1,0:T(8,128)(2,1)}), bf16[16,32,1024]{2,1,0:T(8,128)(2,1)S(1)}, u32[]{:S(2)}, u32[]{:S(2)}) async-start(bf16[16,32,1024]{2,1,0:T(8,128)(2,1)} %adam.2), calls=%async_computation | async-start | bytes 2097152 | tf_op jit(solution)/shard_map/all_to_all | solution.py:212
  36.9 6.8 %adam.3 = bf16[16,32,1024]{2,1,0:T(8,128)(2,1)} custom-call(bf16[32,16384]{1,0:T(8,128)(2,1)} %weight_ref.3, bf16[32,16384]{1,0:T(8,128)(2,1)} %grad_ref.3, bf16[32,16384]{1,0:T(8,128)(2,1)} %moment_ref.3, bf16[32,16384]{1,0:T(8,128)(2,1)} %second_ref.3), custom_call_target="tpu_custom_call" | custom-call | flops 10485760 | bytes 5242880 | tf_op jit(solution)/shard_map/adam/pallas_call | solution.py:69
  43.6 15.4 %all-to-all-done = bf16[16,32,1024]{2,1,0:T(8,128)(2,1)S(1)} async-done(((bf16[16,32,1024]{2,1,0:T(8,128)(2,1)}), bf16[16,32,1024]{2,1,0:T(8,128)(2,1)S(1)}, u32[]{:S(2)}, u32[]{:S(2)}) %all-to-all-start) | async-done | bytes 1048608 | tf_op jit(solution)/shard_map/all_to_all | solution.py:212
  59.0 7.7 %all-to-all-start.1 = ((bf16[16,32,1024]{2,1,0:T(8,128)(2,1)}), bf16[16,32,1024]{2,1,0:T(8,128)(2,1)S(1)}, u32[]{:S(2)}, u32[]{:S(2)}) async-start(bf16[16,32,1024]{2,1,0:T(8,128)(2,1)} %adam.3), calls=%async_computation.1 | async-start | bytes 2097152 | tf_op jit(solution)/shard_map/all_to_all | solution.py:212
  66.7 0.4 collective-permute-start
  67.1 2.6 %collective-permute-start.1 = (bf16[8,8,1024]{2,1,0:T(8,128)(2,1)S(1)}, bf16[8,8,1024]{2,1,0:T(8,128)(2,1)S(1)}, u32[]{:S(2)}, u32[]{:S(2)}) collective-permute-start(bf16[8,8,1024]{2,1,0:T(8,128)(2,1)S(1)} %all-to-all-done.2), channel_id=1, source_target_pairs={{0,2},{1,3},{2,0},{3,1},{4,6},{5,7},{6,4},{7,5},{8,10},{9,11},{10,... | collective-permute-start | bytes 393224 | tf_op jit(solution)/shard_map/ppermute | solution.py:206
  69.8 0.6 collective-permute-start.2
  70.4 18.0 %collective-permute-done = bf16[8,8,1024]{2,1,0:T(8,128)(2,1)S(1)} collective-permute-done((bf16[8,8,1024]{2,1,0:T(8,128)(2,1)S(1)}, bf16[8,8,1024]{2,1,0:T(8,128)(2,1)S(1)}, u32[]{:S(2)}, u32[]{:S(2)}) %collective-permute-start) | collective-permute-done | bytes 131104 | tf_op jit(solution)/shard_map/ppermute | solution.py:206
  88.4 8.3 %collective-permute-done.1 = bf16[8,8,1024]{2,1,0:T(8,128)(2,1)S(1)} collective-permute-done((bf16[8,8,1024]{2,1,0:T(8,128)(2,1)S(1)}, bf16[8,8,1024]{2,1,0:T(8,128)(2,1)S(1)}, u32[]{:S(2)}, u32[]{:S(2)}) %collective-permute-start.1) | collective-permute-done | bytes 131104 | tf_op jit(solution)/shard_map/ppermute | solution.py:206
  96.7 4.7 %collective-permute-done.2 = bf16[8,8,1024]{2,1,0:T(8,128)(2,1)S(1)} collective-permute-done((bf16[8,8,1024]{2,1,0:T(8,128)(2,1)S(1)}, bf16[8,8,1024]{2,1,0:T(8,128)(2,1)S(1)}, u32[]{:S(2)}, u32[]{:S(2)}) %collective-permute-start.2) | collective-permute-done | bytes 131104 | tf_op jit(solution)/shard_map/ppermute | solution.py:206
  101.5 0.1 collective-permute-start.12
  101.6 1.6 collective-permute-start.3
  103.1 2.1 %collective-permute-start.4 = (bf16[8,32,1024]{2,1,0:T(8,128)(2,1)S(1)}, bf16[8,32,1024]{2,1,0:T(8,128)(2,1)}, u32[]{:S(2)}, u32[]{:S(2)}) collective-permute-start(bf16[8,32,1024]{2,1,0:T(8,128)(2,1)S(1)} %constant_dynamic-update-slice_fusion.refs_0_), channel_id=1, source_target_pairs={{0,12},{1,13},{2,14},{3,15},{4,8},{5,9},{6,10},{7,11},{8,4},{9,5},... | collective-permute-start | bytes 1572872 | tf_op jit(solution)/shard_map/ppermute | solution.py:208
  105.2 0.6 collective-permute-start.5
  105.9 10.4 %collective-permute-done.3.refs_1_ = bf16[8,32,1024]{2,1,0:T(8,128)(2,1)S(1)} collective-permute-done((bf16[8,32,1024]{2,1,0:T(8,128)(2,1)S(1)}, bf16[8,32,1024]{2,1,0:T(8,128)(2,1)S(1)}, u32[]{:S(2)}, u32[]{:S(2)}) %collective-permute-start.3) | collective-permute-done | bytes 524320 | tf_op jit(solution)/shard_map/ppermute | solution.py:208
  116.4 13.3 %collective-permute-done.4.refs_2_ = bf16[8,32,1024]{2,1,0:T(8,128)(2,1)} collective-permute-done((bf16[8,32,1024]{2,1,0:T(8,128)(2,1)S(1)}, bf16[8,32,1024]{2,1,0:T(8,128)(2,1)}, u32[]{:S(2)}, u32[]{:S(2)}) %collective-permute-start.4) | collective-permute-done | bytes 524320 | tf_op jit(solution)/shard_map/ppermute | solution.py:208
  129.7 3.9 %products.2 = (bf16[2,2,128,512]{3,2,1,0:T(8,128)(2,1)S(1)}, bf16[2,2,128,512]{3,2,1,0:T(8,128)(2,1)S(1)}, bf16[2,2,128,512]{3,2,1,0:T(8,128)(2,1)S(1)}, bf16[2,2,128,512]{3,2,1,0:T(8,128)(2,1)S(1)}) custom-call(s32[2]{0:T(128)S(1)} %pad_add_fusion.chip_ref, bf16[8,32,1024]{2,1,0:T(8,128)(2,1)S(1)} %constant_dynamic-update-slice_fusion.refs_0_, ...), custom_call_target="tpu_custom_call" | custom-call | flops 2147483648 | bytes 6291456 | tf_op jit(solution)/shard_map/products/pallas_call | solution.py:134
  133.6 0.5 collective-permute-start.7
  134.0 1.3 collective-permute-start.9
  135.4 3.9 %products.3 = (bf16[2,2,128,512]{3,2,1,0:T(8,128)(2,1)S(1)}, bf16[2,2,128,512]{3,2,1,0:T(8,128)(2,1)S(1)}, bf16[2,2,128,512]{3,2,1,0:T(8,128)(2,1)S(1)}, bf16[2,2,128,512]{3,2,1,0:T(8,128)(2,1)S(1)}) custom-call(s32[2]{0:T(128)S(1)} %pad_add_fusion.chip_ref, bf16[8,32,1024]{2,1,0:T(8,128)(2,1)S(1)} %constant_dynamic-update-slice_fusion.refs_0_, ...), custom_call_target="tpu_custom_call" | custom-call | flops 2147483648 | bytes 6291456 | tf_op jit(solution)/shard_map/products/pallas_call | solution.py:134
  139.3 2.0 %collective-permute-start.15 = (bf16[2,2,128,512]{3,2,1,0:T(8,128)(2,1)S(1)}, bf16[2,2,128,512]{3,2,1,0:T(8,128)(2,1)S(1)}, u32[]{:S(2)}, u32[]{:S(2)}) collective-permute-start(bf16[2,2,128,512]{3,2,1,0:T(8,128)(2,1)S(1)} %get-tuple-element.18), channel_id=1, source_target_pairs={{0,192},{16,208},{32,224},{48,240},{64,128},{80,144},{96,160},{112... | collective-permute-start | bytes 1572872 | tf_op jit(solution)/shard_map/ppermute | solution.py:154
  141.3 0.4 collective-permute-start.13
  141.7 6.8 %collective-permute-done.7 = bf16[2,2,128,512]{3,2,1,0:T(8,128)(2,1)S(1)} collective-permute-done((bf16[2,2,128,512]{3,2,1,0:T(8,128)(2,1)S(1)}, bf16[2,2,128,512]{3,2,1,0:T(8,128)(2,1)S(1)}, u32[]{:S(2)}, u32[]{:S(2)}) %collective-permute-start.7) | collective-permute-done | bytes 524320 | tf_op jit(solution)/shard_map/ppermute | solution.py:153
  148.5 0.1 convert_add_fusion.3
  148.7 1.1 collective-permute-start.8
  149.8 0.3 collective-permute-done.9
  150.1 0.1 convert_add_fusion.2
  150.3 0.5 collective-permute-start.10
  150.8 10.5 %collective-permute-done.15 = bf16[2,2,128,512]{3,2,1,0:T(8,128)(2,1)S(1)} collective-permute-done((bf16[2,2,128,512]{3,2,1,0:T(8,128)(2,1)S(1)}, bf16[2,2,128,512]{3,2,1,0:T(8,128)(2,1)S(1)}, u32[]{:S(2)}, u32[]{:S(2)}) %collective-permute-start.15) | collective-permute-done | bytes 524320 | tf_op jit(solution)/shard_map/ppermute | solution.py:154
  161.3 0.2 convert_add_fusion
  161.6 0.5 collective-permute-start.16
  162.1 0.2 convert_add_fusion.1
  162.3 1.1 collective-permute-start.14
  163.4 3.6 %collective-permute-done.8 = bf16[2,128,512]{2,1,0:T(8,128)(2,1)S(1)} collective-permute-done((bf16[2,128,512]{2,1,0:T(8,128)(2,1)S(1)}, bf16[2,128,512]{2,1,0:T(8,128)(2,1)S(1)}, u32[]{:S(2)}, u32[]{:S(2)}) %collective-permute-start.8) | collective-permute-done | bytes 262176 | tf_op jit(solution)/shard_map/ppermute | solution.py:157
  167.2 5.1 %collective-permute-start.11 = (bf16[128,1024]{1,0:T(8,128)(2,1)S(1)}, bf16[128,1024]{1,0:T(8,128)(2,1)}, u32[]{:S(2)}, u32[]{:S(2)}) collective-permute-start(bf16[128,1024]{1,0:T(8,128)(2,1)S(1)} %fusion.21), channel_id=1, source_target_pairs={{0,32},{16,48},{32,0},{48,16},{64,96},{80,112},{96,64},{112,80},{1... | collective-permute-start | bytes 786440 | tf_op jit(solution)/shard_map/ppermute | solution.py:162
  172.4 0.7 copy-done
  173.1 0.8 fusion.24
  174.0 2.6 %collective-permute-start.17 = (bf16[128,1024]{1,0:T(8,128)(2,1)}, bf16[128,1024]{1,0:T(8,128)(2,1)}, u32[]{:S(2)}, u32[]{:S(2)}) collective-permute-start(bf16[128,1024]{1,0:T(8,128)(2,1)} %fusion.24), channel_id=1, source_target_pairs={{0,32},{16,48},{32,0},{48,16},{64,96},{80,112},{96,64},{112,80},{1... | collective-permute-start | bytes 786440 | tf_op jit(solution)/shard_map/ppermute | solution.py:162
  176.6 10.2 %collective-permute-done.11 = bf16[128,1024]{1,0:T(8,128)(2,1)} collective-permute-done((bf16[128,1024]{1,0:T(8,128)(2,1)S(1)}, bf16[128,1024]{1,0:T(8,128)(2,1)}, u32[]{:S(2)}, u32[]{:S(2)}) %collective-permute-start.11) | collective-permute-done | bytes 262176 | tf_op jit(solution)/shard_map/ppermute | solution.py:162
  186.9 4.5 %collective-permute-done.17 = bf16[128,1024]{1,0:T(8,128)(2,1)} collective-permute-done((bf16[128,1024]{1,0:T(8,128)(2,1)}, bf16[128,1024]{1,0:T(8,128)(2,1)}, u32[]{:S(2)}, u32[]{:S(2)}) %collective-permute-start.17) | collective-permute-done | bytes 262176 | tf_op jit(solution)/shard_map/ppermute | solution.py:162
  191.4 2.3 %convolution_convert_fusion = bf16[128,1024]{1,0:T(8,128)(2,1)} fusion(f32[2,128,512]{2,1,0:T(8,128)} %copy-done.1, f32[2,128,512]{2,1,0:T(8,128)} %copy-done, bf16[128,1024]{1,0:T(8,128)(2,1)} %collective-permute-done.17, f32[2,128,512]{2,1,0:T(8,128)S(1)} %fusion.15, f32[2,128,512]{2,1,0:T(8,128)S(1)} %fusion.16, ...), kind=kOutput, calls=%fused_computation | convolution fusion | flops 35274752 | bytes 2884096 | tf_op jit(solution)/shard_map/dot_general | solution.py:226
  193.6 1.0 copy.75
  194.6 1.0 copy.76
  (47 shorter events, 1.0 us)
Async XLA Ops:
  2.8 0.7 copy-start.7
  2.8 0.7 copy-start.5
  4.1 1.8 copy-start.3
  5.1 0.7 copy-start.6
  6.6 0.9 copy-start.2
  7.5 0.7 copy-start.4
  9.4 20.8 %all-to-all-start.2 = ((bf16[8,8,1024]{2,1,0:T(8,128)(2,1)}), bf16[8,8,1024]{2,1,0:T(8,128)(2,1)S(1)}, u32[]{:S(2)}, u32[]{:S(2)}) async-start(bf16[8,8,1024]{2,1,0:T(8,128)(2,1)} %bitcast.11), calls=%async_computation.2 | async-start | bytes 262144 | tf_op jit(solution)/shard_map/all_to_all | solution.py:203
  30.2 28.8 %all-to-all-start = ((bf16[16,32,1024]{2,1,0:T(8,128)(2,1)}), bf16[16,32,1024]{2,1,0:T(8,128)(2,1)S(1)}, u32[]{:S(2)}, u32[]{:S(2)}) async-start(bf16[16,32,1024]{2,1,0:T(8,128)(2,1)} %adam.2), calls=%async_computation | async-start | bytes 2097152 | tf_op jit(solution)/shard_map/all_to_all | solution.py:212
  59.0 42.4 %all-to-all-start.1 = ((bf16[16,32,1024]{2,1,0:T(8,128)(2,1)}), bf16[16,32,1024]{2,1,0:T(8,128)(2,1)S(1)}, u32[]{:S(2)}, u32[]{:S(2)}) async-start(bf16[16,32,1024]{2,1,0:T(8,128)(2,1)} %adam.3), calls=%async_computation.1 | async-start | bytes 2097152 | tf_op jit(solution)/shard_map/all_to_all | solution.py:212
  66.7 62.9 %collective-permute-start.6 = (bf16[512,1024]{1,0:T(8,128)(2,1)S(1)}, bf16[512,1024]{1,0:T(8,128)(2,1)}, u32[]{:S(2)}, u32[]{:S(2)}) collective-permute-start(bf16[512,1024]{1,0:T(8,128)(2,1)S(1)} %bitcast.77), channel_id=1, source_target_pairs={{0,16},{16,0},{32,48},{48,32},{64,80},{80,64},{96,112},{112,96},{1... | collective-permute-start | bytes 3145736 | tf_op jit(solution)/shard_map/ppermute | solution.py:214
  66.7 21.6 %collective-permute-start = (bf16[8,8,1024]{2,1,0:T(8,128)(2,1)S(1)}, bf16[8,8,1024]{2,1,0:T(8,128)(2,1)S(1)}, u32[]{:S(2)}, u32[]{:S(2)}) collective-permute-start(bf16[8,8,1024]{2,1,0:T(8,128)(2,1)S(1)} %all-to-all-done.2), channel_id=1, source_target_pairs={{0,1},{1,0},{2,3},{3,2},{4,5},{5,4},{6,7},{7,6},{8,9},{9,8},{10,11... | collective-permute-start | bytes 393224 | tf_op jit(solution)/shard_map/ppermute | solution.py:206
  67.1 29.5 %collective-permute-start.1 = (bf16[8,8,1024]{2,1,0:T(8,128)(2,1)S(1)}, bf16[8,8,1024]{2,1,0:T(8,128)(2,1)S(1)}, u32[]{:S(2)}, u32[]{:S(2)}) collective-permute-start(bf16[8,8,1024]{2,1,0:T(8,128)(2,1)S(1)} %all-to-all-done.2), channel_id=1, source_target_pairs={{0,2},{1,3},{2,0},{3,1},{4,6},{5,7},{6,4},{7,5},{8,10},{9,11},{10,... | collective-permute-start | bytes 393224 | tf_op jit(solution)/shard_map/ppermute | solution.py:206
  69.8 31.7 %collective-permute-start.2 = (bf16[8,8,1024]{2,1,0:T(8,128)(2,1)S(1)}, bf16[8,8,1024]{2,1,0:T(8,128)(2,1)S(1)}, u32[]{:S(2)}, u32[]{:S(2)}) collective-permute-start(bf16[8,8,1024]{2,1,0:T(8,128)(2,1)S(1)} %all-to-all-done.2), channel_id=1, source_target_pairs={{0,3},{1,2},{2,1},{3,0},{4,7},{5,6},{6,5},{7,4},{8,11},{9,10},{10,... | collective-permute-start | bytes 393224 | tf_op jit(solution)/shard_map/ppermute | solution.py:206
  101.5 33.9 %collective-permute-start.12 = (bf16[512,1024]{1,0:T(8,128)(2,1)S(1)}, bf16[512,1024]{1,0:T(8,128)(2,1)}, u32[]{:S(2)}, u32[]{:S(2)}) collective-permute-start(bf16[512,1024]{1,0:T(8,128)(2,1)S(1)} %bitcast.80), channel_id=1, source_target_pairs={{0,16},{16,0},{32,48},{48,32},{64,80},{80,64},{96,112},{112,96},{1... | collective-permute-start | bytes 3145736 | tf_op jit(solution)/shard_map/ppermute | solution.py:214
  101.6 14.8 %collective-permute-start.3 = (bf16[8,32,1024]{2,1,0:T(8,128)(2,1)S(1)}, bf16[8,32,1024]{2,1,0:T(8,128)(2,1)S(1)}, u32[]{:S(2)}, u32[]{:S(2)}) collective-permute-start(bf16[8,32,1024]{2,1,0:T(8,128)(2,1)S(1)} %constant_dynamic-update-slice_fusion.refs_0_), channel_id=1, source_target_pairs={{0,4},{1,5},{2,6},{3,7},{4,0},{5,1},{6,2},{7,3},{8,12},{9,13},{10,... | collective-permute-start | bytes 1572872 | tf_op jit(solution)/shard_map/ppermute | solution.py:208
  103.1 26.5 %collective-permute-start.4 = (bf16[8,32,1024]{2,1,0:T(8,128)(2,1)S(1)}, bf16[8,32,1024]{2,1,0:T(8,128)(2,1)}, u32[]{:S(2)}, u32[]{:S(2)}) collective-permute-start(bf16[8,32,1024]{2,1,0:T(8,128)(2,1)S(1)} %constant_dynamic-update-slice_fusion.refs_0_), channel_id=1, source_target_pairs={{0,12},{1,13},{2,14},{3,15},{4,8},{5,9},{6,10},{7,11},{8,4},{9,5},... | collective-permute-start | bytes 1572872 | tf_op jit(solution)/shard_map/ppermute | solution.py:208
  105.2 24.4 %collective-permute-start.5 = (bf16[8,32,1024]{2,1,0:T(8,128)(2,1)S(1)}, bf16[8,32,1024]{2,1,0:T(8,128)(2,1)}, u32[]{:S(2)}, u32[]{:S(2)}) collective-permute-start(bf16[8,32,1024]{2,1,0:T(8,128)(2,1)S(1)} %constant_dynamic-update-slice_fusion.refs_0_), channel_id=1, source_target_pairs={{0,8},{1,9},{2,10},{3,11},{4,12},{5,13},{6,14},{7,15},{8,0},{9,1},... | collective-permute-start | bytes 1572872 | tf_op jit(solution)/shard_map/ppermute | solution.py:208
  133.6 14.9 %collective-permute-start.7 = (bf16[2,2,128,512]{3,2,1,0:T(8,128)(2,1)S(1)}, bf16[2,2,128,512]{3,2,1,0:T(8,128)(2,1)S(1)}, u32[]{:S(2)}, u32[]{:S(2)}) collective-permute-start(bf16[2,2,128,512]{3,2,1,0:T(8,128)(2,1)S(1)} %get-tuple-element.12), channel_id=1, source_target_pairs={{0,64},{16,80},{32,96},{48,112},{64,0},{80,16},{96,32},{112,48},{1... | collective-permute-start | bytes 1572872 | tf_op jit(solution)/shard_map/ppermute | solution.py:153
  134.0 16.1 %collective-permute-start.9 = (bf16[2,2,128,512]{3,2,1,0:T(8,128)(2,1)S(1)}, bf16[2,2,128,512]{3,2,1,0:T(8,128)(2,1)S(1)}, u32[]{:S(2)}, u32[]{:S(2)}) collective-permute-start(bf16[2,2,128,512]{3,2,1,0:T(8,128)(2,1)S(1)} %get-tuple-element.14), channel_id=1, source_target_pairs={{0,192},{16,208},{32,224},{48,240},{64,128},{80,144},{96,160},{112... | collective-permute-start | bytes 1572872 | tf_op jit(solution)/shard_map/ppermute | solution.py:154
  139.3 22.1 %collective-permute-start.15 = (bf16[2,2,128,512]{3,2,1,0:T(8,128)(2,1)S(1)}, bf16[2,2,128,512]{3,2,1,0:T(8,128)(2,1)S(1)}, u32[]{:S(2)}, u32[]{:S(2)}) collective-permute-start(bf16[2,2,128,512]{3,2,1,0:T(8,128)(2,1)S(1)} %get-tuple-element.18), channel_id=1, source_target_pairs={{0,192},{16,208},{32,224},{48,240},{64,128},{80,144},{96,160},{112... | collective-permute-start | bytes 1572872 | tf_op jit(solution)/shard_map/ppermute | solution.py:154
  141.3 20.8 %collective-permute-start.13 = (bf16[2,2,128,512]{3,2,1,0:T(8,128)(2,1)S(1)}, bf16[2,2,128,512]{3,2,1,0:T(8,128)(2,1)S(1)}, u32[]{:S(2)}, u32[]{:S(2)}) collective-permute-start(bf16[2,2,128,512]{3,2,1,0:T(8,128)(2,1)S(1)} %get-tuple-element.16), channel_id=1, source_target_pairs={{0,64},{16,80},{32,96},{48,112},{64,0},{80,16},{96,32},{112,48},{1... | collective-permute-start | bytes 1572872 | tf_op jit(solution)/shard_map/ppermute | solution.py:153
  148.7 18.3 %collective-permute-start.8 = (bf16[2,128,512]{2,1,0:T(8,128)(2,1)S(1)}, bf16[2,128,512]{2,1,0:T(8,128)(2,1)S(1)}, u32[]{:S(2)}, u32[]{:S(2)}) collective-permute-start(bf16[2,128,512]{2,1,0:T(8,128)(2,1)S(1)} %fusion.19), channel_id=1, source_target_pairs={{0,192},{16,208},{32,224},{48,240},{64,128},{80,144},{96,160},{112... | collective-permute-start | bytes 786440 | tf_op jit(solution)/shard_map/ppermute | solution.py:157
  150.3 16.7 %collective-permute-start.10 = (bf16[2,128,512]{2,1,0:T(8,128)(2,1)S(1)}, bf16[2,128,512]{2,1,0:T(8,128)(2,1)S(1)}, u32[]{:S(2)}, u32[]{:S(2)}) collective-permute-start(bf16[2,128,512]{2,1,0:T(8,128)(2,1)S(1)} %fusion.20), channel_id=1, source_target_pairs={{0,64},{16,80},{32,96},{48,112},{64,0},{80,16},{96,32},{112,48},{1... | collective-permute-start | bytes 786440 | tf_op jit(solution)/shard_map/ppermute | solution.py:158
  161.6 10.7 %collective-permute-start.16 = (bf16[2,128,512]{2,1,0:T(8,128)(2,1)S(1)}, bf16[2,128,512]{2,1,0:T(8,128)(2,1)S(1)}, u32[]{:S(2)}, u32[]{:S(2)}) collective-permute-start(bf16[2,128,512]{2,1,0:T(8,128)(2,1)S(1)} %fusion.23), channel_id=1, source_target_pairs={{0,64},{16,80},{32,96},{48,112},{64,0},{80,16},{96,32},{112,48},{1... | collective-permute-start | bytes 786440 | tf_op jit(solution)/shard_map/ppermute | solution.py:158
  162.3 10.1 %collective-permute-start.14 = (bf16[2,128,512]{2,1,0:T(8,128)(2,1)S(1)}, bf16[2,128,512]{2,1,0:T(8,128)(2,1)S(1)}, u32[]{:S(2)}, u32[]{:S(2)}) collective-permute-start(bf16[2,128,512]{2,1,0:T(8,128)(2,1)S(1)} %fusion.22), channel_id=1, source_target_pairs={{0,192},{16,208},{32,224},{48,240},{64,128},{80,144},{96,160},{112... | collective-permute-start | bytes 786440 | tf_op jit(solution)/shard_map/ppermute | solution.py:157
  167.2 19.7 %collective-permute-start.11 = (bf16[128,1024]{1,0:T(8,128)(2,1)S(1)}, bf16[128,1024]{1,0:T(8,128)(2,1)}, u32[]{:S(2)}, u32[]{:S(2)}) collective-permute-start(bf16[128,1024]{1,0:T(8,128)(2,1)S(1)} %fusion.21), channel_id=1, source_target_pairs={{0,32},{16,48},{32,0},{48,16},{64,96},{80,112},{96,64},{112,80},{1... | collective-permute-start | bytes 786440 | tf_op jit(solution)/shard_map/ppermute | solution.py:162
  172.3 0.8 copy-start
  173.1 0.9 copy-start.1
  174.0 17.4 %collective-permute-start.17 = (bf16[128,1024]{1,0:T(8,128)(2,1)}, bf16[128,1024]{1,0:T(8,128)(2,1)}, u32[]{:S(2)}, u32[]{:S(2)}) collective-permute-start(bf16[128,1024]{1,0:T(8,128)(2,1)} %fusion.24), channel_id=1, source_target_pairs={{0,32},{16,48},{32,0},{48,16},{64,96},{80,112},{96,64},{112,80},{1... | collective-permute-start | bytes 786440 | tf_op jit(solution)/shard_map/ppermute | solution.py:162

commit v2 on v1

v2 whole, which is shorter than its diff:
```python
import jax
import jax.numpy as jnp
from jax import lax
from jax.experimental import pallas as pl
from jax.experimental.pallas import tpu as pltpu
from jax.sharding import PartitionSpec as P

D = 8192
HD = 128
KVH = 8
GROUP = 8
CTX = 128
STEPS = 4
ROWS_HERE = 2

BRIEF = pl.CostEstimate(flops=1, bytes_accessed=1, transcendentals=0)

GRAY = (0, 1, 3, 2)

beta_one = 0.9
beta_two = 0.95
learn_rate = 0.15
weight_decay = 0.1
adam_eps = 1e-08
first_fix = 1.0 - 0.9**10
second_fix = 1.0 - 0.95**10


def dp_swap(flip_x, flip_z, flip_core):
    pairs = []
    for dp in range(16):
        x, z_hi, core = dp // 4, dp // 2 % 2, dp % 2
        x_to = GRAY[GRAY[x] ^ flip_x]
        pairs.append((dp, x_to * 4 + (z_hi ^ flip_z) * 2 + (core ^ flip_core)))
    return pairs


def mp_swap(flip_y, flip_z):
    pairs = []
    for mp in range(16):
        y, z_lo = mp // 4, mp % 4
        pairs.append((mp, GRAY[GRAY[y] ^ flip_y] * 4 + (z_lo ^ flip_z)))
    return pairs


def adam_kernel(weight_ref, grad_ref, moment_ref, second_ref, cols):
    weight_f = weight_ref[:, cols].astype(jnp.float32)
    grad_f = grad_ref[:, cols].astype(jnp.float32)
    moment_f = moment_ref[:, cols].astype(jnp.float32)
    second_f = second_ref[:, cols].astype(jnp.float32)
    rise = (learn_rate * beta_one / first_fix) * moment_f
    rise += (learn_rate * (1.0 - beta_one) / first_fix) * grad_f
    spread = (beta_two / second_fix) * second_f
    spread += ((1.0 - beta_two) / second_fix) * (grad_f * grad_f)
    root = spread * lax.rsqrt(spread) + adam_eps
    new = (1.0 - learn_rate * weight_decay) * weight_f - rise * lax.rsqrt(root * root)
    return new.astype(jnp.bfloat16)


def adam_places_kernel(*refs):
    *in_refs, out_ref = refs
    width = out_ref.shape[2]
    for part in range(out_ref.shape[0]):
        out_ref[part] = adam_kernel(*in_refs, slice(part * width, (part + 1) * width))


def adam_places(*arrays):
    rows, cols = arrays[0].shape
    width = cols // 16
    return pl.pallas_call(
        adam_places_kernel,
        grid=(4,),
        in_specs=[pl.BlockSpec((rows, 4 * width), lambda i: (0, i))] * 4,
        out_specs=pl.BlockSpec((4, rows, width), lambda i: (i, 0, 0)),
        out_shape=jax.ShapeDtypeStruct((16, rows, width), jnp.bfloat16),
        cost_estimate=BRIEF,
        name="adam_places",
    )(*arrays)


def adam_flips_kernel(at_ref, *refs):
    in_refs, out_refs = refs[:4], refs[4:]
    width = out_refs[0].shape[2]
    for flip in range(4):
        cols = pl.ds(pl.multiple_of((at_ref[4] ^ flip) * width, width), width)
        new = adam_kernel(*in_refs, cols)
        for y_flip, out_ref in enumerate(out_refs):

            @pl.when(pl.program_id(0) == y_flip)
            def _():
                out_ref[flip] = new


def adam_flips(at, *arrays):
    rows, cols = arrays[0].shape
    width = cols // 16
    return pl.pallas_call(
        adam_flips_kernel,
        grid_spec=pltpu.PrefetchScalarGridSpec(
            num_scalar_prefetch=1,
            grid=(4,),
            in_specs=[pl.BlockSpec((rows, 4 * width), lambda i, at: (0, at[i]))] * 4,
            out_specs=[pl.BlockSpec((4, rows, width), lambda i, at: (0, 0, 0))] * 4,
        ),
        out_shape=[jax.ShapeDtypeStruct((4, rows, width), jnp.bfloat16)] * 4,
        cost_estimate=BRIEF,
        name="adam_flips",
    )(at, *arrays)


def whole(kernel, out_shape, name, scalars, *arrays):
    vmem = pl.BlockSpec(memory_space=pltpu.VMEM)
    return pl.pallas_call(
        kernel,
        in_specs=[pl.BlockSpec(memory_space=pltpu.SMEM)] * len(scalars) + [vmem] * len(arrays),
        out_specs=jax.tree.map(lambda _: vmem, out_shape),
        out_shape=out_shape,
        compiler_params=pltpu.CompilerParams(vmem_limit_bytes=20 * 2**20),
        cost_estimate=BRIEF,
        name=name,
    )(*scalars, *arrays)


def regroup_kernel(*refs):
    for outer in range(4):
        for inner in range(4):
            refs[4 + inner][outer] = refs[outer][inner]


def regroup(parts):
    out = [jax.ShapeDtypeStruct(parts[0].shape, parts[0].dtype)] * 4
    return whole(regroup_kernel, out, "regroup", (), *parts)


def assemble_into(out_ref, at_ref, *refs):
    rows = refs[0].shape[1]
    for z_flip in range(4):
        for y_flip in range(4):
            source = at_ref[y_flip] * 4 + (at_ref[4] ^ z_flip)
            place = pl.ds(pl.multiple_of(source * rows, rows), rows)
            out_ref[place] = refs[z_flip][y_flip]


def swap_axes_kernel(*refs):
    for flip in range(4):
        for flip_z in range(2):
            refs[4 + flip_z][flip] = refs[flip][flip_z]


def swap_axes(parts):
    out = [jax.ShapeDtypeStruct((4, *parts[0].shape[1:]), parts[0].dtype)] * 2
    return whole(swap_axes_kernel, out, "swap", (), *parts)


def interleave_kernel(first_ref, second_ref, out_ref):
    for flip in range(4):
        out_ref[2 * flip] = first_ref[flip]
        out_ref[2 * flip + 1] = second_ref[flip]


def interleave(first, second):
    out = jax.ShapeDtypeStruct((8, *first.shape[1:]), first.dtype)
    return whole(interleave_kernel, out, "interleave", (), first, second)


def column_kernel(*refs):
    for at in range(refs[-1].shape[0]):
        rows = [ref[at].astype(jnp.float32) for ref in refs[:-1]]
        refs[-1][at] = jnp.concatenate(rows, axis=0).astype(jnp.bfloat16)


def join_rows(parts):
    blocks, rows, width = parts[0].shape
    out = jax.ShapeDtypeStruct((blocks, len(parts) * rows, width), parts[0].dtype)
    return whole(column_kernel, out, "column", (), *parts)


def attend_kernel(
    to_ref, lengths_ref, query_ref, input_ref, new_k_ref, new_v_ref, old_k_ref, old_v_ref,
    gain_ref, *refs,
):
    *out_refs, summed_ref, normed_ref = refs
    rows = STEPS * ROWS_HERE
    stacked = GROUP * rows

    def flat(ref):
        return ref[...].astype(jnp.float32).reshape(rows, ref.shape[2])

    queries, new_k, new_v = flat(query_ref), flat(new_k_ref), flat(new_v_ref)
    new_k, new_v = new_k.astype(jnp.bfloat16), new_v.astype(jnp.bfloat16)
    at = lax.broadcasted_iota(jnp.int32, (stacked, CTX), 0)
    position = lax.broadcasted_iota(jnp.int32, (stacked, CTX), 1)
    first_row = at % ROWS_HERE == 0
    visible = position < jnp.where(first_row, lengths_ref[0], lengths_ref[1])
    at_new = lax.broadcasted_iota(jnp.int32, (stacked, rows), 0)
    key_new = lax.broadcasted_iota(jnp.int32, (stacked, rows), 1)
    visible_new = (key_new % ROWS_HERE == at_new % ROWS_HERE) & (
        key_new // ROWS_HERE <= at_new // ROWS_HERE % STEPS
    )

    def scores(query, keys):
        found = lax.dot_general(
            query, keys, (((1,), (1,)), ((), ())), preferred_element_type=jnp.float32
        )
        return found * HD ** (-0.5)

    def weighted(probs, values):
        return jnp.dot(probs, values, preferred_element_type=jnp.float32)

    squares = jnp.zeros((rows, HD), jnp.float32)
    for group in range(KVH):
        cols = slice(group * HD, (group + 1) * HD)
        heads = [
            slice((group * GROUP + j) * HD, (group * GROUP + j + 1) * HD) for j in range(GROUP)
        ]
        query = jnp.concatenate([queries[:, head] for head in heads], axis=0).astype(jnp.bfloat16)
        old = jnp.where(
            first_row, scores(query, old_k_ref[0, :, cols]), scores(query, old_k_ref[1, :, cols])
        )
        old = jnp.where(visible, old, -1e30)
        new = jnp.where(visible_new, scores(query, new_k[:, cols]), -1e30)
        peak = jnp.maximum(
            jnp.max(old, axis=1, keepdims=True), jnp.max(new, axis=1, keepdims=True)
        )
        old, new = jnp.exp(old - peak), jnp.exp(new - peak)
        total = jnp.sum(old, axis=1, keepdims=True) + jnp.sum(new, axis=1, keepdims=True)
        old, new = old / total, new / total
        attended = weighted(
            jnp.where(first_row, old, 0.0).astype(jnp.bfloat16), old_v_ref[0, :, cols]
        )
        attended += weighted(
            jnp.where(first_row, 0.0, old).astype(jnp.bfloat16), old_v_ref[1, :, cols]
        )
        attended += weighted(new.astype(jnp.bfloat16), new_v[:, cols])
        for j, head in enumerate(heads):
            part = input_ref[:, :, head].astype(jnp.float32).reshape(rows, HD)
            part += attended[j * rows : (j + 1) * rows]
            summed_ref[:, head] = part
            squares += part * part
    factor = lax.rsqrt(jnp.sum(squares, axis=1, keepdims=True) / D + 1e-06)
    for block in range(8):
        cols = slice(block * 1024, (block + 1) * 1024)
        gain = gain_ref[:, cols].astype(jnp.float32)
        normed_ref[block] = summed_ref[:, cols] * factor * gain
    mine = pl.ds(pl.multiple_of(to_ref[8] * 512, 512), 512)
    its = pl.ds(pl.multiple_of((1 - to_ref[8]) * 512, 512), 512)
    for flip, out_ref in enumerate(out_refs):
        for flip_z in range(2):
            chip = to_ref[2 * flip + flip_z]
            out_ref[flip_z, :, :512] = normed_ref[chip, :, mine].astype(jnp.bfloat16)
            out_ref[flip_z, :, 512:] = normed_ref[chip, :, its].astype(jnp.bfloat16)


def attend(to, lengths, *arrays):
    rows = STEPS * ROWS_HERE
    smem, vmem = pl.BlockSpec(memory_space=pltpu.SMEM), pl.BlockSpec(memory_space=pltpu.VMEM)
    return pl.pallas_call(
        attend_kernel,
        in_specs=[smem] * 2 + [vmem] * len(arrays),
        out_specs=[vmem] * 4,
        out_shape=[jax.ShapeDtypeStruct((2, rows, 1024), jnp.bfloat16)] * 4,
        scratch_shapes=[
            pltpu.VMEM((rows, D), jnp.float32),
            pltpu.VMEM((8, rows, 1024), jnp.float32),
        ],
        compiler_params=pltpu.CompilerParams(vmem_limit_bytes=12 * 2**20),
        cost_estimate=BRIEF,
        name="attend",
    )(to, lengths, *arrays)


def product_kernel(*refs):
    row_refs = refs[:4]
    own_ref, other_ref, send_a, keep_a, send_b, keep_b, new_ref = refs[4:]
    new_ref[...] = own_ref[...]
    half = own_ref.shape[1] // 2
    depth = own_ref.shape[0]
    for flip in (3, 1, 2, 0):
        rows = jnp.concatenate(
            [ref[2 * flip + flip_z] for flip_z in range(2) for ref in row_refs], axis=0
        )
        total = jnp.dot(rows[:, :depth], own_ref[...], preferred_element_type=jnp.float32)
        total += jnp.dot(rows[:, depth:], other_ref[...], preferred_element_type=jnp.float32)
        term = (total * D ** (-0.5)).astype(jnp.bfloat16).reshape(2, 128, 2 * half)
        (send_a if flip & 1 else keep_a)[flip >> 1] = term[:, :, :half]
        (send_b if flip & 2 else keep_b)[flip & 1] = term[:, :, half:]


def product_kernel_and_next(at_ref, *refs):
    *refs, next_ref = refs
    assemble_into(next_ref, at_ref, *refs[6:10])
    product_kernel(*refs[:6], *refs[10:])


def products(row_parts, own, other, at=None, next_parts=()):
    half = own.shape[1] // 2
    out = jax.ShapeDtypeStruct((2, 2, 128, half), jnp.bfloat16)
    whole_own = jax.ShapeDtypeStruct(own.shape, own.dtype)
    arrays = (*row_parts, own, other, *next_parts)
    if next_parts:
        return whole(
            product_kernel_and_next, [out] * 4 + [whole_own] * 2, "products", (at,), *arrays
        )
    return whole(product_kernel, [out] * 4 + [whole_own], "products", (), *arrays)


def add(kept, arrived):
    return kept.astype(jnp.float32) + arrived.astype(jnp.float32)


def over_z(parts):
    return [parts[0]] + [lax.ppermute(parts[k], "mp", mp_swap(0, k)) for k in (1, 2, 3)]


def over_y(parts):
    return [parts[0]] + [lax.ppermute(parts[k], "mp", mp_swap(k, 0)) for k in (1, 2, 3)]


def swap_core(own):
    return lax.ppermute(own, "dp", dp_swap(0, 0, 1))


def first_sums(parts):
    send_a, keep_a, send_b, keep_b = parts
    got_a = lax.ppermute(send_a, "dp", dp_swap(1, 0, 0))
    got_b = lax.ppermute(send_b, "dp", dp_swap(2, 0, 0))
    return add(keep_a, got_a), add(keep_b, got_b)


def second_sums(sum_a, sum_b):
    got_a = lax.ppermute(sum_a[1].astype(jnp.bfloat16), "dp", dp_swap(2, 0, 0))
    got_b = lax.ppermute(sum_b[1].astype(jnp.bfloat16), "dp", dp_swap(1, 0, 0))
    return jnp.concatenate([add(sum_a[0], got_a), add(sum_b[0], got_b)], axis=-1)


def last_sum(both):
    return add(both[0], lax.ppermute(both[1].astype(jnp.bfloat16), "dp", dp_swap(0, 1, 0)))


def local(
    weight_gate,
    weight_up,
    grad_gate,
    grad_up,
    moment_gate,
    moment_up,
    second_gate,
    second_up,
    layer_input,
    queries,
    fresh_keys,
    fresh_values,
    cached_keys,
    cached_values,
    lengths,
    norm_gain,
):
    dp = lax.axis_index("dp")
    mp = lax.axis_index("mp")
    x, z_hi, core = dp // 4, dp // 2 % 2, dp % 2
    y, z_lo = mp // 4, mp % 4
    gray_x, gray_y = x ^ (x >> 1), y ^ (y >> 1)

    def place(gray):
        return gray ^ (gray >> 1)

    at = jnp.stack([place(gray_y ^ flip) for flip in range(4)] + [z_lo]).astype(jnp.int32)
    to = jnp.stack(
        [place(gray_x ^ flip) * 2 + (z_hi ^ flip_z) for flip in range(4) for flip_z in range(2)]
        + [core]
    ).astype(jnp.int32)

    gate_step = adam_places(weight_gate, grad_gate, moment_gate, second_gate)
    gate_step, queries = lax.optimization_barrier((gate_step, queries))
    gate_own = lax.all_to_all(gate_step, "mp", split_axis=0, concat_axis=0, tiled=True)
    gate_own = gate_own.reshape(512, 1024)

    by_x = attend(
        to, lengths, queries, layer_input, fresh_keys, fresh_values, cached_keys, cached_values,
        norm_gain.reshape(1, D),
    )
    by_x, weight_up = lax.optimization_barrier((by_x, weight_up))
    up_parts = adam_flips(at, weight_up, grad_up, moment_up, second_up)
    by_x, up_parts = lax.optimization_barrier((by_x, up_parts))
    up_parts = over_y(up_parts)
    by_x = [by_x[0]] + [lax.ppermute(by_x[k], "dp", dp_swap(k, 0, 0)) for k in (1, 2, 3)]
    here, there = swap_axes(by_x)
    spread = interleave(here, lax.ppermute(there, "dp", dp_swap(0, 1, 0)))
    along_z = over_z([spread] * 4)
    column, up_parts, gate_own = lax.optimization_barrier(
        (join_rows(along_z), up_parts, gate_own)
    )
    gate_other = swap_core(gate_own)
    row_parts = over_y([column] * 4)
    up_parts = over_z(regroup(up_parts))
    *gate_terms, gate_new, up_own = products(row_parts, gate_own, gate_other, at, up_parts)
    *up_terms, up_new = products(row_parts, up_own, swap_core(up_own))

    gate_terms[1], gate_terms[3], up_new = lax.optimization_barrier(
        (gate_terms[1], gate_terms[3], up_new)
    )
    gate_both = second_sums(*first_sums(gate_terms))
    up_both = second_sums(*first_sums(up_terms))
    gate_total, up_both = lax.optimization_barrier((last_sum(gate_both), up_both))
    up_total = last_sum(up_both)
    hidden = (jax.nn.silu(gate_total) * up_total).astype(jnp.bfloat16)

    row = jnp.arange(128)
    y_flip, z_flip, step_at, row_at = row // 32, row // 8 % 4, row // 2 % 4, row % 2
    target = step_at * 32 + (place(gray_y ^ y_flip) * 4 + (z_lo ^ z_flip)) * 2 + row_at
    placed = (row[:, None] == target[None, :]).astype(jnp.bfloat16)
    hidden = jnp.dot(placed, hidden, preferred_element_type=jnp.float32).astype(jnp.bfloat16)
    return gate_new, up_new, hidden.reshape(STEPS, 32, 1024)


def solution(mesh):
    rows = P(("dp", "mp"), None)
    steps = P(None, ("dp", "mp"), None)
    cache = P(("dp", "mp"), None, None)
    in_specs = (rows,) * 8 + (steps,) * 4 + (cache,) * 2 + (P(("dp", "mp")), P())
    out_specs = (P("dp", "mp"), P("dp", "mp"), P(None, "dp", "mp"))
    return jax.shard_map(local, mesh=mesh, in_specs=in_specs, out_specs=out_specs, check_vma=False)
```

time: 197 us -> 151 us (0.77)
  waiting for transfers between devices: 110 us -> 72.8 us
  local copies, waits for them, and re-layouts: 7.97 us -> 1.6 us
  starting transfers between devices: 47.6 us -> 51.8 us
  matrix products: 4.03 us -> 1.04 us
  other arithmetic: 3.52 us -> 1.08 us
    ppermute x18 -> x28, starting transfers between devices: 23.2 us -> 43 us  [the longest x2 8.93 us: last_sum(): lax.ppermute(both[1].astype(jnp.bfloat16), 'dp', dp_swap(0, 1, 0))]
    all_to_all x3 -> x1, waiting for transfers between devices: 19.4 us -> 0.01 us  [local(): lax.all_to_all(gate_step, 'mp', split_axis=0, concat_axis=0, tiled=True)]
    ppermute x18 -> x28, waiting for transfers between devices: 90.8 us -> 72.8 us  [the longest x6 27.9 us: over_z(): lax.ppermute(parts[k], 'mp', mp_swap(0, k))]
    all_to_all x3 -> x1, starting transfers between devices: 24.4 us -> 8.8 us  [local(): lax.all_to_all(gate_step, 'mp', split_axis=0, concat_axis=0, tiled=True)]
    unnamed x23 -> x22, local copies, waits for them, and re-layouts: 6.35 us -> 0.7 us
    pallas_call x4 -> x9, Pallas kernels: 21.3 us -> 21.1 us  [the longest x6 7.37 us: whole(): pl.pallas_call(kernel, in_specs=[pl.BlockSpec(memory_space=pltpu.SMEM)] *...]
  transfers between devices with their start and end apart: 21 -> 29, of which waited for: 13 -> 20; matrix products, arithmetic and copies ran while one was open for 1% -> 1% of each run, Pallas kernels for 11% -> 8%
where the time goes in v2:
time: 151 us; the launch traced here: 150 us
  waiting for transfers between devices  72.8 us (48%)
  starting transfers between devices  51.8 us (34%)
  Pallas kernels  21.1 us (14%)
  local copies, waits for them, and re-layouts  1.6 us (1%)
    ppermute x6, waiting for transfers between devices, over_z(): lax.ppermute(parts[k], 'mp', mp_swap(0, k))  27.9 us
    ppermute x2, waiting for transfers between devices, first_sums(): got_a = lax.ppermute(send_a, 'dp', dp_swap(1, 0, 0))  13 us
    ppermute x2, waiting for transfers between devices, last_sum(): lax.ppermute(both[1].astype(jnp.bfloat16), 'dp', dp_swap(0, 1, 0))  12.6 us
    ppermute x2, starting transfers between devices, last_sum(): lax.ppermute(both[1].astype(jnp.bfloat16), 'dp', dp_swap(0, 1, 0))  8.93 us
    ppermute x6, starting transfers between devices, over_y(): lax.ppermute(parts[k], 'mp', mp_swap(k, 0))  8.81 us
    all_to_all x1, starting transfers between devices, local(): lax.all_to_all(gate_step, 'mp', split_axis=0, concat_axis=0, tiled=True)  8.8 us
    ppermute x2, waiting for transfers between devices, second_sums(): got_a = lax.ppermute(sum_a[1].astype(jnp.bfloat16), 'dp', dp_swap(2, 0, 0))  7.88 us
    pallas_call x6, Pallas kernels, whole(): pl.pallas_call(kernel, in_specs=[pl.BlockSpec(memory_space=pltpu.SMEM)] *...  7.37 us
  transfers between devices with their start and end apart: 29, of which 20 were waited for; matrix products, arithmetic and copies ran while one was open for 1% of the time, Pallas kernels for 8%

profile of v2, /device:TPU:32, one launch (start us, length us, event | category | flops | bytes accessed | tf_op | source)
XLA Modules:
  0.0 150.5 jit_solution(11701044524118945615)
XLA Ops:
  0.6 4.6 %adam_places.1 = bf16[16,32,1024]{2,1,0:T(8,128)(2,1)} custom-call(bf16[32,16384]{1,0:T(8,128)(2,1)} %refs_0_.1, bf16[32,16384]{1,0:T(8,128)(2,1)} %refs_1_.2, bf16[32,16384]{1,0:T(8,128)(2,1)} %refs_2_.2, bf16[32,16384]{1,0:T(8,128)(2,1)} %refs_3_.2), custom_call_target="tpu_custom_call" | custom-call | flops 1 | bytes 1 | tf_op jit(solution)/shard_map/adam_places/pallas_call | solution.py:70
  5.2 8.8 %all-to-all-start = ((bf16[16,32,1024]{2,1,0:T(8,128)(2,1)}), bf16[16,32,1024]{2,1,0:T(8,128)(2,1)S(1)}, u32[]{:S(2)}, u32[]{:S(2)}) async-start(bf16[16,32,1024]{2,1,0:T(8,128)(2,1)} %adam_places.1), calls=%async_computation | async-start | bytes 2097152 | tf_op jit(solution)/shard_map/all_to_all | solution.py:375
  14.2 0.1 stack.63.to_ref
  14.3 0.6 copy-done.3
  14.9 3.7 %attend.1 = (bf16[2,8,1024]{2,1,0:T(8,128)(2,1)S(1)}, bf16[2,8,1024]{2,1,0:T(8,128)(2,1)S(1)}, bf16[2,8,1024]{2,1,0:T(8,128)(2,1)S(1)}, bf16[2,8,1024]{2,1,0:T(8,128)(2,1)S(1)}) custom-call(s32[9]{0:T(128)S(1)} %stack.63.to_ref, s32[2]{0:T(128)S(1)} %copy-done.8, bf16[4,2,8192]{2,1,0:T(2,128)(2,1)S(1)} %copy-done.3, bf16[4,2,8192]{2,1,0:T(2,128)(2,1)S(1)} %copy-done.4, ...), custom_call_target="tpu_custom_call" | custom-call | flops 1 | bytes 1 | tf_op jit(solution)/shard_map/attend/pallas_call | solution.py:257
  18.6 0.6 stack.53.at_ref
  19.3 5.5 %adam_flips.1 = (bf16[4,32,1024]{2,1,0:T(8,128)(2,1)}, bf16[4,32,1024]{2,1,0:T(8,128)(2,1)}, bf16[4,32,1024]{2,1,0:T(8,128)(2,1)}, bf16[4,32,1024]{2,1,0:T(8,128)(2,1)}) custom-call(s32[5]{0:T(128)} %stack.53.at_ref, bf16[32,16384]{1,0:T(8,128)(2,1)} %refs_0_.2, bf16[32,16384]{1,0:T(8,128)(2,1)} %refs_1_.3, bf16[32,16384]{1,0:T(8,128)(2,1)} %refs_2_.3, ...), custom_call_target="tpu_custom_call" | custom-call | flops 1 | bytes 1 | tf_op jit(solution)/shard_map/adam_flips/pallas_call | solution.py:97
  24.8 1.5 collective-permute-start
  26.3 2.1 %collective-permute-start.1 = (bf16[2,8,1024]{2,1,0:T(8,128)(2,1)S(1)}, bf16[2,8,1024]{2,1,0:T(8,128)(2,1)S(1)}, u32[]{:S(2)}, u32[]{:S(2)}) collective-permute-start(bf16[2,8,1024]{2,1,0:T(8,128)(2,1)S(1)} %get-tuple-element.70), channel_id=1, source_target_pairs={{0,192},{16,208},{32,224},{48,240},{64,128},{80,144},{96,160},{112... | collective-permute-start | bytes 98312 | tf_op jit(solution)/shard_map/ppermute | solution.py:386
  28.4 0.6 collective-permute-start.2
  29.0 2.7 %collective-permute-done.1.refs_2_ = bf16[2,8,1024]{2,1,0:T(8,128)(2,1)S(1)} collective-permute-done((bf16[2,8,1024]{2,1,0:T(8,128)(2,1)S(1)}, bf16[2,8,1024]{2,1,0:T(8,128)(2,1)S(1)}, u32[]{:S(2)}, u32[]{:S(2)}) %collective-permute-start.1) | collective-permute-done | bytes 32800 | tf_op jit(solution)/shard_map/ppermute | solution.py:386
  31.8 2.0 %collective-permute-done.2.refs_3_ = bf16[2,8,1024]{2,1,0:T(8,128)(2,1)S(1)} collective-permute-done((bf16[2,8,1024]{2,1,0:T(8,128)(2,1)S(1)}, bf16[2,8,1024]{2,1,0:T(8,128)(2,1)S(1)}, u32[]{:S(2)}, u32[]{:S(2)}) %collective-permute-start.2) | collective-permute-done | bytes 32800 | tf_op jit(solution)/shard_map/ppermute | solution.py:386
  33.8 4.6 %collective-permute-start.3 = (bf16[4,8,1024]{2,1,0:T(8,128)(2,1)S(1)}, bf16[4,8,1024]{2,1,0:T(8,128)(2,1)S(1)}, u32[]{:S(2)}, u32[]{:S(2)}) collective-permute-start(bf16[4,8,1024]{2,1,0:T(8,128)(2,1)S(1)} %get-tuple-element.73), channel_id=1, source_target_pairs={{0,32},{16,48},{32,0},{48,16},{64,96},{80,112},{96,64},{112,80},{1... | collective-permute-start | bytes 196616 | tf_op jit(solution)/shard_map/ppermute | solution.py:388
  38.4 4.0 %collective-permute-done.3.second_ref = bf16[4,8,1024]{2,1,0:T(8,128)(2,1)S(1)} collective-permute-done((bf16[4,8,1024]{2,1,0:T(8,128)(2,1)S(1)}, bf16[4,8,1024]{2,1,0:T(8,128)(2,1)S(1)}, u32[]{:S(2)}, u32[]{:S(2)}) %collective-permute-start.3) | collective-permute-done | bytes 65568 | tf_op jit(solution)/shard_map/ppermute | solution.py:388
  42.5 2.5 %collective-permute-start.6 = (bf16[8,8,1024]{2,1,0:T(8,128)(2,1)S(1)}, bf16[8,8,1024]{2,1,0:T(8,128)(2,1)S(1)}, u32[]{:S(2)}, u32[]{:S(2)}) collective-permute-start(bf16[8,8,1024]{2,1,0:T(8,128)(2,1)S(1)} %interleave.1.refs_0_), channel_id=1, source_target_pairs={{0,3},{1,2},{2,1},{3,0},{4,7},{5,6},{6,5},{7,4},{8,11},{9,10},{10,... | collective-permute-start | bytes 393224 | tf_op jit(solution)/shard_map/ppermute | solution.py:312
  44.9 1.7 %collective-permute-start.7 = (bf16[4,32,1024]{2,1,0:T(8,128)(2,1)}, bf16[4,32,1024]{2,1,0:T(8,128)(2,1)S(1)}, u32[]{:S(2)}, u32[]{:S(2)}) collective-permute-start(bf16[4,32,1024]{2,1,0:T(8,128)(2,1)} %get-tuple-element.75), channel_id=1, source_target_pairs={{0,4},{1,5},{2,6},{3,7},{4,0},{5,1},{6,2},{7,3},{8,12},{9,13},{10,... | collective-permute-start | bytes 786440 | tf_op jit(solution)/shard_map/ppermute | solution.py:316
  46.6 2.1 %collective-permute-start.8 = (bf16[4,32,1024]{2,1,0:T(8,128)(2,1)}, bf16[4,32,1024]{2,1,0:T(8,128)(2,1)S(1)}, u32[]{:S(2)}, u32[]{:S(2)}) collective-permute-start(bf16[4,32,1024]{2,1,0:T(8,128)(2,1)} %get-tuple-element.76), channel_id=1, source_target_pairs={{0,12},{1,13},{2,14},{3,15},{4,8},{5,9},{6,10},{7,11},{8,4},{9,5},... | collective-permute-start | bytes 786440 | tf_op jit(solution)/shard_map/ppermute | solution.py:316
  48.7 0.6 collective-permute-start.9
  49.3 0.2 collective-permute-start.5
  49.4 2.4 %collective-permute-done.6.refs_3_ = bf16[8,8,1024]{2,1,0:T(8,128)(2,1)S(1)} collective-permute-done((bf16[8,8,1024]{2,1,0:T(8,128)(2,1)S(1)}, bf16[8,8,1024]{2,1,0:T(8,128)(2,1)S(1)}, u32[]{:S(2)}, u32[]{:S(2)}) %collective-permute-start.6) | collective-permute-done | bytes 131104 | tf_op jit(solution)/shard_map/ppermute | solution.py:312
  51.8 3.4 %collective-permute-done.5.refs_2_ = bf16[8,8,1024]{2,1,0:T(8,128)(2,1)S(1)} collective-permute-done((bf16[8,8,1024]{2,1,0:T(8,128)(2,1)S(1)}, bf16[8,8,1024]{2,1,0:T(8,128)(2,1)S(1)}, u32[]{:S(2)}, u32[]{:S(2)}) %collective-permute-start.5) | collective-permute-done | bytes 131104 | tf_op jit(solution)/shard_map/ppermute | solution.py:312
  55.3 1.6 %collective-permute-done.4.refs_1_ = bf16[8,8,1024]{2,1,0:T(8,128)(2,1)S(1)} collective-permute-done((bf16[8,8,1024]{2,1,0:T(8,128)(2,1)S(1)}, bf16[8,8,1024]{2,1,0:T(8,128)(2,1)S(1)}, u32[]{:S(2)}, u32[]{:S(2)}) %collective-permute-start.4) | collective-permute-done | bytes 131104 | tf_op jit(solution)/shard_map/ppermute | solution.py:312
  56.9 0.3 collective-permute-done.8.refs_2_
  57.3 1.9 %collective-permute-start.14 = (bf16[4,32,1024]{2,1,0:T(8,128)(2,1)S(1)}, bf16[4,32,1024]{2,1,0:T(8,128)(2,1)S(1)}, u32[]{:S(2)}, u32[]{:S(2)}) collective-permute-start(bf16[4,32,1024]{2,1,0:T(8,128)(2,1)S(1)} %get-tuple-element.86), channel_id=1, source_target_pairs={{0,1},{1,0},{2,3},{3,2},{4,5},{5,4},{6,7},{7,6},{8,9},{9,8},{10,11... | collective-permute-start | bytes 786440 | tf_op jit(solution)/shard_map/ppermute | solution.py:312
  59.2 0.9 collective-permute-start.15
  60.1 2.7 %collective-permute-start.12 = (bf16[8,32,1024]{2,1,0:T(8,128)(2,1)S(1)}, bf16[8,32,1024]{2,1,0:T(8,128)(2,1)S(1)}, u32[]{:S(2)}, u32[]{:S(2)}) collective-permute-start(bf16[8,32,1024]{2,1,0:T(8,128)(2,1)S(1)} %column.1.refs_0_), channel_id=1, source_target_pairs={{0,8},{1,9},{2,10},{3,11},{4,12},{5,13},{6,14},{7,15},{8,0},{9,1},... | collective-permute-start | bytes 1572872 | tf_op jit(solution)/shard_map/ppermute | solution.py:316
  62.8 1.2 collective-permute-start.11
  63.9 6.4 %collective-permute-done.14.refs_7_ = bf16[4,32,1024]{2,1,0:T(8,128)(2,1)S(1)} collective-permute-done((bf16[4,32,1024]{2,1,0:T(8,128)(2,1)S(1)}, bf16[4,32,1024]{2,1,0:T(8,128)(2,1)S(1)}, u32[]{:S(2)}, u32[]{:S(2)}) %collective-permute-start.14) | collective-permute-done | bytes 262176 | tf_op jit(solution)/shard_map/ppermute | solution.py:312
  70.4 0.5 collective-permute-start.10
  70.9 1.5 %collective-permute-done.15.refs_8_ = bf16[4,32,1024]{2,1,0:T(8,128)(2,1)S(1)} collective-permute-done((bf16[4,32,1024]{2,1,0:T(8,128)(2,1)S(1)}, bf16[4,32,1024]{2,1,0:T(8,128)(2,1)S(1)}, u32[]{:S(2)}, u32[]{:S(2)}) %collective-permute-start.15) | collective-permute-done | bytes 262176 | tf_op jit(solution)/shard_map/ppermute | solution.py:312
  72.4 0.9 collective-permute-start.16
  73.3 12.6 %collective-permute-done.16.refs_9_ = bf16[4,32,1024]{2,1,0:T(8,128)(2,1)S(1)} collective-permute-done((bf16[4,32,1024]{2,1,0:T(8,128)(2,1)S(1)}, bf16[4,32,1024]{2,1,0:T(8,128)(2,1)S(1)}, u32[]{:S(2)}, u32[]{:S(2)}) %collective-permute-start.16) | collective-permute-done | bytes 262176 | tf_op jit(solution)/shard_map/ppermute | solution.py:312
  85.9 0.6 collective-permute-done.11.refs_2_
  86.6 3.9 %products.2 = (bf16[2,2,128,512]{3,2,1,0:T(8,128)(2,1)S(1)}, bf16[2,2,128,512]{3,2,1,0:T(8,128)(2,1)S(1)}, bf16[2,2,128,512]{3,2,1,0:T(8,128)(2,1)S(1)}, bf16[2,...) custom-call(s32[5]{0:T(128)S(1)} %copy-done.7, ...), custom_call_target="tpu_custom_call" | custom-call | flops 1 | bytes 1 | tf_op jit(solution)/shard_map/products/pallas_call | solution.py:113
  90.5 0.8 collective-permute-start.18
  91.3 2.0 %collective-permute-start.20 = (bf16[2,2,128,512]{3,2,1,0:T(8,128)(2,1)S(1)}, bf16[2,2,128,512]{3,2,1,0:T(8,128)(2,1)S(1)}, u32[]{:S(2)}, u32[]{:S(2)}) collective-permute-start(bf16[2,2,128,512]{3,2,1,0:T(8,128)(2,1)S(1)} %get-tuple-element.98), channel_id=1, source_target_pairs={{0,192},{16,208},{32,224},{48,240},{64,128},{80,144},{96,160},{112... | collective-permute-start | bytes 1572872 | tf_op jit(solution)/shard_map/ppermute | solution.py:326
  93.3 3.3 %products.3 = (bf16[2,2,128,512]{3,2,1,0:T(8,128)(2,1)S(1)}, bf16[2,2,128,512]{3,2,1,0:T(8,128)(2,1)S(1)}, bf16[2,2,128,512]{3,2,1,0:T(8,128)(2,1)S(1)}, bf16[2,...) custom-call(bf16[8,32,1024]{2,1,0:T(8,128)(2,1)S(1)} %column.1.refs_0_, ...), custom_call_target="tpu_custom_call" | custom-call | flops 1 | bytes 1 | tf_op jit(solution)/shard_map/products/pallas_call | solution.py:113
  96.6 8.2 %collective-permute-done.18 = bf16[2,2,128,512]{3,2,1,0:T(8,128)(2,1)S(1)} collective-permute-done((bf16[2,2,128,512]{3,2,1,0:T(8,128)(2,1)S(1)}, bf16[2,2,128,512]{3,2,1,0:T(8,128)(2,1)S(1)}, u32[]{:S(2)}, u32[]{:S(2)}) %collective-permute-start.18) | collective-permute-done | bytes 524320 | tf_op jit(solution)/shard_map/ppermute | solution.py:325
  104.8 0.2 convert_add_fusion.3
  105.0 1.1 collective-permute-start.19
  106.1 0.4 collective-permute-done.20
  106.5 0.2 convert_add_fusion.2
  106.7 0.9 collective-permute-start.21
  107.6 1.2 collective-permute-start.23
  108.9 2.0 %collective-permute-start.25 = (bf16[2,2,128,512]{3,2,1,0:T(8,128)(2,1)S(1)}, bf16[2,2,128,512]{3,2,1,0:T(8,128)(2,1)S(1)}, u32[]{:S(2)}, u32[]{:S(2)}) collective-permute-start(bf16[2,2,128,512]{3,2,1,0:T(8,128)(2,1)S(1)} %get-tuple-element.102), channel_id=1, source_target_pairs={{0,192},{16,208},{32,224},{48,240},{64,128},{80,144},{96,160},{112... | collective-permute-start | bytes 1572872 | tf_op jit(solution)/shard_map/ppermute | solution.py:326
  110.8 4.7 %collective-permute-done.19 = bf16[2,128,512]{2,1,0:T(8,128)(2,1)S(1)} collective-permute-done((bf16[2,128,512]{2,1,0:T(8,128)(2,1)S(1)}, bf16[2,128,512]{2,1,0:T(8,128)(2,1)S(1)}, u32[]{:S(2)}, u32[]{:S(2)}) %collective-permute-start.19) | collective-permute-done | bytes 262176 | tf_op jit(solution)/shard_map/ppermute | solution.py:331
  115.5 0.1 fusion.7
  115.6 0.5 collective-permute-done.21
  116.1 0.1 fusion.6
  116.2 4.7 %collective-permute-start.22 = (bf16[128,1024]{1,0:T(8,128)(2,1)S(1)}, bf16[128,1024]{1,0:T(8,128)(2,1)S(1)}, u32[]{:S(2)}, u32[]{:S(2)}) collective-permute-start(bf16[128,1024]{1,0:T(8,128)(2,1)S(1)} %fusion.12), channel_id=1, source_target_pairs={{0,32},{16,48},{32,0},{48,16},{64,96},{80,112},{96,64},{112,80},{1... | collective-permute-start | bytes 786440 | tf_op jit(solution)/shard_map/ppermute | solution.py:337
  120.9 4.8 %collective-permute-done.23 = bf16[2,2,128,512]{3,2,1,0:T(8,128)(2,1)S(1)} collective-permute-done((bf16[2,2,128,512]{3,2,1,0:T(8,128)(2,1)S(1)}, bf16[2,2,128,512]{3,2,1,0:T(8,128)(2,1)S(1)}, u32[]{:S(2)}, u32[]{:S(2)}) %collective-permute-start.23) | collective-permute-done | bytes 524320 | tf_op jit(solution)/shard_map/ppermute | solution.py:325
  125.7 0.2 convert_add_fusion.1
  125.9 2.1 %collective-permute-start.24 = (bf16[2,128,512]{2,1,0:T(8,128)(2,1)S(1)}, bf16[2,128,512]{2,1,0:T(8,128)(2,1)S(1)}, u32[]{:S(2)}, u32[]{:S(2)}) collective-permute-start(bf16[2,128,512]{2,1,0:T(8,128)(2,1)S(1)} %fusion.13), channel_id=1, source_target_pairs={{0,192},{16,208},{32,224},{48,240},{64,128},{80,144},{96,160},{112... | collective-permute-start | bytes 786440 | tf_op jit(solution)/shard_map/ppermute | solution.py:331
  128.0 0.2 convert_add_fusion
  128.2 0.1 collective-permute-start.26
  128.3 2.3 %collective-permute-done.22 = bf16[128,1024]{1,0:T(8,128)(2,1)S(1)} collective-permute-done((bf16[128,1024]{1,0:T(8,128)(2,1)S(1)}, bf16[128,1024]{1,0:T(8,128)(2,1)S(1)}, u32[]{:S(2)}, u32[]{:S(2)}) %collective-permute-start.22) | collective-permute-done | bytes 262176 | tf_op jit(solution)/shard_map/ppermute | solution.py:337
  130.7 3.2 %collective-permute-done.24 = bf16[2,128,512]{2,1,0:T(8,128)(2,1)S(1)} collective-permute-done((bf16[2,128,512]{2,1,0:T(8,128)(2,1)S(1)}, bf16[2,128,512]{2,1,0:T(8,128)(2,1)S(1)}, u32[]{:S(2)}, u32[]{:S(2)}) %collective-permute-start.24) | collective-permute-done | bytes 262176 | tf_op jit(solution)/shard_map/ppermute | solution.py:331
  133.9 0.1 fusion.4
  133.9 0.7 collective-permute-done.26
  134.7 0.1 fusion.3
  134.8 0.1 pad_maximum_fusion
  134.9 4.3 %collective-permute-start.27 = (bf16[128,1024]{1,0:T(8,128)(2,1)S(1)}, bf16[128,1024]{1,0:T(8,128)(2,1)S(1)}, u32[]{:S(2)}, u32[]{:S(2)}) collective-permute-start(bf16[128,1024]{1,0:T(8,128)(2,1)S(1)} %fusion.15), channel_id=1, source_target_pairs={{0,32},{16,48},{32,0},{48,16},{64,96},{80,112},{96,64},{112,80},{1... | collective-permute-start | bytes 786440 | tf_op jit(solution)/shard_map/ppermute | solution.py:337
  139.2 10.3 %collective-permute-done.27 = bf16[128,1024]{1,0:T(8,128)(2,1)S(1)} collective-permute-done((bf16[128,1024]{1,0:T(8,128)(2,1)S(1)}, bf16[128,1024]{1,0:T(8,128)(2,1)S(1)}, u32[]{:S(2)}, u32[]{:S(2)}) %collective-permute-start.27) | collective-permute-done | bytes 262176 | tf_op jit(solution)/shard_map/ppermute | solution.py:337
  149.4 1.0 convolution_convert_fusion
  (46 shorter events, 0.5 us)
Async XLA Ops:
  5.2 8.9 %copy-start.9 = (bf16[8192]{0:T(1024)(128)(2,1)S(1)}, bf16[8192]{0:T(1024)(128)(2,1)}, u32[]{:S(2)}) copy-start(bf16[8192]{0:T(1024)(128)(2,1)} %param.31) | copy-start | bytes 49156
  5.2 9.1 %copy-start = (bf16[2,128,1024]{2,1,0:T(8,128)(2,1)S(1)}, bf16[2,128,1024]{2,1,0:T(8,128)(2,1)}, u32[]{:S(2)}) copy-start(bf16[2,128,1024]{2,1,0:T(8,128)(2,1)} %old_k_ref.1) | copy-start | bytes 1572868
  5.2 9.1 %copy-start.1 = (bf16[2,128,1024]{2,1,0:T(8,128)(2,1)S(1)}, bf16[2,128,1024]{2,1,0:T(8,128)(2,1)}, u32[]{:S(2)}) copy-start(bf16[2,128,1024]{2,1,0:T(8,128)(2,1)} %old_v_ref.1) | copy-start | bytes 1572868
  5.2 9.1 %copy-start.4 = (bf16[4,2,8192]{2,1,0:T(2,128)(2,1)S(1)}, bf16[4,2,8192]{2,1,0:T(2,128)(2,1)}, u32[]{:S(2)}) copy-start(bf16[4,2,8192]{2,1,0:T(2,128)(2,1)} %input_ref.1) | copy-start | bytes 393220
  5.2 52.0 %all-to-all-start = ((bf16[16,32,1024]{2,1,0:T(8,128)(2,1)}), bf16[16,32,1024]{2,1,0:T(8,128)(2,1)S(1)}, u32[]{:S(2)}, u32[]{:S(2)}) async-start(bf16[16,32,1024]{2,1,0:T(8,128)(2,1)} %adam_places.1), calls=%async_computation | async-start | bytes 2097152 | tf_op jit(solution)/shard_map/all_to_all | solution.py:375
  14.0 0.9 copy-start.3
  14.1 0.8 copy-start.6
  14.1 0.8 copy-start.5
  14.1 0.8 copy-start.8
  24.8 23.9 %copy-start.10 = (bf16[4,32,1024]{2,1,0:T(8,128)(2,1)S(1)}, bf16[4,32,1024]{2,1,0:T(8,128)(2,1)}, u32[]{:S(2)}) copy-start(bf16[4,32,1024]{2,1,0:T(8,128)(2,1)} %get-tuple-element.77) | copy-start | bytes 786436
  24.8 4.2 %collective-permute-start = (bf16[2,8,1024]{2,1,0:T(8,128)(2,1)S(1)}, bf16[2,8,1024]{2,1,0:T(8,128)(2,1)S(1)}, u32[]{:S(2)}, u32[]{:S(2)}) collective-permute-start(bf16[2,8,1024]{2,1,0:T(8,128)(2,1)S(1)} %get-tuple-element.69), channel_id=1, source_target_pairs={{0,64},{16,80},{32,96},{48,112},{64,0},{80,16},{96,32},{112,48},{1... | collective-permute-start | bytes 98312 | tf_op jit(solution)/shard_map/ppermute | solution.py:386
  26.3 5.5 %collective-permute-start.1 = (bf16[2,8,1024]{2,1,0:T(8,128)(2,1)S(1)}, bf16[2,8,1024]{2,1,0:T(8,128)(2,1)S(1)}, u32[]{:S(2)}, u32[]{:S(2)}) collective-permute-start(bf16[2,8,1024]{2,1,0:T(8,128)(2,1)S(1)} %get-tuple-element.70), channel_id=1, source_target_pairs={{0,192},{16,208},{32,224},{48,240},{64,128},{80,144},{96,160},{112... | collective-permute-start | bytes 98312 | tf_op jit(solution)/shard_map/ppermute | solution.py:386
  28.4 5.4 %collective-permute-start.2 = (bf16[2,8,1024]{2,1,0:T(8,128)(2,1)S(1)}, bf16[2,8,1024]{2,1,0:T(8,128)(2,1)S(1)}, u32[]{:S(2)}, u32[]{:S(2)}) collective-permute-start(bf16[2,8,1024]{2,1,0:T(8,128)(2,1)S(1)} %get-tuple-element.71), channel_id=1, source_target_pairs={{0,128},{16,144},{32,160},{48,176},{64,192},{80,208},{96,224},{112... | collective-permute-start | bytes 98312 | tf_op jit(solution)/shard_map/ppermute | solution.py:386
  33.8 8.6 %collective-permute-start.3 = (bf16[4,8,1024]{2,1,0:T(8,128)(2,1)S(1)}, bf16[4,8,1024]{2,1,0:T(8,128)(2,1)S(1)}, u32[]{:S(2)}, u32[]{:S(2)}) collective-permute-start(bf16[4,8,1024]{2,1,0:T(8,128)(2,1)S(1)} %get-tuple-element.73), channel_id=1, source_target_pairs={{0,32},{16,48},{32,0},{48,16},{64,96},{80,112},{96,64},{112,80},{1... | collective-permute-start | bytes 196616 | tf_op jit(solution)/shard_map/ppermute | solution.py:388
  42.4 14.8 %copy-start.2 = (bf16[4,32,1024]{2,1,0:T(8,128)(2,1)S(1)}, bf16[4,32,1024]{2,1,0:T(8,128)(2,1)}, u32[]{:S(2)}) copy-start(bf16[4,32,1024]{2,1,0:T(8,128)(2,1)} %get-tuple-element.81.refs_0_) | copy-start | bytes 786436
  42.5 9.4 %collective-permute-start.6 = (bf16[8,8,1024]{2,1,0:T(8,128)(2,1)S(1)}, bf16[8,8,1024]{2,1,0:T(8,128)(2,1)S(1)}, u32[]{:S(2)}, u32[]{:S(2)}) collective-permute-start(bf16[8,8,1024]{2,1,0:T(8,128)(2,1)S(1)} %interleave.1.refs_0_), channel_id=1, source_target_pairs={{0,3},{1,2},{2,1},{3,0},{4,7},{5,6},{6,5},{7,4},{8,11},{9,10},{10,... | collective-permute-start | bytes 393224 | tf_op jit(solution)/shard_map/ppermute | solution.py:312
  44.9 11.9 %collective-permute-start.7 = (bf16[4,32,1024]{2,1,0:T(8,128)(2,1)}, bf16[4,32,1024]{2,1,0:T(8,128)(2,1)S(1)}, u32[]{:S(2)}, u32[]{:S(2)}) collective-permute-start(bf16[4,32,1024]{2,1,0:T(8,128)(2,1)} %get-tuple-element.75), channel_id=1, source_target_pairs={{0,4},{1,5},{2,6},{3,7},{4,0},{5,1},{6,2},{7,3},{8,12},{9,13},{10,... | collective-permute-start | bytes 786440 | tf_op jit(solution)/shard_map/ppermute | solution.py:316
  46.6 10.6 %collective-permute-start.8 = (bf16[4,32,1024]{2,1,0:T(8,128)(2,1)}, bf16[4,32,1024]{2,1,0:T(8,128)(2,1)S(1)}, u32[]{:S(2)}, u32[]{:S(2)}) collective-permute-start(bf16[4,32,1024]{2,1,0:T(8,128)(2,1)} %get-tuple-element.76), channel_id=1, source_target_pairs={{0,12},{1,13},{2,14},{3,15},{4,8},{5,9},{6,10},{7,11},{8,4},{9,5},... | collective-permute-start | bytes 786440 | tf_op jit(solution)/shard_map/ppermute | solution.py:316
  48.7 8.5 %collective-permute-start.9 = (bf16[4,32,1024]{2,1,0:T(8,128)(2,1)S(1)}, bf16[4,32,1024]{2,1,0:T(8,128)(2,1)S(1)}, u32[]{:S(2)}, u32[]{:S(2)}) collective-permute-start(bf16[4,32,1024]{2,1,0:T(8,128)(2,1)S(1)} %copy-done.10), channel_id=1, source_target_pairs={{0,8},{1,9},{2,10},{3,11},{4,12},{5,13},{6,14},{7,15},{8,0},{9,1},... | collective-permute-start | bytes 786440 | tf_op jit(solution)/shard_map/ppermute | solution.py:316
  49.3 6.0 %collective-permute-start.5 = (bf16[8,8,1024]{2,1,0:T(8,128)(2,1)S(1)}, bf16[8,8,1024]{2,1,0:T(8,128)(2,1)S(1)}, u32[]{:S(2)}, u32[]{:S(2)}) collective-permute-start(bf16[8,8,1024]{2,1,0:T(8,128)(2,1)S(1)} %interleave.1.refs_0_), channel_id=1, source_target_pairs={{0,2},{1,3},{2,0},{3,1},{4,6},{5,7},{6,4},{7,5},{8,10},{9,11},{10,... | collective-permute-start | bytes 393224 | tf_op jit(solution)/shard_map/ppermute | solution.py:312
  51.8 5.0 %collective-permute-start.4 = (bf16[8,8,1024]{2,1,0:T(8,128)(2,1)S(1)}, bf16[8,8,1024]{2,1,0:T(8,128)(2,1)S(1)}, u32[]{:S(2)}, u32[]{:S(2)}) collective-permute-start(bf16[8,8,1024]{2,1,0:T(8,128)(2,1)S(1)} %interleave.1.refs_0_), channel_id=1, source_target_pairs={{0,1},{1,0},{2,3},{3,2},{4,5},{5,4},{6,7},{7,6},{8,9},{9,8},{10,11... | collective-permute-start | bytes 393224 | tf_op jit(solution)/shard_map/ppermute | solution.py:312
  57.2 29.4 %collective-permute-start.13 = (bf16[512,1024]{1,0:T(8,128)(2,1)S(1)}, bf16[512,1024]{1,0:T(8,128)(2,1)S(1)}, u32[]{:S(2)}, u32[]{:S(2)}) collective-permute-start(bf16[512,1024]{1,0:T(8,128)(2,1)S(1)} %bitcast.55), channel_id=1, source_target_pairs={{0,16},{16,0},{32,48},{48,32},{64,80},{80,64},{96,112},{112,96},{1... | collective-permute-start | bytes 3145736 | tf_op jit(solution)/shard_map/ppermute | solution.py:320
  57.3 13.1 %collective-permute-start.14 = (bf16[4,32,1024]{2,1,0:T(8,128)(2,1)S(1)}, bf16[4,32,1024]{2,1,0:T(8,128)(2,1)S(1)}, u32[]{:S(2)}, u32[]{:S(2)}) collective-permute-start(bf16[4,32,1024]{2,1,0:T(8,128)(2,1)S(1)} %get-tuple-element.86), channel_id=1, source_target_pairs={{0,1},{1,0},{2,3},{3,2},{4,5},{5,4},{6,7},{7,6},{8,9},{9,8},{10,11... | collective-permute-start | bytes 786440 | tf_op jit(solution)/shard_map/ppermute | solution.py:312
  59.2 13.3 %collective-permute-start.15 = (bf16[4,32,1024]{2,1,0:T(8,128)(2,1)S(1)}, bf16[4,32,1024]{2,1,0:T(8,128)(2,1)S(1)}, u32[]{:S(2)}, u32[]{:S(2)}) collective-permute-start(bf16[4,32,1024]{2,1,0:T(8,128)(2,1)S(1)} %get-tuple-element.87), channel_id=1, source_target_pairs={{0,2},{1,3},{2,0},{3,1},{4,6},{5,7},{6,4},{7,5},{8,10},{9,11},{10,... | collective-permute-start | bytes 786440 | tf_op jit(solution)/shard_map/ppermute | solution.py:312
  60.1 25.9 %collective-permute-start.12 = (bf16[8,32,1024]{2,1,0:T(8,128)(2,1)S(1)}, bf16[8,32,1024]{2,1,0:T(8,128)(2,1)S(1)}, u32[]{:S(2)}, u32[]{:S(2)}) collective-permute-start(bf16[8,32,1024]{2,1,0:T(8,128)(2,1)S(1)} %column.1.refs_0_), channel_id=1, source_target_pairs={{0,8},{1,9},{2,10},{3,11},{4,12},{5,13},{6,14},{7,15},{8,0},{9,1},... | collective-permute-start | bytes 1572872 | tf_op jit(solution)/shard_map/ppermute | solution.py:316
  62.8 23.8 %collective-permute-start.11 = (bf16[8,32,1024]{2,1,0:T(8,128)(2,1)S(1)}, bf16[8,32,1024]{2,1,0:T(8,128)(2,1)S(1)}, u32[]{:S(2)}, u32[]{:S(2)}) collective-permute-start(bf16[8,32,1024]{2,1,0:T(8,128)(2,1)S(1)} %column.1.refs_0_), channel_id=1, source_target_pairs={{0,12},{1,13},{2,14},{3,15},{4,8},{5,9},{6,10},{7,11},{8,4},{9,5},... | collective-permute-start | bytes 1572872 | tf_op jit(solution)/shard_map/ppermute | solution.py:316
  70.4 16.2 %collective-permute-start.10 = (bf16[8,32,1024]{2,1,0:T(8,128)(2,1)S(1)}, bf16[8,32,1024]{2,1,0:T(8,128)(2,1)S(1)}, u32[]{:S(2)}, u32[]{:S(2)}) collective-permute-start(bf16[8,32,1024]{2,1,0:T(8,128)(2,1)S(1)} %column.1.refs_0_), channel_id=1, source_target_pairs={{0,4},{1,5},{2,6},{3,7},{4,0},{5,1},{6,2},{7,3},{8,12},{9,13},{10,... | collective-permute-start | bytes 1572872 | tf_op jit(solution)/shard_map/ppermute | solution.py:316
  72.4 14.1 %copy-start.7 = (s32[5]{0:T(128)S(1)}, s32[5]{0:T(128)}, u32[]{:S(2)}) copy-start(s32[5]{0:T(128)} %stack.53.at_ref) | copy-start | bytes 64
  72.4 13.5 %collective-permute-start.16 = (bf16[4,32,1024]{2,1,0:T(8,128)(2,1)S(1)}, bf16[4,32,1024]{2,1,0:T(8,128)(2,1)S(1)}, u32[]{:S(2)}, u32[]{:S(2)}) collective-permute-start(bf16[4,32,1024]{2,1,0:T(8,128)(2,1)S(1)} %get-tuple-element.88), channel_id=1, source_target_pairs={{0,3},{1,2},{2,1},{3,0},{4,7},{5,6},{6,5},{7,4},{8,11},{9,10},{10,... | collective-permute-start | bytes 786440 | tf_op jit(solution)/shard_map/ppermute | solution.py:312
  90.5 2.8 %collective-permute-start.17 = (bf16[512,1024]{1,0:T(8,128)(2,1)S(1)}, bf16[512,1024]{1,0:T(8,128)(2,1)S(1)}, u32[]{:S(2)}, u32[]{:S(2)}) collective-permute-start(bf16[512,1024]{1,0:T(8,128)(2,1)S(1)} %get-tuple-element.92.refs_4_), channel_id=1, source_target_pairs={{0,16},{16,0},{32,48},{48,32},{64,80},{80,64},{96,112},{112,96},{1... | collective-permute-start | bytes 3145736 | tf_op jit(solution)/shard_map/ppermute | solution.py:320
  90.5 14.3 %collective-permute-start.18 = (bf16[2,2,128,512]{3,2,1,0:T(8,128)(2,1)S(1)}, bf16[2,2,128,512]{3,2,1,0:T(8,128)(2,1)S(1)}, u32[]{:S(2)}, u32[]{:S(2)}) collective-permute-start(bf16[2,2,128,512]{3,2,1,0:T(8,128)(2,1)S(1)} %get-tuple-element.96), channel_id=1, source_target_pairs={{0,64},{16,80},{32,96},{48,112},{64,0},{80,16},{96,32},{112,48},{1... | collective-permute-start | bytes 1572872 | tf_op jit(solution)/shard_map/ppermute | solution.py:325
  91.3 15.3 %collective-permute-start.20 = (bf16[2,2,128,512]{3,2,1,0:T(8,128)(2,1)S(1)}, bf16[2,2,128,512]{3,2,1,0:T(8,128)(2,1)S(1)}, u32[]{:S(2)}, u32[]{:S(2)}) collective-permute-start(bf16[2,2,128,512]{3,2,1,0:T(8,128)(2,1)S(1)} %get-tuple-element.98), channel_id=1, source_target_pairs={{0,192},{16,208},{32,224},{48,240},{64,128},{80,144},{96,160},{112... | collective-permute-start | bytes 1572872 | tf_op jit(solution)/shard_map/ppermute | solution.py:326
  105.0 10.5 %collective-permute-start.19 = (bf16[2,128,512]{2,1,0:T(8,128)(2,1)S(1)}, bf16[2,128,512]{2,1,0:T(8,128)(2,1)S(1)}, u32[]{:S(2)}, u32[]{:S(2)}) collective-permute-start(bf16[2,128,512]{2,1,0:T(8,128)(2,1)S(1)} %fusion.10), channel_id=1, source_target_pairs={{0,192},{16,208},{32,224},{48,240},{64,128},{80,144},{96,160},{112... | collective-permute-start | bytes 786440 | tf_op jit(solution)/shard_map/ppermute | solution.py:331
  106.7 9.3 %collective-permute-start.21 = (bf16[2,128,512]{2,1,0:T(8,128)(2,1)S(1)}, bf16[2,128,512]{2,1,0:T(8,128)(2,1)S(1)}, u32[]{:S(2)}, u32[]{:S(2)}) collective-permute-start(bf16[2,128,512]{2,1,0:T(8,128)(2,1)S(1)} %fusion.11), channel_id=1, source_target_pairs={{0,64},{16,80},{32,96},{48,112},{64,0},{80,16},{96,32},{112,48},{1... | collective-permute-start | bytes 786440 | tf_op jit(solution)/shard_map/ppermute | solution.py:332
  107.6 18.1 %collective-permute-start.23 = (bf16[2,2,128,512]{3,2,1,0:T(8,128)(2,1)S(1)}, bf16[2,2,128,512]{3,2,1,0:T(8,128)(2,1)S(1)}, u32[]{:S(2)}, u32[]{:S(2)}) collective-permute-start(bf16[2,2,128,512]{3,2,1,0:T(8,128)(2,1)S(1)} %get-tuple-element.100), channel_id=1, source_target_pairs={{0,64},{16,80},{32,96},{48,112},{64,0},{80,16},{96,32},{112,48},{1... | collective-permute-start | bytes 1572872 | tf_op jit(solution)/shard_map/ppermute | solution.py:325
  108.9 19.1 %collective-permute-start.25 = (bf16[2,2,128,512]{3,2,1,0:T(8,128)(2,1)S(1)}, bf16[2,2,128,512]{3,2,1,0:T(8,128)(2,1)S(1)}, u32[]{:S(2)}, u32[]{:S(2)}) collective-permute-start(bf16[2,2,128,512]{3,2,1,0:T(8,128)(2,1)S(1)} %get-tuple-element.102), channel_id=1, source_target_pairs={{0,192},{16,208},{32,224},{48,240},{64,128},{80,144},{96,160},{112... | collective-permute-start | bytes 1572872 | tf_op jit(solution)/shard_map/ppermute | solution.py:326
  116.2 14.4 %collective-permute-start.22 = (bf16[128,1024]{1,0:T(8,128)(2,1)S(1)}, bf16[128,1024]{1,0:T(8,128)(2,1)S(1)}, u32[]{:S(2)}, u32[]{:S(2)}) collective-permute-start(bf16[128,1024]{1,0:T(8,128)(2,1)S(1)} %fusion.12), channel_id=1, source_target_pairs={{0,32},{16,48},{32,0},{48,16},{64,96},{80,112},{96,64},{112,80},{1... | collective-permute-start | bytes 786440 | tf_op jit(solution)/shard_map/ppermute | solution.py:337
  125.9 8.0 %collective-permute-start.24 = (bf16[2,128,512]{2,1,0:T(8,128)(2,1)S(1)}, bf16[2,128,512]{2,1,0:T(8,128)(2,1)S(1)}, u32[]{:S(2)}, u32[]{:S(2)}) collective-permute-start(bf16[2,128,512]{2,1,0:T(8,128)(2,1)S(1)} %fusion.13), channel_id=1, source_target_pairs={{0,192},{16,208},{32,224},{48,240},{64,128},{80,144},{96,160},{112... | collective-permute-start | bytes 786440 | tf_op jit(solution)/shard_map/ppermute | solution.py:331
  128.2 6.5 %collective-permute-start.26 = (bf16[2,128,512]{2,1,0:T(8,128)(2,1)S(1)}, bf16[2,128,512]{2,1,0:T(8,128)(2,1)S(1)}, u32[]{:S(2)}, u32[]{:S(2)}) collective-permute-start(bf16[2,128,512]{2,1,0:T(8,128)(2,1)S(1)} %fusion.14), channel_id=1, source_target_pairs={{0,64},{16,80},{32,96},{48,112},{64,0},{80,16},{96,32},{112,48},{1... | collective-permute-start | bytes 786440 | tf_op jit(solution)/shard_map/ppermute | solution.py:332
  134.9 14.5 %collective-permute-start.27 = (bf16[128,1024]{1,0:T(8,128)(2,1)S(1)}, bf16[128,1024]{1,0:T(8,128)(2,1)S(1)}, u32[]{:S(2)}, u32[]{:S(2)}) collective-permute-start(bf16[128,1024]{1,0:T(8,128)(2,1)S(1)} %fusion.15), channel_id=1, source_target_pairs={{0,32},{16,48},{32,0},{48,16},{64,96},{80,112},{96,64},{112,80},{1... | collective-permute-start | bytes 786440 | tf_op jit(solution)/shard_map/ppermute | solution.py:337

commit v3 on v2

--- a/solution.py
+++ b/solution.py
@@ -132,13 +132,19 @@
     return whole(regroup_kernel, out, "regroup", (), *parts)
 
 
-def assemble_into(out_ref, at_ref, *refs):
+def assemble_kernel(at_ref, *refs):
+    out_ref = refs[4]
     rows = refs[0].shape[1]
     for z_flip in range(4):
         for y_flip in range(4):
             source = at_ref[y_flip] * 4 + (at_ref[4] ^ z_flip)
             place = pl.ds(pl.multiple_of(source * rows, rows), rows)
             out_ref[place] = refs[z_flip][y_flip]
+
+
+def assemble(at, parts):
+    out = jax.ShapeDtypeStruct((16 * parts[0].shape[1], parts[0].shape[2]), parts[0].dtype)
+    return whole(assemble_kernel, out, "assemble", (at,), *parts)
 
 
 def swap_axes_kernel(*refs):
@@ -270,15 +276,21 @@
 
 
 def product_kernel(*refs):
-    row_refs = refs[:4]
-    own_ref, other_ref, send_a, keep_a, send_b, keep_b, new_ref = refs[4:]
+    near_refs, far_refs = refs[:3], refs[3:5]
+    own_ref, *piece_refs = refs[5:-6]
+    send_a, keep_a, send_b, keep_b, new_ref, other_ref = refs[-6:]
+    at = 0
+    for ref in piece_refs:
+        other_ref[at : at + ref.shape[0]] = ref[...]
+        at += ref.shape[0]
     new_ref[...] = own_ref[...]
     half = own_ref.shape[1] // 2
     depth = own_ref.shape[0]
     for flip in (3, 1, 2, 0):
-        rows = jnp.concatenate(
-            [ref[2 * flip + flip_z] for flip_z in range(2) for ref in row_refs], axis=0
-        )
+        parts = []
+        for at in (2 * flip, 2 * flip + 1):
+            parts += [ref[at] for ref in near_refs] + [far_refs[at // 4][at % 4]]
+        rows = jnp.concatenate(parts, axis=0)
         total = jnp.dot(rows[:, :depth], own_ref[...], preferred_element_type=jnp.float32)
         total += jnp.dot(rows[:, depth:], other_ref[...], preferred_element_type=jnp.float32)
         term = (total * D ** (-0.5)).astype(jnp.bfloat16).reshape(2, 128, 2 * half)
@@ -286,22 +298,21 @@
         (send_b if flip & 2 else keep_b)[flip & 1] = term[:, :, half:]
 
 
-def product_kernel_and_next(at_ref, *refs):
-    *refs, next_ref = refs
-    assemble_into(next_ref, at_ref, *refs[6:10])
-    product_kernel(*refs[:6], *refs[10:])
-
-
-def products(row_parts, own, other, at=None, next_parts=()):
+def products(row_parts, own, pieces, after=()):
     half = own.shape[1] // 2
     out = jax.ShapeDtypeStruct((2, 2, 128, half), jnp.bfloat16)
-    whole_own = jax.ShapeDtypeStruct(own.shape, own.dtype)
-    arrays = (*row_parts, own, other, *next_parts)
-    if next_parts:
-        return whole(
-            product_kernel_and_next, [out] * 4 + [whole_own] * 2, "products", (at,), *arrays
-        )
-    return whole(product_kernel, [out] * 4 + [whole_own], "products", (), *arrays)
+    vmem = pl.BlockSpec(memory_space=pltpu.VMEM)
+    arrays = (*row_parts, own, *pieces)
+    return pl.pallas_call(
+        lambda *refs: product_kernel(*refs[: len(arrays)], *refs[-6:]),
+        in_specs=[vmem] * len(arrays) + [pl.BlockSpec(memory_space=pl.ANY)] * len(after),
+        out_specs=[vmem] * 5,
+        out_shape=[out] * 4 + [jax.ShapeDtypeStruct(own.shape, own.dtype)],
+        scratch_shapes=[pltpu.VMEM(own.shape, own.dtype)],
+        compiler_params=pltpu.CompilerParams(vmem_limit_bytes=20 * 2**20),
+        cost_estimate=BRIEF,
+        name="products",
+    )(*arrays, *after)
 
 
 def add(kept, arrived):
@@ -316,21 +327,33 @@
     return [parts[0]] + [lax.ppermute(parts[k], "mp", mp_swap(k, 0)) for k in (1, 2, 3)]
 
 
-def swap_core(own):
-    return lax.ppermute(own, "dp", dp_swap(0, 0, 1))
+def over_y_ring(column):
+    near = [lax.ppermute(column, "mp", mp_swap(k, 0)) for k in (1, 2)]
+    far = [
+        lax.ppermute(near[0][:4], "mp", mp_swap(2, 0)),
+        lax.ppermute(near[1][4:], "mp", mp_swap(1, 0)),
+    ]
+    return [column, *near, *far]
+
+
+def swap_core(own, cuts):
+    return [
+        lax.ppermute(piece, "dp", dp_swap(0, 0, 1)) for piece in jnp.split(own, cuts)
+    ]
 
 
 def first_sums(parts):
     send_a, keep_a, send_b, keep_b = parts
     got_a = lax.ppermute(send_a, "dp", dp_swap(1, 0, 0))
     got_b = lax.ppermute(send_b, "dp", dp_swap(2, 0, 0))
-    return add(keep_a, got_a), add(keep_b, got_b)
-
-
-def second_sums(sum_a, sum_b):
-    got_a = lax.ppermute(sum_a[1].astype(jnp.bfloat16), "dp", dp_swap(2, 0, 0))
-    got_b = lax.ppermute(sum_b[1].astype(jnp.bfloat16), "dp", dp_swap(1, 0, 0))
-    return jnp.concatenate([add(sum_a[0], got_a), add(sum_b[0], got_b)], axis=-1)
+    sends = [add(k[1], g[1]).astype(jnp.bfloat16) for k, g in ((keep_a, got_a), (keep_b, got_b))]
+    return sends, [add(keep_a[0], got_a[0]), add(keep_b[0], got_b[0])]
+
+
+def second_sums(sends, keeps):
+    got_a = lax.ppermute(sends[0], "dp", dp_swap(2, 0, 0))
+    got_b = lax.ppermute(sends[1], "dp", dp_swap(1, 0, 0))
+    return jnp.concatenate([add(keeps[0], got_a), add(keeps[1], got_b)], axis=-1)
 
 
 def last_sum(both):
@@ -390,16 +413,20 @@
     column, up_parts, gate_own = lax.optimization_barrier(
         (join_rows(along_z), up_parts, gate_own)
     )
-    gate_other = swap_core(gate_own)
-    row_parts = over_y([column] * 4)
+    gate_other = swap_core(gate_own, (176, 352))
+    row_parts = over_y_ring(column)
     up_parts = over_z(regroup(up_parts))
-    *gate_terms, gate_new, up_own = products(row_parts, gate_own, gate_other, at, up_parts)
-    *up_terms, up_new = products(row_parts, up_own, swap_core(up_own))
+    *gate_terms, gate_new = products(row_parts, gate_own, gate_other, up_parts[1:3])
+    gate_new, up_parts = lax.optimization_barrier((gate_new, up_parts))
+    up_own = assemble(at, up_parts)
+    *up_terms, up_new = products(row_parts, up_own, swap_core(up_own, (256,)))
 
     gate_terms[1], gate_terms[3], up_new = lax.optimization_barrier(
         (gate_terms[1], gate_terms[3], up_new)
     )
-    gate_both = second_sums(*first_sums(gate_terms))
+    gate_sends, gate_keeps = first_sums(gate_terms)
+    gate_sends, up_terms = lax.optimization_barrier((gate_sends, up_terms))
+    gate_both = second_sums(gate_sends, gate_keeps)
     up_both = second_sums(*first_sums(up_terms))
     gate_total, up_both = lax.optimization_barrier((last_sum(gate_both), up_both))
     up_total = last_sum(up_both)

time: 151 us -> 148 us (0.980)
  waiting for transfers between devices: 72.8 us -> 68 us
    ppermute x6, waiting for transfers between devices: 27.9 us -> 10.7 us  [over_z(): lax.ppermute(parts[k], 'mp', mp_swap(0, k))]
    ppermute x6 -> x13, waiting for transfers between devices: 9.07 us -> 20.7 us  [the longest x2 7.79 us: second_sums(): got_a = lax.ppermute(sends[0], 'dp', dp_swap(2, 0, 0))]
    pallas_call x6 -> x5, Pallas kernels: 7.37 us -> 0.74 us  [whole(): pl.pallas_call(kernel, in_specs=[pl.BlockSpec(memory_space=pltpu.SMEM)] *...]
    pallas_call x0 -> x2, Pallas kernels: none -> 6.63 us  [products(): pl.pallas_call(lambda *refs: product_kernel(*refs[:len(arrays)], *refs[-6...]
    ppermute x6 -> x13, starting transfers between devices: 4.18 us -> 8.8 us  [the longest x2 3.99 us: over_y_ring(): near = [lax.ppermute(column, 'mp', mp_swap(k, 0)) for k in (1, 2)]]
    ppermute x6 -> x3, starting transfers between devices: 8.81 us -> 4.45 us  [over_y(): lax.ppermute(parts[k], 'mp', mp_swap(k, 0))]
  transfers between devices with their start and end apart: 29 -> 33, of which waited for: 20 -> 21; matrix products, arithmetic and copies ran while one was open for 1% -> 1% of each run, Pallas kernels for 8% -> 11%
where the time goes in v3:
time: 148 us; the launch traced here: 147 us
  waiting for transfers between devices  68 us (46%)
  starting transfers between devices  53.3 us (36%)
  Pallas kernels  21.1 us (14%)
  local copies, waits for them, and re-layouts  2.15 us (1%)
    ppermute x2, waiting for transfers between devices, last_sum(): lax.ppermute(both[1].astype(jnp.bfloat16), 'dp', dp_swap(0, 1, 0))  12.8 us
    ppermute x2, waiting for transfers between devices, first_sums(): got_a = lax.ppermute(send_a, 'dp', dp_swap(1, 0, 0))  12.6 us
    ppermute x6, waiting for transfers between devices, over_z(): lax.ppermute(parts[k], 'mp', mp_swap(0, k))  10.7 us
    ppermute x2, starting transfers between devices, last_sum(): lax.ppermute(both[1].astype(jnp.bfloat16), 'dp', dp_swap(0, 1, 0))  9.13 us
    all_to_all x1, starting transfers between devices, local(): lax.all_to_all(gate_step, 'mp', split_axis=0, concat_axis=0, tiled=True)  8.8 us
    ppermute x2, waiting for transfers between devices, second_sums(): got_a = lax.ppermute(sends[0], 'dp', dp_swap(2, 0, 0))  7.79 us
    ppermute x6, starting transfers between devices, over_z(): lax.ppermute(parts[k], 'mp', mp_swap(0, k))  7.26 us
    pallas_call x2, Pallas kernels, products(): pl.pallas_call(lambda *refs: product_kernel(*refs[:len(arrays)], *refs[-6...  6.63 us
  transfers between devices with their start and end apart: 33, of which 21 were waited for; matrix products, arithmetic and copies ran while one was open for 1% of the time, Pallas kernels for 11%

profile of v3, /device:TPU:32, one launch (start us, length us, event | category | flops | bytes accessed | tf_op | source)
XLA Modules:
  0.0 147.4 jit_solution(9936910856806820788)
XLA Ops:
  0.6 4.6 %adam_places.1 = bf16[16,32,1024]{2,1,0:T(8,128)(2,1)} custom-call(bf16[32,16384]{1,0:T(8,128)(2,1)} %refs_0_.1, bf16[32,16384]{1,0:T(8,128)(2,1)} %refs_1_.2, bf16[32,16384]{1,0:T(8,128)(2,1)} %refs_2_.2, bf16[32,16384]{1,0:T(8,128)(2,1)} %refs_3_.2), custom_call_target="tpu_custom_call" | custom-call | flops 1 | bytes 1 | tf_op jit(solution)/shard_map/adam_places/pallas_call | solution.py:70
  5.2 8.8 %all-to-all-start = ((bf16[16,32,1024]{2,1,0:T(8,128)(2,1)}), bf16[16,32,1024]{2,1,0:T(8,128)(2,1)S(1)}, u32[]{:S(2)}, u32[]{:S(2)}) async-start(bf16[16,32,1024]{2,1,0:T(8,128)(2,1)} %adam_places.1), calls=%async_computation | async-start | bytes 2097152 | tf_op jit(solution)/shard_map/all_to_all | solution.py:398
  14.2 0.1 stack.57.to_ref
  14.3 0.6 copy-done.3
  14.9 3.7 %attend.1 = (bf16[2,8,1024]{2,1,0:T(8,128)(2,1)S(1)}, bf16[2,8,1024]{2,1,0:T(8,128)(2,1)S(1)}, bf16[2,8,1024]{2,1,0:T(8,128)(2,1)S(1)}, bf16[2,8,1024]{2,1,0:T(8,128)(2,1)S(1)}) custom-call(s32[9]{0:T(128)S(1)} %stack.57.to_ref, s32[2]{0:T(128)S(1)} %copy-done.8, bf16[4,2,8192]{2,1,0:T(2,128)(2,1)S(1)} %copy-done.3, bf16[4,2,8192]{2,1,0:T(2,128)(2,1)S(1)} %copy-done.4, ...), custom_call_target="tpu_custom_call" | custom-call | flops 1 | bytes 1 | tf_op jit(solution)/shard_map/attend/pallas_call | solution.py:263
  18.6 0.6 stack.63.at_ref
  19.2 5.5 %adam_flips.1 = (bf16[4,32,1024]{2,1,0:T(8,128)(2,1)}, bf16[4,32,1024]{2,1,0:T(8,128)(2,1)}, bf16[4,32,1024]{2,1,0:T(8,128)(2,1)}, bf16[4,32,1024]{2,1,0:T(8,128)(2,1)}) custom-call(s32[5]{0:T(128)} %stack.63.at_ref, bf16[32,16384]{1,0:T(8,128)(2,1)} %refs_0_.2, bf16[32,16384]{1,0:T(8,128)(2,1)} %refs_1_.3, bf16[32,16384]{1,0:T(8,128)(2,1)} %refs_2_.3, ...), custom_call_target="tpu_custom_call" | custom-call | flops 1 | bytes 1 | tf_op jit(solution)/shard_map/adam_flips/pallas_call | solution.py:97
  24.7 1.5 %collective-permute-start = (bf16[2,8,1024]{2,1,0:T(8,128)(2,1)S(1)}, bf16[2,8,1024]{2,1,0:T(8,128)(2,1)S(1)}, u32[]{:S(2)}, u32[]{:S(2)}) collective-permute-start(bf16[2,8,1024]{2,1,0:T(8,128)(2,1)S(1)} %get-tuple-element.79), channel_id=1, source_target_pairs={{0,64},{16,80},{32,96},{48,112},{64,0},{80,16},{96,32},{112,48},{1... | collective-permute-start | bytes 98312 | tf_op jit(solution)/shard_map/ppermute | solution.py:409
  26.2 2.1 %collective-permute-start.1 = (bf16[2,8,1024]{2,1,0:T(8,128)(2,1)S(1)}, bf16[2,8,1024]{2,1,0:T(8,128)(2,1)S(1)}, u32[]{:S(2)}, u32[]{:S(2)}) collective-permute-start(bf16[2,8,1024]{2,1,0:T(8,128)(2,1)S(1)} %get-tuple-element.80), channel_id=1, source_target_pairs={{0,192},{16,208},{32,224},{48,240},{64,128},{80,144},{96,160},{112... | collective-permute-start | bytes 98312 | tf_op jit(solution)/shard_map/ppermute | solution.py:409
  28.3 0.6 collective-permute-start.2
  28.9 2.7 %collective-permute-done.1.refs_2_ = bf16[2,8,1024]{2,1,0:T(8,128)(2,1)S(1)} collective-permute-done((bf16[2,8,1024]{2,1,0:T(8,128)(2,1)S(1)}, bf16[2,8,1024]{2,1,0:T(8,128)(2,1)S(1)}, u32[]{:S(2)}, u32[]{:S(2)}) %collective-permute-start.1) | collective-permute-done | bytes 32800 | tf_op jit(solution)/shard_map/ppermute | solution.py:409
  31.7 2.0 %collective-permute-done.2.refs_3_ = bf16[2,8,1024]{2,1,0:T(8,128)(2,1)S(1)} collective-permute-done((bf16[2,8,1024]{2,1,0:T(8,128)(2,1)S(1)}, bf16[2,8,1024]{2,1,0:T(8,128)(2,1)S(1)}, u32[]{:S(2)}, u32[]{:S(2)}) %collective-permute-start.2) | collective-permute-done | bytes 32800 | tf_op jit(solution)/shard_map/ppermute | solution.py:409
  33.7 4.6 %collective-permute-start.3 = (bf16[4,8,1024]{2,1,0:T(8,128)(2,1)S(1)}, bf16[4,8,1024]{2,1,0:T(8,128)(2,1)S(1)}, u32[]{:S(2)}, u32[]{:S(2)}) collective-permute-start(bf16[4,8,1024]{2,1,0:T(8,128)(2,1)S(1)} %get-tuple-element.83), channel_id=1, source_target_pairs={{0,32},{16,48},{32,0},{48,16},{64,96},{80,112},{96,64},{112,80},{1... | collective-permute-start | bytes 196616 | tf_op jit(solution)/shard_map/ppermute | solution.py:411
  38.3 4.1 %collective-permute-done.3.second_ref = bf16[4,8,1024]{2,1,0:T(8,128)(2,1)S(1)} collective-permute-done((bf16[4,8,1024]{2,1,0:T(8,128)(2,1)S(1)}, bf16[4,8,1024]{2,1,0:T(8,128)(2,1)S(1)}, u32[]{:S(2)}, u32[]{:S(2)}) %collective-permute-start.3) | collective-permute-done | bytes 65568 | tf_op jit(solution)/shard_map/ppermute | solution.py:411
  42.4 2.4 %collective-permute-start.6 = (bf16[8,8,1024]{2,1,0:T(8,128)(2,1)S(1)}, bf16[8,8,1024]{2,1,0:T(8,128)(2,1)S(1)}, u32[]{:S(2)}, u32[]{:S(2)}) collective-permute-start(bf16[8,8,1024]{2,1,0:T(8,128)(2,1)S(1)} %interleave.1.refs_0_), channel_id=1, source_target_pairs={{0,3},{1,2},{2,1},{3,0},{4,7},{5,6},{6,5},{7,4},{8,11},{9,10},{10,... | collective-permute-start | bytes 393224 | tf_op jit(solution)/shard_map/ppermute | solution.py:323
  44.9 1.7 %collective-permute-start.7 = (bf16[4,32,1024]{2,1,0:T(8,128)(2,1)}, bf16[4,32,1024]{2,1,0:T(8,128)(2,1)S(1)}, u32[]{:S(2)}, u32[]{:S(2)}) collective-permute-start(bf16[4,32,1024]{2,1,0:T(8,128)(2,1)} %get-tuple-element.85), channel_id=1, source_target_pairs={{0,4},{1,5},{2,6},{3,7},{4,0},{5,1},{6,2},{7,3},{8,12},{9,13},{10,... | collective-permute-start | bytes 786440 | tf_op jit(solution)/shard_map/ppermute | solution.py:327
  46.6 2.2 %collective-permute-start.8 = (bf16[4,32,1024]{2,1,0:T(8,128)(2,1)}, bf16[4,32,1024]{2,1,0:T(8,128)(2,1)S(1)}, u32[]{:S(2)}, u32[]{:S(2)}) collective-permute-start(bf16[4,32,1024]{2,1,0:T(8,128)(2,1)} %get-tuple-element.86), channel_id=1, source_target_pairs={{0,12},{1,13},{2,14},{3,15},{4,8},{5,9},{6,10},{7,11},{8,4},{9,5},... | collective-permute-start | bytes 786440 | tf_op jit(solution)/shard_map/ppermute | solution.py:327
  48.8 0.5 collective-permute-start.9
  49.4 2.4 %collective-permute-done.6.refs_3_ = bf16[8,8,1024]{2,1,0:T(8,128)(2,1)S(1)} collective-permute-done((bf16[8,8,1024]{2,1,0:T(8,128)(2,1)S(1)}, bf16[8,8,1024]{2,1,0:T(8,128)(2,1)S(1)}, u32[]{:S(2)}, u32[]{:S(2)}) %collective-permute-start.6) | collective-permute-done | bytes 131104 | tf_op jit(solution)/shard_map/ppermute | solution.py:323
  51.8 3.5 %collective-permute-done.5.refs_2_ = bf16[8,8,1024]{2,1,0:T(8,128)(2,1)S(1)} collective-permute-done((bf16[8,8,1024]{2,1,0:T(8,128)(2,1)S(1)}, bf16[8,8,1024]{2,1,0:T(8,128)(2,1)S(1)}, u32[]{:S(2)}, u32[]{:S(2)}) %collective-permute-start.5) | collective-permute-done | bytes 131104 | tf_op jit(solution)/shard_map/ppermute | solution.py:323
  55.3 1.5 collective-permute-done.4.refs_1_
  56.8 0.7 collective-permute-done.8.refs_2_
  57.5 3.8 %collective-permute-start.11 = (bf16[8,32,1024]{2,1,0:T(8,128)(2,1)S(1)}, bf16[8,32,1024]{2,1,0:T(8,128)(2,1)S(1)}, u32[]{:S(2)}, u32[]{:S(2)}) collective-permute-start(bf16[8,32,1024]{2,1,0:T(8,128)(2,1)S(1)} %column.1.refs_0_), channel_id=1, source_target_pairs={{0,12},{1,13},{2,14},{3,15},{4,8},{5,9},{6,10},{7,11},{8,4},{9,5},... | collective-permute-start | bytes 1572872 | tf_op jit(solution)/shard_map/ppermute | solution.py:331
  61.3 0.2 collective-permute-start.10
  61.6 0.1 collective-permute-start.17
  61.7 3.3 %collective-permute-start.18 = (bf16[4,32,1024]{2,1,0:T(8,128)(2,1)S(1)}, bf16[4,32,1024]{2,1,0:T(8,128)(2,1)S(1)}, u32[]{:S(2)}, u32[]{:S(2)}) collective-permute-start(bf16[4,32,1024]{2,1,0:T(8,128)(2,1)S(1)} %get-tuple-element.96), channel_id=1, source_target_pairs={{0,2},{1,3},{2,0},{3,1},{4,6},{5,7},{6,4},{7,5},{8,10},{9,11},{10,... | collective-permute-start | bytes 786440 | tf_op jit(solution)/shard_map/ppermute | solution.py:323
  65.0 0.1 collective-permute-start.16
  65.2 3.3 %collective-permute-done.11.refs_2_ = bf16[8,32,1024]{2,1,0:T(8,128)(2,1)S(1)} collective-permute-done((bf16[8,32,1024]{2,1,0:T(8,128)(2,1)S(1)}, bf16[8,32,1024]{2,1,0:T(8,128)(2,1)S(1)}, u32[]{:S(2)}, u32[]{:S(2)}) %collective-permute-start.11) | collective-permute-done | bytes 524320 | tf_op jit(solution)/shard_map/ppermute | solution.py:331
  68.4 2.0 %collective-permute-done.10.refs_1_ = bf16[8,32,1024]{2,1,0:T(8,128)(2,1)S(1)} collective-permute-done((bf16[8,32,1024]{2,1,0:T(8,128)(2,1)S(1)}, bf16[8,32,1024]{2,1,0:T(8,128)(2,1)S(1)}, u32[]{:S(2)}, u32[]{:S(2)}) %collective-permute-start.10) | collective-permute-done | bytes 524320 | tf_op jit(solution)/shard_map/ppermute | solution.py:331
  70.5 0.3 collective-permute-start.13
  70.9 1.3 collective-permute-done.18.refs_10_.refs_2_
  72.2 0.3 collective-permute-start.12
  72.4 1.4 collective-permute-start.19
  73.8 5.5 %collective-permute-done.13.refs_4_ = bf16[4,32,1024]{2,1,0:T(8,128)(2,1)S(1)} collective-permute-done((bf16[4,32,1024]{2,1,0:T(8,128)(2,1)S(1)}, bf16[4,32,1024]{2,1,0:T(8,128)(2,1)S(1)}, u32[]{:S(2)}, u32[]{:S(2)}) %collective-permute-start.13) | collective-permute-done | bytes 262176 | tf_op jit(solution)/shard_map/ppermute | solution.py:334
  79.3 1.3 collective-permute-done.12.refs_3_
  80.7 3.3 %products.2 = (bf16[2,2,128,512]{3,2,1,0:T(8,128)(2,1)S(1)}, bf16[2,2,128,512]{3,2,1,0:T(8,128)(2,1)S(1)}, bf16[2,2,128,512]{3,2,1,0:T(8,128)(2,1)S(1)}, bf16[2,...) custom-call(bf16[8,32,1024]{2,1,0:T(8,128)(2,1)S(1)} %column.1.refs_0_, ...), custom_call_target="tpu_custom_call" | custom-call | flops 1 | bytes 1 | tf_op jit(solution)/shard_map/products/pallas_call | solution.py:306
  84.0 2.0 %collective-permute-done.19.refs_3_ = bf16[4,32,1024]{2,1,0:T(8,128)(2,1)S(1)} collective-permute-done((bf16[4,32,1024]{2,1,0:T(8,128)(2,1)S(1)}, bf16[4,32,1024]{2,1,0:T(8,128)(2,1)S(1)}, u32[]{:S(2)}, u32[]{:S(2)}) %collective-permute-start.19) | collective-permute-done | bytes 262176 | tf_op jit(solution)/shard_map/ppermute | solution.py:323
  86.0 0.6 copy-done.7
  86.6 0.6 assemble.1.refs_5_
  87.3 0.1 collective-permute-start.21
  87.4 0.5 collective-permute-start.20
  87.9 0.8 collective-permute-start.22
  88.6 1.4 collective-permute-start.23
  90.0 3.3 %products.3 = (bf16[2,2,128,512]{3,2,1,0:T(8,128)(2,1)S(1)}, bf16[2,2,128,512]{3,2,1,0:T(8,128)(2,1)S(1)}, bf16[2,2,128,512]{3,2,1,0:T(8,128)(2,1)S(1)}, bf16[2,...) custom-call(bf16[8,32,1024]{2,1,0:T(8,128)(2,1)S(1)} %column.1.refs_0_, ...), custom_call_target="tpu_custom_call" | custom-call | flops 1 | bytes 1 | tf_op jit(solution)/shard_map/products/pallas_call | solution.py:306
  93.3 8.5 %collective-permute-done.22 = bf16[2,2,128,512]{3,2,1,0:T(8,128)(2,1)S(1)} collective-permute-done((bf16[2,2,128,512]{3,2,1,0:T(8,128)(2,1)S(1)}, bf16[2,2,128,512]{3,2,1,0:T(8,128)(2,1)S(1)}, u32[]{:S(2)}, u32[]{:S(2)}) %collective-permute-start.22) | collective-permute-done | bytes 524320 | tf_op jit(solution)/shard_map/ppermute | solution.py:347
  101.9 1.6 %collective-permute-done.23 = bf16[2,2,128,512]{3,2,1,0:T(8,128)(2,1)S(1)} collective-permute-done((bf16[2,2,128,512]{3,2,1,0:T(8,128)(2,1)S(1)}, bf16[2,2,128,512]{3,2,1,0:T(8,128)(2,1)S(1)}, u32[]{:S(2)}, u32[]{:S(2)}) %collective-permute-start.23) | collective-permute-done | bytes 524320 | tf_op jit(solution)/shard_map/ppermute | solution.py:348
  103.6 1.4 collective-permute-start.24
  105.0 2.0 %collective-permute-start.27 = (bf16[2,2,128,512]{3,2,1,0:T(8,128)(2,1)S(1)}, bf16[2,2,128,512]{3,2,1,0:T(8,128)(2,1)S(1)}, u32[]{:S(2)}, u32[]{:S(2)}) collective-permute-start(bf16[2,2,128,512]{3,2,1,0:T(8,128)(2,1)S(1)} %get-tuple-element.120), channel_id=1, source_target_pairs={{0,64},{16,80},{32,96},{48,112},{64,0},{80,16},{96,32},{112,48},{1... | collective-permute-start | bytes 1572872 | tf_op jit(solution)/shard_map/ppermute | solution.py:347
  107.0 1.9 %collective-permute-start.29 = (bf16[2,2,128,512]{3,2,1,0:T(8,128)(2,1)S(1)}, bf16[2,2,128,512]{3,2,1,0:T(8,128)(2,1)S(1)}, u32[]{:S(2)}, u32[]{:S(2)}) collective-permute-start(bf16[2,2,128,512]{3,2,1,0:T(8,128)(2,1)S(1)} %get-tuple-element.122), channel_id=1, source_target_pairs={{0,192},{16,208},{32,224},{48,240},{64,128},{80,144},{96,160},{112... | collective-permute-start | bytes 1572872 | tf_op jit(solution)/shard_map/ppermute | solution.py:348
  108.9 5.2 %collective-permute-done.24 = bf16[2,128,512]{2,1,0:T(8,128)(2,1)S(1)} collective-permute-done((bf16[2,128,512]{2,1,0:T(8,128)(2,1)S(1)}, bf16[2,128,512]{2,1,0:T(8,128)(2,1)S(1)}, u32[]{:S(2)}, u32[]{:S(2)}) %collective-permute-start.24) | collective-permute-done | bytes 262176 | tf_op jit(solution)/shard_map/ppermute | solution.py:354
  114.1 0.1 bitcast_add_fusion.4
  114.2 0.1 bitcast_add_fusion.3
  114.4 4.5 %collective-permute-start.26 = (bf16[128,1024]{1,0:T(8,128)(2,1)S(1)}, bf16[128,1024]{1,0:T(8,128)(2,1)S(1)}, u32[]{:S(2)}, u32[]{:S(2)}) collective-permute-start(bf16[128,1024]{1,0:T(8,128)(2,1)S(1)} %fusion.10), channel_id=1, source_target_pairs={{0,32},{16,48},{32,0},{48,16},{64,96},{80,112},{96,64},{112,80},{1... | collective-permute-start | bytes 786440 | tf_op jit(solution)/shard_map/ppermute | solution.py:360
  118.9 4.2 %collective-permute-done.27 = bf16[2,2,128,512]{3,2,1,0:T(8,128)(2,1)S(1)} collective-permute-done((bf16[2,2,128,512]{3,2,1,0:T(8,128)(2,1)S(1)}, bf16[2,2,128,512]{3,2,1,0:T(8,128)(2,1)S(1)}, u32[]{:S(2)}, u32[]{:S(2)}) %collective-permute-start.27) | collective-permute-done | bytes 524320 | tf_op jit(solution)/shard_map/ppermute | solution.py:347
  123.2 2.0 %collective-permute-start.28 = (bf16[2,128,512]{2,1,0:T(8,128)(2,1)S(1)}, bf16[2,128,512]{2,1,0:T(8,128)(2,1)S(1)}, u32[]{:S(2)}, u32[]{:S(2)}) collective-permute-start(bf16[2,128,512]{2,1,0:T(8,128)(2,1)S(1)} %fusion.8), channel_id=1, source_target_pairs={{0,192},{16,208},{32,224},{48,240},{64,128},{80,144},{96,160},{112... | collective-permute-start | bytes 786440 | tf_op jit(solution)/shard_map/ppermute | solution.py:354
  125.2 0.1 collective-permute-start.30
  125.3 2.9 %collective-permute-done.26 = bf16[128,1024]{1,0:T(8,128)(2,1)S(1)} collective-permute-done((bf16[128,1024]{1,0:T(8,128)(2,1)S(1)}, bf16[128,1024]{1,0:T(8,128)(2,1)S(1)}, u32[]{:S(2)}, u32[]{:S(2)}) %collective-permute-start.26) | collective-permute-done | bytes 262176 | tf_op jit(solution)/shard_map/ppermute | solution.py:360
  128.3 2.6 %collective-permute-done.28 = bf16[2,128,512]{2,1,0:T(8,128)(2,1)S(1)} collective-permute-done((bf16[2,128,512]{2,1,0:T(8,128)(2,1)S(1)}, bf16[2,128,512]{2,1,0:T(8,128)(2,1)S(1)}, u32[]{:S(2)}, u32[]{:S(2)}) %collective-permute-start.28) | collective-permute-done | bytes 262176 | tf_op jit(solution)/shard_map/ppermute | solution.py:354
  130.9 0.1 bitcast_add_fusion.2
  131.0 0.7 collective-permute-done.30
  131.7 0.1 bitcast_add_fusion.1
  131.9 4.6 %collective-permute-start.31 = (bf16[128,1024]{1,0:T(8,128)(2,1)S(1)}, bf16[128,1024]{1,0:T(8,128)(2,1)S(1)}, u32[]{:S(2)}, u32[]{:S(2)}) collective-permute-start(bf16[128,1024]{1,0:T(8,128)(2,1)S(1)} %fusion.11), channel_id=1, source_target_pairs={{0,32},{16,48},{32,0},{48,16},{64,96},{80,112},{96,64},{112,80},{1... | collective-permute-start | bytes 786440 | tf_op jit(solution)/shard_map/ppermute | solution.py:360
  136.5 9.9 %collective-permute-done.31 = bf16[128,1024]{1,0:T(8,128)(2,1)S(1)} collective-permute-done((bf16[128,1024]{1,0:T(8,128)(2,1)S(1)}, bf16[128,1024]{1,0:T(8,128)(2,1)S(1)}, u32[]{:S(2)}, u32[]{:S(2)}) %collective-permute-start.31) | collective-permute-done | bytes 262176 | tf_op jit(solution)/shard_map/ppermute | solution.py:360
  146.4 1.0 convolution_convert_fusion
  (56 shorter events, 1.0 us)
Async XLA Ops:
  5.2 8.9 %copy-start.9 = (bf16[8192]{0:T(1024)(128)(2,1)S(1)}, bf16[8192]{0:T(1024)(128)(2,1)}, u32[]{:S(2)}) copy-start(bf16[8192]{0:T(1024)(128)(2,1)} %param.31) | copy-start | bytes 49156
  5.2 9.1 %copy-start = (bf16[2,128,1024]{2,1,0:T(8,128)(2,1)S(1)}, bf16[2,128,1024]{2,1,0:T(8,128)(2,1)}, u32[]{:S(2)}) copy-start(bf16[2,128,1024]{2,1,0:T(8,128)(2,1)} %old_k_ref.1) | copy-start | bytes 1572868
  5.2 9.1 %copy-start.1 = (bf16[2,128,1024]{2,1,0:T(8,128)(2,1)S(1)}, bf16[2,128,1024]{2,1,0:T(8,128)(2,1)}, u32[]{:S(2)}) copy-start(bf16[2,128,1024]{2,1,0:T(8,128)(2,1)} %old_v_ref.1) | copy-start | bytes 1572868
  5.2 9.1 %copy-start.4 = (bf16[4,2,8192]{2,1,0:T(2,128)(2,1)S(1)}, bf16[4,2,8192]{2,1,0:T(2,128)(2,1)}, u32[]{:S(2)}) copy-start(bf16[4,2,8192]{2,1,0:T(2,128)(2,1)} %input_ref.1) | copy-start | bytes 393220
  5.2 52.3 %all-to-all-start = ((bf16[16,32,1024]{2,1,0:T(8,128)(2,1)}), bf16[16,32,1024]{2,1,0:T(8,128)(2,1)S(1)}, u32[]{:S(2)}, u32[]{:S(2)}) async-start(bf16[16,32,1024]{2,1,0:T(8,128)(2,1)} %adam_places.1), calls=%async_computation | async-start | bytes 2097152 | tf_op jit(solution)/shard_map/all_to_all | solution.py:398
  14.0 0.9 copy-start.3
  14.1 0.8 copy-start.6
  14.1 0.8 copy-start.5
  14.1 0.8 copy-start.8
  24.7 24.1 %copy-start.10 = (bf16[4,32,1024]{2,1,0:T(8,128)(2,1)S(1)}, bf16[4,32,1024]{2,1,0:T(8,128)(2,1)}, u32[]{:S(2)}) copy-start(bf16[4,32,1024]{2,1,0:T(8,128)(2,1)} %get-tuple-element.87) | copy-start | bytes 786436
  24.7 4.2 %collective-permute-start = (bf16[2,8,1024]{2,1,0:T(8,128)(2,1)S(1)}, bf16[2,8,1024]{2,1,0:T(8,128)(2,1)S(1)}, u32[]{:S(2)}, u32[]{:S(2)}) collective-permute-start(bf16[2,8,1024]{2,1,0:T(8,128)(2,1)S(1)} %get-tuple-element.79), channel_id=1, source_target_pairs={{0,64},{16,80},{32,96},{48,112},{64,0},{80,16},{96,32},{112,48},{1... | collective-permute-start | bytes 98312 | tf_op jit(solution)/shard_map/ppermute | solution.py:409
  26.2 5.5 %collective-permute-start.1 = (bf16[2,8,1024]{2,1,0:T(8,128)(2,1)S(1)}, bf16[2,8,1024]{2,1,0:T(8,128)(2,1)S(1)}, u32[]{:S(2)}, u32[]{:S(2)}) collective-permute-start(bf16[2,8,1024]{2,1,0:T(8,128)(2,1)S(1)} %get-tuple-element.80), channel_id=1, source_target_pairs={{0,192},{16,208},{32,224},{48,240},{64,128},{80,144},{96,160},{112... | collective-permute-start | bytes 98312 | tf_op jit(solution)/shard_map/ppermute | solution.py:409
  28.3 5.4 %collective-permute-start.2 = (bf16[2,8,1024]{2,1,0:T(8,128)(2,1)S(1)}, bf16[2,8,1024]{2,1,0:T(8,128)(2,1)S(1)}, u32[]{:S(2)}, u32[]{:S(2)}) collective-permute-start(bf16[2,8,1024]{2,1,0:T(8,128)(2,1)S(1)} %get-tuple-element.81), channel_id=1, source_target_pairs={{0,128},{16,144},{32,160},{48,176},{64,192},{80,208},{96,224},{112... | collective-permute-start | bytes 98312 | tf_op jit(solution)/shard_map/ppermute | solution.py:409
  33.7 8.7 %collective-permute-start.3 = (bf16[4,8,1024]{2,1,0:T(8,128)(2,1)S(1)}, bf16[4,8,1024]{2,1,0:T(8,128)(2,1)S(1)}, u32[]{:S(2)}, u32[]{:S(2)}) collective-permute-start(bf16[4,8,1024]{2,1,0:T(8,128)(2,1)S(1)} %get-tuple-element.83), channel_id=1, source_target_pairs={{0,32},{16,48},{32,0},{48,16},{64,96},{80,112},{96,64},{112,80},{1... | collective-permute-start | bytes 196616 | tf_op jit(solution)/shard_map/ppermute | solution.py:411
  42.4 19.1 %copy-start.2 = (bf16[4,32,1024]{2,1,0:T(8,128)(2,1)S(1)}, bf16[4,32,1024]{2,1,0:T(8,128)(2,1)}, u32[]{:S(2)}) copy-start(bf16[4,32,1024]{2,1,0:T(8,128)(2,1)} %get-tuple-element.91.refs_0_) | copy-start | bytes 786436
  42.4 9.3 %collective-permute-start.6 = (bf16[8,8,1024]{2,1,0:T(8,128)(2,1)S(1)}, bf16[8,8,1024]{2,1,0:T(8,128)(2,1)S(1)}, u32[]{:S(2)}, u32[]{:S(2)}) collective-permute-start(bf16[8,8,1024]{2,1,0:T(8,128)(2,1)S(1)} %interleave.1.refs_0_), channel_id=1, source_target_pairs={{0,3},{1,2},{2,1},{3,0},{4,7},{5,6},{6,5},{7,4},{8,11},{9,10},{10,... | collective-permute-start | bytes 393224 | tf_op jit(solution)/shard_map/ppermute | solution.py:323
  44.9 11.9 %collective-permute-start.7 = (bf16[4,32,1024]{2,1,0:T(8,128)(2,1)}, bf16[4,32,1024]{2,1,0:T(8,128)(2,1)S(1)}, u32[]{:S(2)}, u32[]{:S(2)}) collective-permute-start(bf16[4,32,1024]{2,1,0:T(8,128)(2,1)} %get-tuple-element.85), channel_id=1, source_target_pairs={{0,4},{1,5},{2,6},{3,7},{4,0},{5,1},{6,2},{7,3},{8,12},{9,13},{10,... | collective-permute-start | bytes 786440 | tf_op jit(solution)/shard_map/ppermute | solution.py:327
  46.6 10.9 %collective-permute-start.8 = (bf16[4,32,1024]{2,1,0:T(8,128)(2,1)}, bf16[4,32,1024]{2,1,0:T(8,128)(2,1)S(1)}, u32[]{:S(2)}, u32[]{:S(2)}) collective-permute-start(bf16[4,32,1024]{2,1,0:T(8,128)(2,1)} %get-tuple-element.86), channel_id=1, source_target_pairs={{0,12},{1,13},{2,14},{3,15},{4,8},{5,9},{6,10},{7,11},{8,4},{9,5},... | collective-permute-start | bytes 786440 | tf_op jit(solution)/shard_map/ppermute | solution.py:327
  48.8 8.7 %collective-permute-start.9 = (bf16[4,32,1024]{2,1,0:T(8,128)(2,1)S(1)}, bf16[4,32,1024]{2,1,0:T(8,128)(2,1)S(1)}, u32[]{:S(2)}, u32[]{:S(2)}) collective-permute-start(bf16[4,32,1024]{2,1,0:T(8,128)(2,1)S(1)} %copy-done.10), channel_id=1, source_target_pairs={{0,8},{1,9},{2,10},{3,11},{4,12},{5,13},{6,14},{7,15},{8,0},{9,1},... | collective-permute-start | bytes 786440 | tf_op jit(solution)/shard_map/ppermute | solution.py:327
  49.3 6.0 %collective-permute-start.5 = (bf16[8,8,1024]{2,1,0:T(8,128)(2,1)S(1)}, bf16[8,8,1024]{2,1,0:T(8,128)(2,1)S(1)}, u32[]{:S(2)}, u32[]{:S(2)}) collective-permute-start(bf16[8,8,1024]{2,1,0:T(8,128)(2,1)S(1)} %interleave.1.refs_0_), channel_id=1, source_target_pairs={{0,2},{1,3},{2,0},{3,1},{4,6},{5,7},{6,4},{7,5},{8,10},{9,11},{10,... | collective-permute-start | bytes 393224 | tf_op jit(solution)/shard_map/ppermute | solution.py:323
  51.8 5.0 %collective-permute-start.4 = (bf16[8,8,1024]{2,1,0:T(8,128)(2,1)S(1)}, bf16[8,8,1024]{2,1,0:T(8,128)(2,1)S(1)}, u32[]{:S(2)}, u32[]{:S(2)}) collective-permute-start(bf16[8,8,1024]{2,1,0:T(8,128)(2,1)S(1)} %interleave.1.refs_0_), channel_id=1, source_target_pairs={{0,1},{1,0},{2,3},{3,2},{4,5},{5,4},{6,7},{7,6},{8,9},{9,8},{10,11... | collective-permute-start | bytes 393224 | tf_op jit(solution)/shard_map/ppermute | solution.py:323
  57.5 10.9 %collective-permute-start.11 = (bf16[8,32,1024]{2,1,0:T(8,128)(2,1)S(1)}, bf16[8,32,1024]{2,1,0:T(8,128)(2,1)S(1)}, u32[]{:S(2)}, u32[]{:S(2)}) collective-permute-start(bf16[8,32,1024]{2,1,0:T(8,128)(2,1)S(1)} %column.1.refs_0_), channel_id=1, source_target_pairs={{0,12},{1,13},{2,14},{3,15},{4,8},{5,9},{6,10},{7,11},{8,4},{9,5},... | collective-permute-start | bytes 1572872 | tf_op jit(solution)/shard_map/ppermute | solution.py:331
  61.3 9.2 %collective-permute-start.10 = (bf16[8,32,1024]{2,1,0:T(8,128)(2,1)S(1)}, bf16[8,32,1024]{2,1,0:T(8,128)(2,1)S(1)}, u32[]{:S(2)}, u32[]{:S(2)}) collective-permute-start(bf16[8,32,1024]{2,1,0:T(8,128)(2,1)S(1)} %column.1.refs_0_), channel_id=1, source_target_pairs={{0,4},{1,5},{2,6},{3,7},{4,0},{5,1},{6,2},{7,3},{8,12},{9,13},{10,... | collective-permute-start | bytes 1572872 | tf_op jit(solution)/shard_map/ppermute | solution.py:331
  61.6 8.9 %collective-permute-start.17 = (bf16[4,32,1024]{2,1,0:T(8,128)(2,1)S(1)}, bf16[4,32,1024]{2,1,0:T(8,128)(2,1)S(1)}, u32[]{:S(2)}, u32[]{:S(2)}) collective-permute-start(bf16[4,32,1024]{2,1,0:T(8,128)(2,1)S(1)} %get-tuple-element.95), channel_id=1, source_target_pairs={{0,1},{1,0},{2,3},{3,2},{4,5},{5,4},{6,7},{7,6},{8,9},{9,8},{10,11... | collective-permute-start | bytes 786440 | tf_op jit(solution)/shard_map/ppermute | solution.py:323
  61.7 10.5 %collective-permute-start.18 = (bf16[4,32,1024]{2,1,0:T(8,128)(2,1)S(1)}, bf16[4,32,1024]{2,1,0:T(8,128)(2,1)S(1)}, u32[]{:S(2)}, u32[]{:S(2)}) collective-permute-start(bf16[4,32,1024]{2,1,0:T(8,128)(2,1)S(1)} %get-tuple-element.96), channel_id=1, source_target_pairs={{0,2},{1,3},{2,0},{3,1},{4,6},{5,7},{6,4},{7,5},{8,10},{9,11},{10,... | collective-permute-start | bytes 786440 | tf_op jit(solution)/shard_map/ppermute | solution.py:323
  65.0 7.4 %collective-permute-start.16 = (bf16[160,1024]{1,0:T(8,128)(2,1)S(1)}, bf16[160,1024]{1,0:T(8,128)(2,1)S(1)}, u32[]{:S(2)}, u32[]{:S(2)}) collective-permute-start(bf16[160,1024]{1,0:T(8,128)(2,1)S(1)} %split.17), channel_id=1, source_target_pairs={{0,16},{16,0},{32,48},{48,32},{64,80},{80,64},{96,112},{112,96},{1... | collective-permute-start | bytes 983048 | tf_op jit(solution)/shard_map/ppermute | solution.py:341
  68.4 5.4 %collective-permute-start.15 = (bf16[176,1024]{1,0:T(8,128)(2,1)S(1)}, bf16[176,1024]{1,0:T(8,128)(2,1)S(1)}, u32[]{:S(2)}, u32[]{:S(2)}) collective-permute-start(bf16[176,1024]{1,0:T(8,128)(2,1)S(1)} %get-tuple-element.127), channel_id=1, source_target_pairs={{0,16},{16,0},{32,48},{48,32},{64,80},{80,64},{96,112},{112,96},{1... | collective-permute-start | bytes 1081352 | tf_op jit(solution)/shard_map/ppermute | solution.py:341
  70.5 3.4 %collective-permute-start.14 = (bf16[176,1024]{1,0:T(8,128)(2,1)S(1)}, bf16[176,1024]{1,0:T(8,128)(2,1)S(1)}, u32[]{:S(2)}, u32[]{:S(2)}) collective-permute-start(bf16[176,1024]{1,0:T(8,128)(2,1)S(1)} %get-tuple-element.128), channel_id=1, source_target_pairs={{0,16},{16,0},{32,48},{48,32},{64,80},{80,64},{96,112},{112,96},{1... | collective-permute-start | bytes 1081352 | tf_op jit(solution)/shard_map/ppermute | solution.py:341
  70.5 8.8 %collective-permute-start.13 = (bf16[4,32,1024]{2,1,0:T(8,128)(2,1)S(1)}, bf16[4,32,1024]{2,1,0:T(8,128)(2,1)S(1)}, u32[]{:S(2)}, u32[]{:S(2)}) collective-permute-start(bf16[4,32,1024]{2,1,0:T(8,128)(2,1)S(1)} %slice.91), channel_id=1, source_target_pairs={{0,4},{1,5},{2,6},{3,7},{4,0},{5,1},{6,2},{7,3},{8,12},{9,13},{10,... | collective-permute-start | bytes 786440 | tf_op jit(solution)/shard_map/ppermute | solution.py:334
  72.2 8.5 %collective-permute-start.12 = (bf16[4,32,1024]{2,1,0:T(8,128)(2,1)S(1)}, bf16[4,32,1024]{2,1,0:T(8,128)(2,1)S(1)}, u32[]{:S(2)}, u32[]{:S(2)}) collective-permute-start(bf16[4,32,1024]{2,1,0:T(8,128)(2,1)S(1)} %slice.90), channel_id=1, source_target_pairs={{0,12},{1,13},{2,14},{3,15},{4,8},{5,9},{6,10},{7,11},{8,4},{9,5},... | collective-permute-start | bytes 786440 | tf_op jit(solution)/shard_map/ppermute | solution.py:333
  72.4 13.6 %collective-permute-start.19 = (bf16[4,32,1024]{2,1,0:T(8,128)(2,1)S(1)}, bf16[4,32,1024]{2,1,0:T(8,128)(2,1)S(1)}, u32[]{:S(2)}, u32[]{:S(2)}) collective-permute-start(bf16[4,32,1024]{2,1,0:T(8,128)(2,1)S(1)} %get-tuple-element.99), channel_id=1, source_target_pairs={{0,3},{1,2},{2,1},{3,0},{4,7},{5,6},{6,5},{7,4},{8,11},{9,10},{10,... | collective-permute-start | bytes 786440 | tf_op jit(solution)/shard_map/ppermute | solution.py:323
  86.0 0.6 copy-start.7
  87.3 2.7 %collective-permute-start.21 = (bf16[256,1024]{1,0:T(8,128)(2,1)S(1)}, bf16[256,1024]{1,0:T(8,128)(2,1)S(1)}, u32[]{:S(2)}, u32[]{:S(2)}) collective-permute-start(bf16[256,1024]{1,0:T(8,128)(2,1)S(1)} %get-tuple-element.125), channel_id=1, source_target_pairs={{0,16},{16,0},{32,48},{48,32},{64,80},{80,64},{96,112},{112,96},{1... | collective-permute-start | bytes 1572872 | tf_op jit(solution)/shard_map/ppermute | solution.py:341
  87.4 2.6 %collective-permute-start.20 = (bf16[256,1024]{1,0:T(8,128)(2,1)S(1)}, bf16[256,1024]{1,0:T(8,128)(2,1)S(1)}, u32[]{:S(2)}, u32[]{:S(2)}) collective-permute-start(bf16[256,1024]{1,0:T(8,128)(2,1)S(1)} %get-tuple-element.126), channel_id=1, source_target_pairs={{0,16},{16,0},{32,48},{48,32},{64,80},{80,64},{96,112},{112,96},{1... | collective-permute-start | bytes 1572872 | tf_op jit(solution)/shard_map/ppermute | solution.py:341
  87.9 13.9 %collective-permute-start.22 = (bf16[2,2,128,512]{3,2,1,0:T(8,128)(2,1)S(1)}, bf16[2,2,128,512]{3,2,1,0:T(8,128)(2,1)S(1)}, u32[]{:S(2)}, u32[]{:S(2)}) collective-permute-start(bf16[2,2,128,512]{3,2,1,0:T(8,128)(2,1)S(1)} %get-tuple-element.110), channel_id=1, source_target_pairs={{0,64},{16,80},{32,96},{48,112},{64,0},{80,16},{96,32},{112,48},{1... | collective-permute-start | bytes 1572872 | tf_op jit(solution)/shard_map/ppermute | solution.py:347
  88.6 14.9 %collective-permute-start.23 = (bf16[2,2,128,512]{3,2,1,0:T(8,128)(2,1)S(1)}, bf16[2,2,128,512]{3,2,1,0:T(8,128)(2,1)S(1)}, u32[]{:S(2)}, u32[]{:S(2)}) collective-permute-start(bf16[2,2,128,512]{3,2,1,0:T(8,128)(2,1)S(1)} %get-tuple-element.112), channel_id=1, source_target_pairs={{0,192},{16,208},{32,224},{48,240},{64,128},{80,144},{96,160},{112... | collective-permute-start | bytes 1572872 | tf_op jit(solution)/shard_map/ppermute | solution.py:348
  103.6 10.5 %collective-permute-start.24 = (bf16[2,128,512]{2,1,0:T(8,128)(2,1)S(1)}, bf16[2,128,512]{2,1,0:T(8,128)(2,1)S(1)}, u32[]{:S(2)}, u32[]{:S(2)}) collective-permute-start(bf16[2,128,512]{2,1,0:T(8,128)(2,1)S(1)} %fusion.6), channel_id=1, source_target_pairs={{0,192},{16,208},{32,224},{48,240},{64,128},{80,144},{96,160},{112... | collective-permute-start | bytes 786440 | tf_op jit(solution)/shard_map/ppermute | solution.py:354
  105.0 9.2 %collective-permute-start.25 = (bf16[2,128,512]{2,1,0:T(8,128)(2,1)S(1)}, bf16[2,128,512]{2,1,0:T(8,128)(2,1)S(1)}, u32[]{:S(2)}, u32[]{:S(2)}) collective-permute-start(bf16[2,128,512]{2,1,0:T(8,128)(2,1)S(1)} %fusion.7), channel_id=1, source_target_pairs={{0,64},{16,80},{32,96},{48,112},{64,0},{80,16},{96,32},{112,48},{1... | collective-permute-start | bytes 786440 | tf_op jit(solution)/shard_map/ppermute | solution.py:355
  105.0 18.1 %collective-permute-start.27 = (bf16[2,2,128,512]{3,2,1,0:T(8,128)(2,1)S(1)}, bf16[2,2,128,512]{3,2,1,0:T(8,128)(2,1)S(1)}, u32[]{:S(2)}, u32[]{:S(2)}) collective-permute-start(bf16[2,2,128,512]{3,2,1,0:T(8,128)(2,1)S(1)} %get-tuple-element.120), channel_id=1, source_target_pairs={{0,64},{16,80},{32,96},{48,112},{64,0},{80,16},{96,32},{112,48},{1... | collective-permute-start | bytes 1572872 | tf_op jit(solution)/shard_map/ppermute | solution.py:347
  107.0 18.1 %collective-permute-start.29 = (bf16[2,2,128,512]{3,2,1,0:T(8,128)(2,1)S(1)}, bf16[2,2,128,512]{3,2,1,0:T(8,128)(2,1)S(1)}, u32[]{:S(2)}, u32[]{:S(2)}) collective-permute-start(bf16[2,2,128,512]{3,2,1,0:T(8,128)(2,1)S(1)} %get-tuple-element.122), channel_id=1, source_target_pairs={{0,192},{16,208},{32,224},{48,240},{64,128},{80,144},{96,160},{112... | collective-permute-start | bytes 1572872 | tf_op jit(solution)/shard_map/ppermute | solution.py:348
  114.4 13.8 %collective-permute-start.26 = (bf16[128,1024]{1,0:T(8,128)(2,1)S(1)}, bf16[128,1024]{1,0:T(8,128)(2,1)S(1)}, u32[]{:S(2)}, u32[]{:S(2)}) collective-permute-start(bf16[128,1024]{1,0:T(8,128)(2,1)S(1)} %fusion.10), channel_id=1, source_target_pairs={{0,32},{16,48},{32,0},{48,16},{64,96},{80,112},{96,64},{112,80},{1... | collective-permute-start | bytes 786440 | tf_op jit(solution)/shard_map/ppermute | solution.py:360
  123.2 7.7 %collective-permute-start.28 = (bf16[2,128,512]{2,1,0:T(8,128)(2,1)S(1)}, bf16[2,128,512]{2,1,0:T(8,128)(2,1)S(1)}, u32[]{:S(2)}, u32[]{:S(2)}) collective-permute-start(bf16[2,128,512]{2,1,0:T(8,128)(2,1)S(1)} %fusion.8), channel_id=1, source_target_pairs={{0,192},{16,208},{32,224},{48,240},{64,128},{80,144},{96,160},{112... | collective-permute-start | bytes 786440 | tf_op jit(solution)/shard_map/ppermute | solution.py:354
  125.2 6.5 %collective-permute-start.30 = (bf16[2,128,512]{2,1,0:T(8,128)(2,1)S(1)}, bf16[2,128,512]{2,1,0:T(8,128)(2,1)S(1)}, u32[]{:S(2)}, u32[]{:S(2)}) collective-permute-start(bf16[2,128,512]{2,1,0:T(8,128)(2,1)S(1)} %fusion.9), channel_id=1, source_target_pairs={{0,64},{16,80},{32,96},{48,112},{64,0},{80,16},{96,32},{112,48},{1... | collective-permute-start | bytes 786440 | tf_op jit(solution)/shard_map/ppermute | solution.py:355
  131.9 14.5 %collective-permute-start.31 = (bf16[128,1024]{1,0:T(8,128)(2,1)S(1)}, bf16[128,1024]{1,0:T(8,128)(2,1)S(1)}, u32[]{:S(2)}, u32[]{:S(2)}) collective-permute-start(bf16[128,1024]{1,0:T(8,128)(2,1)S(1)} %fusion.11), channel_id=1, source_target_pairs={{0,32},{16,48},{32,0},{48,16},{64,96},{80,112},{96,64},{112,80},{1... | collective-permute-start | bytes 786440 | tf_op jit(solution)/shard_map/ppermute | solution.py:360

commit v4 on v3

--- a/solution.py
+++ b/solution.py
@@ -13,6 +13,7 @@
 STEPS = 4
 ROWS_HERE = 2
 
+PIECE = 256
 BRIEF = pl.CostEstimate(flops=1, bytes_accessed=1, transcendentals=0)
 
 GRAY = (0, 1, 3, 2)
@@ -59,9 +60,11 @@
 
 def adam_places_kernel(*refs):
     *in_refs, out_ref = refs
-    width = out_ref.shape[2]
-    for part in range(out_ref.shape[0]):
-        out_ref[part] = adam_kernel(*in_refs, slice(part * width, (part + 1) * width))
+    parts, _, width = out_ref.shape
+    for part in range(parts):
+        for at in range(0, width, PIECE):
+            cols = pl.ds(part * width + at, PIECE)
+            out_ref[part, :, at : at + PIECE] = adam_kernel(*in_refs, cols)
 
 
 def adam_places(*arrays):
@@ -69,43 +72,48 @@
     width = cols // 16
     return pl.pallas_call(
         adam_places_kernel,
-        grid=(4,),
-        in_specs=[pl.BlockSpec((rows, 4 * width), lambda i: (0, i))] * 4,
-        out_specs=pl.BlockSpec((4, rows, width), lambda i: (i, 0, 0)),
+        grid=(2,),
+        in_specs=[pl.BlockSpec((rows, 8 * width), lambda i: (0, i))] * 4,
+        out_specs=pl.BlockSpec((8, rows, width), lambda i: (i, 0, 0)),
         out_shape=jax.ShapeDtypeStruct((16, rows, width), jnp.bfloat16),
         cost_estimate=BRIEF,
         name="adam_places",
     )(*arrays)
 
 
-def adam_flips_kernel(at_ref, *refs):
-    in_refs, out_refs = refs[:4], refs[4:]
+def adam_flips_kernel(to_ref, *refs):
+    in_refs, out_refs = refs[:8], refs[8:]
     width = out_refs[0].shape[2]
-    for flip in range(4):
-        cols = pl.ds(pl.multiple_of((at_ref[4] ^ flip) * width, width), width)
-        new = adam_kernel(*in_refs, cols)
-        for y_flip, out_ref in enumerate(out_refs):
-
-            @pl.when(pl.program_id(0) == y_flip)
-            def _():
-                out_ref[flip] = new
-
-
-def adam_flips(at, *arrays):
+    for half in range(2):
+        for flip in range(4):
+            cols = pl.ds(pl.multiple_of((to_ref[13] ^ flip) * width, width), width)
+            new = adam_kernel(*in_refs[half::2], cols)
+            for step in range(2):
+
+                @pl.when(pl.program_id(0) == step)
+                def _():
+                    out_refs[2 * step + half][flip] = new
+
+
+def adam_flips(to, *arrays):
     rows, cols = arrays[0].shape
     width = cols // 16
+    in_specs = [
+        pl.BlockSpec((rows, 4 * width), lambda i, to: (0, to[9 + 2 * i])),
+        pl.BlockSpec((rows, 4 * width), lambda i, to: (0, to[10 + 2 * i])),
+    ]
     return pl.pallas_call(
         adam_flips_kernel,
         grid_spec=pltpu.PrefetchScalarGridSpec(
             num_scalar_prefetch=1,
-            grid=(4,),
-            in_specs=[pl.BlockSpec((rows, 4 * width), lambda i, at: (0, at[i]))] * 4,
-            out_specs=[pl.BlockSpec((4, rows, width), lambda i, at: (0, 0, 0))] * 4,
+            grid=(2,),
+            in_specs=in_specs * 4,
+            out_specs=[pl.BlockSpec((4, rows, width), lambda i, to: (0, 0, 0))] * 4,
         ),
         out_shape=[jax.ShapeDtypeStruct((4, rows, width), jnp.bfloat16)] * 4,
         cost_estimate=BRIEF,
         name="adam_flips",
-    )(at, *arrays)
+    )(to, *[array for array in arrays for _ in range(2)])
 
 
 def whole(kernel, out_shape, name, scalars, *arrays):
@@ -132,19 +140,13 @@
     return whole(regroup_kernel, out, "regroup", (), *parts)
 
 
-def assemble_kernel(at_ref, *refs):
-    out_ref = refs[4]
+def assemble_into(out_ref, to_ref, *refs):
     rows = refs[0].shape[1]
     for z_flip in range(4):
         for y_flip in range(4):
-            source = at_ref[y_flip] * 4 + (at_ref[4] ^ z_flip)
+            source = to_ref[9 + y_flip] * 4 + (to_ref[13] ^ z_flip)
             place = pl.ds(pl.multiple_of(source * rows, rows), rows)
             out_ref[place] = refs[z_flip][y_flip]
-
-
-def assemble(at, parts):
-    out = jax.ShapeDtypeStruct((16 * parts[0].shape[1], parts[0].shape[2]), parts[0].dtype)
-    return whole(assemble_kernel, out, "assemble", (at,), *parts)
 
 
 def swap_axes_kernel(*refs):
@@ -275,15 +277,8 @@
     )(to, lengths, *arrays)
 
 
-def product_kernel(*refs):
-    near_refs, far_refs = refs[:3], refs[3:5]
-    own_ref, *piece_refs = refs[5:-6]
-    send_a, keep_a, send_b, keep_b, new_ref, other_ref = refs[-6:]
-    at = 0
-    for ref in piece_refs:
-        other_ref[at : at + ref.shape[0]] = ref[...]
-        at += ref.shape[0]
-    new_ref[...] = own_ref[...]
+def product_kernel(row_refs, own_ref, other_ref, send_a, keep_a, send_b, keep_b):
+    near_refs, far_refs = row_refs[:3], row_refs[3:]
     half = own_ref.shape[1] // 2
     depth = own_ref.shape[0]
     for flip in (3, 1, 2, 0):
@@ -298,16 +293,36 @@
         (send_b if flip & 2 else keep_b)[flip & 1] = term[:, :, half:]
 
 
-def products(row_parts, own, pieces, after=()):
-    half = own.shape[1] // 2
-    out = jax.ShapeDtypeStruct((2, 2, 128, half), jnp.bfloat16)
+def first_kernel(*refs):
+    row_refs, own_ref, piece_refs = refs[:5], refs[5], refs[6:10]
+    *term_refs, new_ref, other_ref = refs[-6:]
+    new_ref[...] = own_ref[...]
+    at = 0
+    for ref in piece_refs:
+        other_ref[at : at + ref.shape[0]] = ref[...]
+        at += ref.shape[0]
+    product_kernel(row_refs, own_ref, other_ref, *term_refs)
+
+
+def second_kernel(to_ref, *refs):
+    *term_refs, new_ref, other_ref = refs[-6:]
+    assemble_into(new_ref, to_ref, *refs[5:9])
+    assemble_into(other_ref, to_ref, *refs[9:13])
+    product_kernel(refs[:5], new_ref, other_ref, *term_refs)
+
+
+def products(kernel, scalars, row_parts, weights, after=()):
+    term = jax.ShapeDtypeStruct((2, 2, 128, 512), jnp.bfloat16)
+    own = jax.ShapeDtypeStruct((512, 1024), jnp.bfloat16)
     vmem = pl.BlockSpec(memory_space=pltpu.VMEM)
-    arrays = (*row_parts, own, *pieces)
+    arrays = (*scalars, *row_parts, *weights)
     return pl.pallas_call(
-        lambda *refs: product_kernel(*refs[: len(arrays)], *refs[-6:]),
-        in_specs=[vmem] * len(arrays) + [pl.BlockSpec(memory_space=pl.ANY)] * len(after),
+        lambda *refs: kernel(*refs[: len(arrays)], *refs[-6:]),
+        in_specs=[pl.BlockSpec(memory_space=pltpu.SMEM)] * len(scalars)
+        + [vmem] * (len(arrays) - len(scalars))
+        + [pl.BlockSpec(memory_space=pl.ANY)] * len(after),
         out_specs=[vmem] * 5,
-        out_shape=[out] * 4 + [jax.ShapeDtypeStruct(own.shape, own.dtype)],
+        out_shape=[term] * 4 + [own],
         scratch_shapes=[pltpu.VMEM(own.shape, own.dtype)],
         compiler_params=pltpu.CompilerParams(vmem_limit_bytes=20 * 2**20),
         cost_estimate=BRIEF,
@@ -387,14 +402,15 @@
     def place(gray):
         return gray ^ (gray >> 1)
 
-    at = jnp.stack([place(gray_y ^ flip) for flip in range(4)] + [z_lo]).astype(jnp.int32)
     to = jnp.stack(
         [place(gray_x ^ flip) * 2 + (z_hi ^ flip_z) for flip in range(4) for flip_z in range(2)]
         + [core]
+        + [place(gray_y ^ flip) for flip in range(4)]
+        + [z_lo]
     ).astype(jnp.int32)
 
     gate_step = adam_places(weight_gate, grad_gate, moment_gate, second_gate)
-    gate_step, queries = lax.optimization_barrier((gate_step, queries))
+    gate_step, lengths = lax.optimization_barrier((gate_step, lengths))
     gate_own = lax.all_to_all(gate_step, "mp", split_axis=0, concat_axis=0, tiled=True)
     gate_own = gate_own.reshape(512, 1024)
 
@@ -403,7 +419,7 @@
         norm_gain.reshape(1, D),
     )
     by_x, weight_up = lax.optimization_barrier((by_x, weight_up))
-    up_parts = adam_flips(at, weight_up, grad_up, moment_up, second_up)
+    up_parts = adam_flips(to, weight_up, grad_up, moment_up, second_up)
     by_x, up_parts = lax.optimization_barrier((by_x, up_parts))
     up_parts = over_y(up_parts)
     by_x = [by_x[0]] + [lax.ppermute(by_x[k], "dp", dp_swap(k, 0, 0)) for k in (1, 2, 3)]
@@ -413,13 +429,15 @@
     column, up_parts, gate_own = lax.optimization_barrier(
         (join_rows(along_z), up_parts, gate_own)
     )
-    gate_other = swap_core(gate_own, (176, 352))
+    gate_other = swap_core(gate_own, (128, 256, 384))
     row_parts = over_y_ring(column)
     up_parts = over_z(regroup(up_parts))
-    *gate_terms, gate_new = products(row_parts, gate_own, gate_other, up_parts[1:3])
-    gate_new, up_parts = lax.optimization_barrier((gate_new, up_parts))
-    up_own = assemble(at, up_parts)
-    *up_terms, up_new = products(row_parts, up_own, swap_core(up_own, (256,)))
+    *gate_terms, gate_new = products(
+        first_kernel, (), row_parts, (gate_own, *gate_other), up_parts[1:3]
+    )
+    gate_new, up_parts[3] = lax.optimization_barrier((gate_new, up_parts[3]))
+    up_other = [swap_core(part, ())[0] for part in up_parts]
+    *up_terms, up_new = products(second_kernel, (to,), row_parts, (*up_parts, *up_other))
 
     gate_terms[1], gate_terms[3], up_new = lax.optimization_barrier(
         (gate_terms[1], gate_terms[3], up_new)

time: 148 us -> 140 us (0.946)
  the two profiles are of different devices: /device:TPU:32 before, /device:TPU:8 now
where the time goes in v4:
time: 140 us
  waiting for transfers between devices  62.9 us (45%)
  starting transfers between devices  53.8 us (38%)
  Pallas kernels  19.6 us (14%)
    ppermute x6, starting transfers between devices, over_z(): lax.ppermute(parts[k], 'mp', mp_swap(0, k))  15.7 us
    ppermute x2, waiting for transfers between devices, last_sum(): lax.ppermute(both[1].astype(jnp.bfloat16), 'dp', dp_swap(0, 1, 0))  15.4 us
    ppermute x2, waiting for transfers between devices, second_sums(): got_a = lax.ppermute(sends[0], 'dp', dp_swap(2, 0, 0))  9.37 us
    all_to_all x1, starting transfers between devices, local(): lax.all_to_all(gate_step, 'mp', split_axis=0, concat_axis=0, tiled=True)  9.14 us
    ppermute x6, waiting for transfers between devices, over_z(): lax.ppermute(parts[k], 'mp', mp_swap(0, k))  8.47 us
    ppermute x2, waiting for transfers between devices, first_sums(): got_a = lax.ppermute(send_a, 'dp', dp_swap(1, 0, 0))  8.29 us
    pallas_call x2, Pallas kernels, products(): pl.pallas_call(lambda *refs: kernel(*refs[:len(arrays)], *refs[-6:]), in_...  7.14 us
    pallas_call x1, Pallas kernels, adam_flips(): pl.pallas_call(adam_flips_kernel, grid_spec=pltpu.PrefetchScalarGridSpec(...  4.97 us
  transfers between devices with their start and end apart: 36, of which 21 were waited for; matrix products, arithmetic and copies ran while one was open for 1% of the time, Pallas kernels for 11%

profile of v4, /device:TPU:8, one launch (start us, length us, event | category | flops | bytes accessed | tf_op | source)
XLA Modules:
  0.0 140.2 jit_solution(14525124835793942428)
XLA Ops:
  0.6 3.7 %adam_places.1 = bf16[16,32,1024]{2,1,0:T(8,128)(2,1)} custom-call(bf16[32,16384]{1,0:T(8,128)(2,1)} %refs_0_.1, bf16[32,16384]{1,0:T(8,128)(2,1)} %refs_1_.1, bf16[32,16384]{1,0:T(8,128)(2,1)} %refs_2_.2, bf16[32,16384]{1,0:T(8,128)(2,1)} %refs_3_.2), custom_call_target="tpu_custom_call" | custom-call | flops 1 | bytes 1 | tf_op jit(solution)/shard_map/adam_places/pallas_call | solution.py:73
  4.4 9.1 %all-to-all-start = ((bf16[16,32,1024]{2,1,0:T(8,128)(2,1)}), bf16[16,32,1024]{2,1,0:T(8,128)(2,1)S(1)}, u32[]{:S(2)}, u32[]{:S(2)}) async-start(bf16[16,32,1024]{2,1,0:T(8,128)(2,1)} %adam_places.1), calls=%async_computation | async-start | bytes 2097152 | tf_op jit(solution)/shard_map/all_to_all | solution.py:414
  13.7 0.1 stack.59.to_ref.refs_0_
  13.8 0.6 copy-done.4
  14.5 3.7 %attend.1 = (bf16[2,8,1024]{2,1,0:T(8,128)(2,1)S(1)}, bf16[2,8,1024]{2,1,0:T(8,128)(2,1)S(1)}, bf16[2,8,1024]{2,1,0:T(8,128)(2,1)S(1)}, bf16[2,8,1024]{2,1,0:T(8,128)(2,1)S(1)}) custom-call(s32[14]{0:T(128)S(1)} %stack.59.to_ref.refs_0_, s32[2]{0:T(128)S(1)} %copy-done.9, bf16[4,2,8192]{2,1,0:T(2,128)(2,1)S(1)} %copy-done.3, ...), custom_call_target="tpu_custom_call" | custom-call | flops 1 | bytes 1 | tf_op jit(solution)/shard_map/attend/pallas_call | solution.py:265
  18.2 5.0 %adam_flips.1 = (bf16[4,32,1024]{2,1,0:T(8,128)(2,1)}, bf16[4,32,1024]{2,1,0:T(8,128)(2,1)}, bf16[4,32,1024]{2,1,0:T(8,128)(2,1)}, bf16[4,32,1024]{2,1,0:T(8,128)(2,1)}) custom-call(s32[14]{0:T(128)} %copy-done.7, bf16[32,16384]{1,0:T(8,128)(2,1)} %refs_1_.2, bf16[32,16384]{1,0:T(8,128)(2,1)} %refs_1_.2, bf16[32,16384]{1,0:T(8,128)(2,1)} %refs_3_.3, ...), custom_call_target="tpu_custom_call" | custom-call | flops 1 | bytes 1 | tf_op jit(solution)/shard_map/adam_flips/pallas_call | solution.py:105
  23.1 1.6 %collective-permute-start = (bf16[2,8,1024]{2,1,0:T(8,128)(2,1)S(1)}, bf16[2,8,1024]{2,1,0:T(8,128)(2,1)S(1)}, u32[]{:S(2)}, u32[]{:S(2)}) collective-permute-start(bf16[2,8,1024]{2,1,0:T(8,128)(2,1)S(1)} %get-tuple-element.76), channel_id=1, source_target_pairs={{0,64},{16,80},{32,96},{48,112},{64,0},{80,16},{96,32},{112,48},{1... | collective-permute-start | bytes 98312 | tf_op jit(solution)/shard_map/ppermute | solution.py:425
  24.7 2.1 %collective-permute-start.1 = (bf16[2,8,1024]{2,1,0:T(8,128)(2,1)S(1)}, bf16[2,8,1024]{2,1,0:T(8,128)(2,1)S(1)}, u32[]{:S(2)}, u32[]{:S(2)}) collective-permute-start(bf16[2,8,1024]{2,1,0:T(8,128)(2,1)S(1)} %get-tuple-element.77), channel_id=1, source_target_pairs={{0,192},{16,208},{32,224},{48,240},{64,128},{80,144},{96,160},{112... | collective-permute-start | bytes 98312 | tf_op jit(solution)/shard_map/ppermute | solution.py:425
  26.8 0.6 collective-permute-start.2
  27.5 2.7 %collective-permute-done.1.refs_2_ = bf16[2,8,1024]{2,1,0:T(8,128)(2,1)S(1)} collective-permute-done((bf16[2,8,1024]{2,1,0:T(8,128)(2,1)S(1)}, bf16[2,8,1024]{2,1,0:T(8,128)(2,1)S(1)}, u32[]{:S(2)}, u32[]{:S(2)}) %collective-permute-start.1) | collective-permute-done | bytes 32800 | tf_op jit(solution)/shard_map/ppermute | solution.py:425
  30.2 2.0 %collective-permute-done.2.refs_3_ = bf16[2,8,1024]{2,1,0:T(8,128)(2,1)S(1)} collective-permute-done((bf16[2,8,1024]{2,1,0:T(8,128)(2,1)S(1)}, bf16[2,8,1024]{2,1,0:T(8,128)(2,1)S(1)}, u32[]{:S(2)}, u32[]{:S(2)}) %collective-permute-start.2) | collective-permute-done | bytes 32800 | tf_op jit(solution)/shard_map/ppermute | solution.py:425
  32.2 4.6 %collective-permute-start.3 = (bf16[4,8,1024]{2,1,0:T(8,128)(2,1)S(1)}, bf16[4,8,1024]{2,1,0:T(8,128)(2,1)S(1)}, u32[]{:S(2)}, u32[]{:S(2)}) collective-permute-start(bf16[4,8,1024]{2,1,0:T(8,128)(2,1)S(1)} %get-tuple-element.80), channel_id=1, source_target_pairs={{0,32},{16,48},{32,0},{48,16},{64,96},{80,112},{96,64},{112,80},{1... | collective-permute-start | bytes 196616 | tf_op jit(solution)/shard_map/ppermute | solution.py:427
  36.8 3.9 %collective-permute-done.3.second_ref = bf16[4,8,1024]{2,1,0:T(8,128)(2,1)S(1)} collective-permute-done((bf16[4,8,1024]{2,1,0:T(8,128)(2,1)S(1)}, bf16[4,8,1024]{2,1,0:T(8,128)(2,1)S(1)}, u32[]{:S(2)}, u32[]{:S(2)}) %collective-permute-start.3) | collective-permute-done | bytes 65568 | tf_op jit(solution)/shard_map/ppermute | solution.py:427
  40.7 3.2 %collective-permute-start.6 = (bf16[8,8,1024]{2,1,0:T(8,128)(2,1)S(1)}, bf16[8,8,1024]{2,1,0:T(8,128)(2,1)S(1)}, u32[]{:S(2)}, u32[]{:S(2)}) collective-permute-start(bf16[8,8,1024]{2,1,0:T(8,128)(2,1)S(1)} %interleave.1.refs_0_), channel_id=1, source_target_pairs={{0,3},{1,2},{2,1},{3,0},{4,7},{5,6},{6,5},{7,4},{8,11},{9,10},{10,... | collective-permute-start | bytes 393224 | tf_op jit(solution)/shard_map/ppermute | solution.py:338
  44.0 0.6 collective-permute-start.7
  44.5 2.1 %collective-permute-start.8 = (bf16[4,32,1024]{2,1,0:T(8,128)(2,1)}, bf16[4,32,1024]{2,1,0:T(8,128)(2,1)S(1)}, u32[]{:S(2)}, u32[]{:S(2)}) collective-permute-start(bf16[4,32,1024]{2,1,0:T(8,128)(2,1)} %get-tuple-element.83), channel_id=1, source_target_pairs={{0,12},{1,13},{2,14},{3,15},{4,8},{5,9},{6,10},{7,11},{8,4},{9,5},... | collective-permute-start | bytes 786440 | tf_op jit(solution)/shard_map/ppermute | solution.py:342
  46.6 1.5 %collective-permute-start.9 = (bf16[4,32,1024]{2,1,0:T(8,128)(2,1)S(1)}, bf16[4,32,1024]{2,1,0:T(8,128)(2,1)S(1)}, u32[]{:S(2)}, u32[]{:S(2)}) collective-permute-start(bf16[4,32,1024]{2,1,0:T(8,128)(2,1)S(1)} %copy-done.11), channel_id=1, source_target_pairs={{0,8},{1,9},{2,10},{3,11},{4,12},{5,13},{6,14},{7,15},{8,0},{9,1},... | collective-permute-start | bytes 786440 | tf_op jit(solution)/shard_map/ppermute | solution.py:342
  48.1 1.2 collective-permute-start.5
  49.2 3.1 %collective-permute-start.4 = (bf16[8,8,1024]{2,1,0:T(8,128)(2,1)S(1)}, bf16[8,8,1024]{2,1,0:T(8,128)(2,1)S(1)}, u32[]{:S(2)}, u32[]{:S(2)}) collective-permute-start(bf16[8,8,1024]{2,1,0:T(8,128)(2,1)S(1)} %interleave.1.refs_0_), channel_id=1, source_target_pairs={{0,1},{1,0},{2,3},{3,2},{4,5},{5,4},{6,7},{7,6},{8,9},{9,8},{10,11... | collective-permute-start | bytes 393224 | tf_op jit(solution)/shard_map/ppermute | solution.py:338
  52.3 3.1 %collective-permute-done.5.refs_2_ = bf16[8,8,1024]{2,1,0:T(8,128)(2,1)S(1)} collective-permute-done((bf16[8,8,1024]{2,1,0:T(8,128)(2,1)S(1)}, bf16[8,8,1024]{2,1,0:T(8,128)(2,1)S(1)}, u32[]{:S(2)}, u32[]{:S(2)}) %collective-permute-start.5) | collective-permute-done | bytes 131104 | tf_op jit(solution)/shard_map/ppermute | solution.py:338
  55.6 1.9 %collective-permute-start.11 = (bf16[8,32,1024]{2,1,0:T(8,128)(2,1)S(1)}, bf16[8,32,1024]{2,1,0:T(8,128)(2,1)S(1)}, u32[]{:S(2)}, u32[]{:S(2)}) collective-permute-start(bf16[8,32,1024]{2,1,0:T(8,128)(2,1)S(1)} %column.1.refs_0_.refs_1_), channel_id=1, source_target_pairs={{0,12},{1,13},{2,14},{3,15},{4,8},{5,9},{6,10},{7,11},{8,4},{9,5},... | collective-permute-start | bytes 1572872 | tf_op jit(solution)/shard_map/ppermute | solution.py:346
  57.5 2.1 %collective-permute-start.10 = (bf16[8,32,1024]{2,1,0:T(8,128)(2,1)S(1)}, bf16[8,32,1024]{2,1,0:T(8,128)(2,1)S(1)}, u32[]{:S(2)}, u32[]{:S(2)}) collective-permute-start(bf16[8,32,1024]{2,1,0:T(8,128)(2,1)S(1)} %column.1.refs_0_.refs_1_), channel_id=1, source_target_pairs={{0,4},{1,5},{2,6},{3,7},{4,0},{5,1},{6,2},{7,3},{8,12},{9,13},{10,... | collective-permute-start | bytes 1572872 | tf_op jit(solution)/shard_map/ppermute | solution.py:346
  59.6 0.1 regroup.1
  59.7 2.6 %collective-permute-start.18 = (bf16[4,32,1024]{2,1,0:T(8,128)(2,1)S(1)}, bf16[4,32,1024]{2,1,0:T(8,128)(2,1)S(1)}, u32[]{:S(2)}, u32[]{:S(2)}) collective-permute-start(bf16[4,32,1024]{2,1,0:T(8,128)(2,1)S(1)} %get-tuple-element.92), channel_id=1, source_target_pairs={{0,1},{1,0},{2,3},{3,2},{4,5},{5,4},{6,7},{7,6},{8,9},{9,8},{10,11... | collective-permute-start | bytes 786440 | tf_op jit(solution)/shard_map/ppermute | solution.py:338
  62.3 3.0 %collective-permute-start.19 = (bf16[4,32,1024]{2,1,0:T(8,128)(2,1)S(1)}, bf16[4,32,1024]{2,1,0:T(8,128)(2,1)S(1)}, u32[]{:S(2)}, u32[]{:S(2)}) collective-permute-start(bf16[4,32,1024]{2,1,0:T(8,128)(2,1)S(1)} %get-tuple-element.93), channel_id=1, source_target_pairs={{0,2},{1,3},{2,0},{3,1},{4,6},{5,7},{6,4},{7,5},{8,10},{9,11},{10,... | collective-permute-start | bytes 786440 | tf_op jit(solution)/shard_map/ppermute | solution.py:338
  65.3 0.1 fusion.26
  65.3 0.3 collective-permute-start.17
  65.6 0.8 collective-permute-done.11.refs_2_.refs_3_
  66.4 0.7 collective-permute-done.10.refs_1_.refs_2_
  67.2 2.1 %collective-permute-done.18.refs_10_.refs_7_ = bf16[4,32,1024]{2,1,0:T(8,128)(2,1)S(1)} collective-permute-done((bf16[4,32,1024]{2,1,0:T(8,128)(2,1)S(1)}, bf16[4,32,1024]{2,1,0:T(8,128)(2,1)S(1)}, u32[]{:S(2)}, u32[]{:S(2)}) %collective-permute-start.18) | collective-permute-done | bytes 262176 | tf_op jit(solution)/shard_map/ppermute | solution.py:338
  69.3 3.2 %collective-permute-done.19.refs_11_.refs_8_ = bf16[4,32,1024]{2,1,0:T(8,128)(2,1)S(1)} collective-permute-done((bf16[4,32,1024]{2,1,0:T(8,128)(2,1)S(1)}, bf16[4,32,1024]{2,1,0:T(8,128)(2,1)S(1)}, u32[]{:S(2)}, u32[]{:S(2)}) %collective-permute-start.19) | collective-permute-done | bytes 262176 | tf_op jit(solution)/shard_map/ppermute | solution.py:338
  72.5 2.6 %collective-permute-start.20 = (bf16[4,32,1024]{2,1,0:T(8,128)(2,1)S(1)}, bf16[4,32,1024]{2,1,0:T(8,128)(2,1)S(1)}, u32[]{:S(2)}, u32[]{:S(2)}) collective-permute-start(bf16[4,32,1024]{2,1,0:T(8,128)(2,1)S(1)} %get-tuple-element.95), channel_id=1, source_target_pairs={{0,3},{1,2},{2,1},{3,0},{4,7},{5,6},{6,5},{7,4},{8,11},{9,10},{10,... | collective-permute-start | bytes 786440 | tf_op jit(solution)/shard_map/ppermute | solution.py:338
  75.1 3.7 %collective-permute-done.13.refs_4_.refs_5_ = bf16[4,32,1024]{2,1,0:T(8,128)(2,1)S(1)} collective-permute-done((bf16[4,32,1024]{2,1,0:T(8,128)(2,1)S(1)}, bf16[4,32,1024]{2,1,0:T(8,128)(2,1)S(1)}, u32[]{:S(2)}, u32[]{:S(2)}) %collective-permute-start.13) | collective-permute-done | bytes 262176 | tf_op jit(solution)/shard_map/ppermute | solution.py:349
  78.9 3.3 %products.2 = (bf16[2,2,128,512]{3,2,1,0:T(8,128)(2,1)S(1)}, bf16[2,2,128,512]{3,2,1,0:T(8,128)(2,1)S(1)}, bf16[2,2,128,512]{3,2,1,0:T(8,128)(2,1)S(1)}, bf16[2,...) custom-call(bf16[8,32,1024]{2,1,0:T(8,128)(2,1)S(1)} %column.1.refs_0_.refs_1_, ...), custom_call_target="tpu_custom_call" | custom-call | flops 1 | bytes 1 | tf_op jit(solution)/shard_map/products/pallas_call | solution.py:319
  82.2 2.7 %collective-permute-start.26 = (bf16[2,2,128,512]{3,2,1,0:T(8,128)(2,1)S(1)}, bf16[2,2,128,512]{3,2,1,0:T(8,128)(2,1)S(1)}, u32[]{:S(2)}, u32[]{:S(2)}) collective-permute-start(bf16[2,2,128,512]{3,2,1,0:T(8,128)(2,1)S(1)} %get-tuple-element.106), channel_id=1, source_target_pairs={{0,192},{16,208},{32,224},{48,240},{64,128},{80,144},{96,160},{112... | collective-permute-start | bytes 1572872 | tf_op jit(solution)/shard_map/ppermute | solution.py:363
  84.8 0.5 collective-permute-start.23
  85.4 0.1 collective-permute-start.24
  85.5 0.9 collective-permute-done.22.refs_11_
  86.4 0.4 collective-permute-done.23.refs_12_
  86.8 0.4 collective-permute-done.24.refs_13_
  87.1 3.8 %products.3 = (bf16[2,2,128,512]{3,2,1,0:T(8,128)(2,1)S(1)}, bf16[2,2,128,512]{3,2,1,0:T(8,128)(2,1)S(1)}, bf16[2,2,128,512]{3,2,1,0:T(8,128)(2,1)S(1)}, bf16[2,...) custom-call(s32[14]{0:T(128)S(1)} %copy-done.8, bf16[8,32,1024]{2,1,0:T(8,128)(2,1)S(1)} %column.1.refs_0_.refs_1_, ...), custom_call_target="tpu_custom_call" | custom-call | flops 1 | bytes 1 | tf_op jit(solution)/shard_map/products/pallas_call | solution.py:319
  91.0 1.8 %collective-permute-done.25 = bf16[2,2,128,512]{3,2,1,0:T(8,128)(2,1)S(1)} collective-permute-done((bf16[2,2,128,512]{3,2,1,0:T(8,128)(2,1)S(1)}, bf16[2,2,128,512]{3,2,1,0:T(8,128)(2,1)S(1)}, u32[]{:S(2)}, u32[]{:S(2)}) %collective-permute-start.25) | collective-permute-done | bytes 524320 | tf_op jit(solution)/shard_map/ppermute | solution.py:362
  92.8 0.1 fusion.6
  92.9 3.5 %collective-permute-done.26 = bf16[2,2,128,512]{3,2,1,0:T(8,128)(2,1)S(1)} collective-permute-done((bf16[2,2,128,512]{3,2,1,0:T(8,128)(2,1)S(1)}, bf16[2,2,128,512]{3,2,1,0:T(8,128)(2,1)S(1)}, u32[]{:S(2)}, u32[]{:S(2)}) %collective-permute-start.26) | collective-permute-done | bytes 524320 | tf_op jit(solution)/shard_map/ppermute | solution.py:363
  96.4 3.0 %collective-permute-start.27 = (bf16[2,128,512]{2,1,0:T(8,128)(2,1)S(1)}, bf16[2,128,512]{2,1,0:T(8,128)(2,1)S(1)}, u32[]{:S(2)}, u32[]{:S(2)}) collective-permute-start(bf16[2,128,512]{2,1,0:T(8,128)(2,1)S(1)} %fusion.6), channel_id=1, source_target_pairs={{0,192},{16,208},{32,224},{48,240},{64,128},{80,144},{96,160},{112... | collective-permute-start | bytes 786440 | tf_op jit(solution)/shard_map/ppermute | solution.py:369
  99.4 2.0 %collective-permute-start.30 = (bf16[2,2,128,512]{3,2,1,0:T(8,128)(2,1)S(1)}, bf16[2,2,128,512]{3,2,1,0:T(8,128)(2,1)S(1)}, u32[]{:S(2)}, u32[]{:S(2)}) collective-permute-start(bf16[2,2,128,512]{3,2,1,0:T(8,128)(2,1)S(1)} %get-tuple-element.114), channel_id=1, source_target_pairs={{0,64},{16,80},{32,96},{48,112},{64,0},{80,16},{96,32},{112,48},{1... | collective-permute-start | bytes 1572872 | tf_op jit(solution)/shard_map/ppermute | solution.py:362
  101.5 0.3 collective-permute-start.32
  101.8 4.5 %collective-permute-done.27 = bf16[2,128,512]{2,1,0:T(8,128)(2,1)S(1)} collective-permute-done((bf16[2,128,512]{2,1,0:T(8,128)(2,1)S(1)}, bf16[2,128,512]{2,1,0:T(8,128)(2,1)S(1)}, u32[]{:S(2)}, u32[]{:S(2)}) %collective-permute-start.27) | collective-permute-done | bytes 262176 | tf_op jit(solution)/shard_map/ppermute | solution.py:369
  106.2 0.1 bitcast_add_fusion.4
  106.3 2.4 %collective-permute-done.28 = bf16[2,128,512]{2,1,0:T(8,128)(2,1)S(1)} collective-permute-done((bf16[2,128,512]{2,1,0:T(8,128)(2,1)S(1)}, bf16[2,128,512]{2,1,0:T(8,128)(2,1)S(1)}, u32[]{:S(2)}, u32[]{:S(2)}) %collective-permute-start.28) | collective-permute-done | bytes 262176 | tf_op jit(solution)/shard_map/ppermute | solution.py:370
  108.7 0.1 bitcast_add_fusion.3
  108.8 1.8 %collective-permute-start.29 = (bf16[128,1024]{1,0:T(8,128)(2,1)S(1)}, bf16[128,1024]{1,0:T(8,128)(2,1)S(1)}, u32[]{:S(2)}, u32[]{:S(2)}) collective-permute-start(bf16[128,1024]{1,0:T(8,128)(2,1)S(1)} %fusion.10), channel_id=1, source_target_pairs={{0,32},{16,48},{32,0},{48,16},{64,96},{80,112},{96,64},{112,80},{1... | collective-permute-start | bytes 786440 | tf_op jit(solution)/shard_map/ppermute | solution.py:375
  110.6 6.5 %collective-permute-done.30 = bf16[2,2,128,512]{3,2,1,0:T(8,128)(2,1)S(1)} collective-permute-done((bf16[2,2,128,512]{3,2,1,0:T(8,128)(2,1)S(1)}, bf16[2,2,128,512]{3,2,1,0:T(8,128)(2,1)S(1)}, u32[]{:S(2)}, u32[]{:S(2)}) %collective-permute-start.30) | collective-permute-done | bytes 524320 | tf_op jit(solution)/shard_map/ppermute | solution.py:362
  117.1 0.1 fusion.8
  117.2 0.5 collective-permute-start.31
  117.7 0.1 collective-permute-start.33
  117.8 2.0 %collective-permute-done.29 = bf16[128,1024]{1,0:T(8,128)(2,1)S(1)} collective-permute-done((bf16[128,1024]{1,0:T(8,128)(2,1)S(1)}, bf16[128,1024]{1,0:T(8,128)(2,1)S(1)}, u32[]{:S(2)}, u32[]{:S(2)}) %collective-permute-start.29) | collective-permute-done | bytes 262176 | tf_op jit(solution)/shard_map/ppermute | solution.py:375
  119.9 4.9 %collective-permute-done.31 = bf16[2,128,512]{2,1,0:T(8,128)(2,1)S(1)} collective-permute-done((bf16[2,128,512]{2,1,0:T(8,128)(2,1)S(1)}, bf16[2,128,512]{2,1,0:T(8,128)(2,1)S(1)}, u32[]{:S(2)}, u32[]{:S(2)}) %collective-permute-start.31) | collective-permute-done | bytes 262176 | tf_op jit(solution)/shard_map/ppermute | solution.py:369
  124.8 0.1 bitcast_add_fusion.2
  125.0 0.1 bitcast_add_fusion.1
  125.1 0.1 pad_maximum_fusion
  125.2 0.7 collective-permute-start.34
  125.9 13.3 %collective-permute-done.34 = bf16[128,1024]{1,0:T(8,128)(2,1)S(1)} collective-permute-done((bf16[128,1024]{1,0:T(8,128)(2,1)S(1)}, bf16[128,1024]{1,0:T(8,128)(2,1)S(1)}, u32[]{:S(2)}, u32[]{:S(2)}) %collective-permute-start.34) | collective-permute-done | bytes 262176 | tf_op jit(solution)/shard_map/ppermute | solution.py:375
  139.2 1.0 convolution_convert_fusion
  (60 shorter events, 0.6 us)
Async XLA Ops:
  4.3 9.3 %copy-start.10 = (bf16[8192]{0:T(1024)(128)(2,1)S(1)}, bf16[8192]{0:T(1024)(128)(2,1)}, u32[]{:S(2)}) copy-start(bf16[8192]{0:T(1024)(128)(2,1)} %param.31) | copy-start | bytes 49156
  4.3 9.4 %copy-start = (bf16[2,128,1024]{2,1,0:T(8,128)(2,1)S(1)}, bf16[2,128,1024]{2,1,0:T(8,128)(2,1)}, u32[]{:S(2)}) copy-start(bf16[2,128,1024]{2,1,0:T(8,128)(2,1)} %old_k_ref.1) | copy-start | bytes 1572868
  4.3 9.4 %copy-start.1 = (bf16[2,128,1024]{2,1,0:T(8,128)(2,1)S(1)}, bf16[2,128,1024]{2,1,0:T(8,128)(2,1)}, u32[]{:S(2)}) copy-start(bf16[2,128,1024]{2,1,0:T(8,128)(2,1)} %old_v_ref.1) | copy-start | bytes 1572868
  4.3 9.4 %copy-start.5 = (bf16[4,2,1024]{2,1,0:T(2,128)(2,1)S(1)}, bf16[4,2,1024]{2,1,0:T(2,128)(2,1)}, u32[]{:S(2)}) copy-start(bf16[4,2,1024]{2,1,0:T(2,128)(2,1)} %new_k_ref.1) | copy-start | bytes 49156
  4.3 9.4 %copy-start.6 = (bf16[4,2,1024]{2,1,0:T(2,128)(2,1)S(1)}, bf16[4,2,1024]{2,1,0:T(2,128)(2,1)}, u32[]{:S(2)}) copy-start(bf16[4,2,1024]{2,1,0:T(2,128)(2,1)} %new_v_ref.1) | copy-start | bytes 49156
  4.4 51.2 %all-to-all-start = ((bf16[16,32,1024]{2,1,0:T(8,128)(2,1)}), bf16[16,32,1024]{2,1,0:T(8,128)(2,1)S(1)}, u32[]{:S(2)}, u32[]{:S(2)}) async-start(bf16[16,32,1024]{2,1,0:T(8,128)(2,1)} %adam_places.1), calls=%async_computation | async-start | bytes 2097152 | tf_op jit(solution)/shard_map/all_to_all | solution.py:414
  13.5 0.9 copy-start.4
  13.5 1.0 copy-start.3
  13.6 0.8 copy-start.9
  14.5 3.7 %copy-start.7 = (s32[14]{0:T(128)}, s32[14]{0:T(128)S(1)}, u32[]{:S(2)}) copy-start(s32[14]{0:T(128)S(1)} %stack.59.to_ref.refs_0_) | copy-start | bytes 172
  23.1 23.5 %copy-start.11 = (bf16[4,32,1024]{2,1,0:T(8,128)(2,1)S(1)}, bf16[4,32,1024]{2,1,0:T(8,128)(2,1)}, u32[]{:S(2)}) copy-start(bf16[4,32,1024]{2,1,0:T(8,128)(2,1)} %get-tuple-element.84) | copy-start | bytes 786436
  23.1 4.3 %collective-permute-start = (bf16[2,8,1024]{2,1,0:T(8,128)(2,1)S(1)}, bf16[2,8,1024]{2,1,0:T(8,128)(2,1)S(1)}, u32[]{:S(2)}, u32[]{:S(2)}) collective-permute-start(bf16[2,8,1024]{2,1,0:T(8,128)(2,1)S(1)} %get-tuple-element.76), channel_id=1, source_target_pairs={{0,64},{16,80},{32,96},{48,112},{64,0},{80,16},{96,32},{112,48},{1... | collective-permute-start | bytes 98312 | tf_op jit(solution)/shard_map/ppermute | solution.py:425
  24.7 5.5 %collective-permute-start.1 = (bf16[2,8,1024]{2,1,0:T(8,128)(2,1)S(1)}, bf16[2,8,1024]{2,1,0:T(8,128)(2,1)S(1)}, u32[]{:S(2)}, u32[]{:S(2)}) collective-permute-start(bf16[2,8,1024]{2,1,0:T(8,128)(2,1)S(1)} %get-tuple-element.77), channel_id=1, source_target_pairs={{0,192},{16,208},{32,224},{48,240},{64,128},{80,144},{96,160},{112... | collective-permute-start | bytes 98312 | tf_op jit(solution)/shard_map/ppermute | solution.py:425
  26.8 5.4 %collective-permute-start.2 = (bf16[2,8,1024]{2,1,0:T(8,128)(2,1)S(1)}, bf16[2,8,1024]{2,1,0:T(8,128)(2,1)S(1)}, u32[]{:S(2)}, u32[]{:S(2)}) collective-permute-start(bf16[2,8,1024]{2,1,0:T(8,128)(2,1)S(1)} %get-tuple-element.78), channel_id=1, source_target_pairs={{0,128},{16,144},{32,160},{48,176},{64,192},{80,208},{96,224},{112... | collective-permute-start | bytes 98312 | tf_op jit(solution)/shard_map/ppermute | solution.py:425
  32.2 8.5 %collective-permute-start.3 = (bf16[4,8,1024]{2,1,0:T(8,128)(2,1)S(1)}, bf16[4,8,1024]{2,1,0:T(8,128)(2,1)S(1)}, u32[]{:S(2)}, u32[]{:S(2)}) collective-permute-start(bf16[4,8,1024]{2,1,0:T(8,128)(2,1)S(1)} %get-tuple-element.80), channel_id=1, source_target_pairs={{0,32},{16,48},{32,0},{48,16},{64,96},{80,112},{96,64},{112,80},{1... | collective-permute-start | bytes 196616 | tf_op jit(solution)/shard_map/ppermute | solution.py:427
  40.7 18.9 %copy-start.2 = (bf16[4,32,1024]{2,1,0:T(8,128)(2,1)S(1)}, bf16[4,32,1024]{2,1,0:T(8,128)(2,1)}, u32[]{:S(2)}) copy-start(bf16[4,32,1024]{2,1,0:T(8,128)(2,1)} %get-tuple-element.88.refs_0_) | copy-start | bytes 786436
  40.7 8.5 %collective-permute-start.6 = (bf16[8,8,1024]{2,1,0:T(8,128)(2,1)S(1)}, bf16[8,8,1024]{2,1,0:T(8,128)(2,1)S(1)}, u32[]{:S(2)}, u32[]{:S(2)}) collective-permute-start(bf16[8,8,1024]{2,1,0:T(8,128)(2,1)S(1)} %interleave.1.refs_0_), channel_id=1, source_target_pairs={{0,3},{1,2},{2,1},{3,0},{4,7},{5,6},{6,5},{7,4},{8,11},{9,10},{10,... | collective-permute-start | bytes 393224 | tf_op jit(solution)/shard_map/ppermute | solution.py:338
  44.0 11.6 %collective-permute-start.7 = (bf16[4,32,1024]{2,1,0:T(8,128)(2,1)}, bf16[4,32,1024]{2,1,0:T(8,128)(2,1)S(1)}, u32[]{:S(2)}, u32[]{:S(2)}) collective-permute-start(bf16[4,32,1024]{2,1,0:T(8,128)(2,1)} %get-tuple-element.82), channel_id=1, source_target_pairs={{0,4},{1,5},{2,6},{3,7},{4,0},{5,1},{6,2},{7,3},{8,12},{9,13},{10,... | collective-permute-start | bytes 786440 | tf_op jit(solution)/shard_map/ppermute | solution.py:342
  44.5 11.0 %collective-permute-start.8 = (bf16[4,32,1024]{2,1,0:T(8,128)(2,1)}, bf16[4,32,1024]{2,1,0:T(8,128)(2,1)S(1)}, u32[]{:S(2)}, u32[]{:S(2)}) collective-permute-start(bf16[4,32,1024]{2,1,0:T(8,128)(2,1)} %get-tuple-element.83), channel_id=1, source_target_pairs={{0,12},{1,13},{2,14},{3,15},{4,8},{5,9},{6,10},{7,11},{8,4},{9,5},... | collective-permute-start | bytes 786440 | tf_op jit(solution)/shard_map/ppermute | solution.py:342
  46.6 9.0 %collective-permute-start.9 = (bf16[4,32,1024]{2,1,0:T(8,128)(2,1)S(1)}, bf16[4,32,1024]{2,1,0:T(8,128)(2,1)S(1)}, u32[]{:S(2)}, u32[]{:S(2)}) collective-permute-start(bf16[4,32,1024]{2,1,0:T(8,128)(2,1)S(1)} %copy-done.11), channel_id=1, source_target_pairs={{0,8},{1,9},{2,10},{3,11},{4,12},{5,13},{6,14},{7,15},{8,0},{9,1},... | collective-permute-start | bytes 786440 | tf_op jit(solution)/shard_map/ppermute | solution.py:342
  48.1 7.4 %collective-permute-start.5 = (bf16[8,8,1024]{2,1,0:T(8,128)(2,1)S(1)}, bf16[8,8,1024]{2,1,0:T(8,128)(2,1)S(1)}, u32[]{:S(2)}, u32[]{:S(2)}) collective-permute-start(bf16[8,8,1024]{2,1,0:T(8,128)(2,1)S(1)} %interleave.1.refs_0_), channel_id=1, source_target_pairs={{0,2},{1,3},{2,0},{3,1},{4,6},{5,7},{6,4},{7,5},{8,10},{9,11},{10,... | collective-permute-start | bytes 393224 | tf_op jit(solution)/shard_map/ppermute | solution.py:338
  49.2 6.3 %collective-permute-start.4 = (bf16[8,8,1024]{2,1,0:T(8,128)(2,1)S(1)}, bf16[8,8,1024]{2,1,0:T(8,128)(2,1)S(1)}, u32[]{:S(2)}, u32[]{:S(2)}) collective-permute-start(bf16[8,8,1024]{2,1,0:T(8,128)(2,1)S(1)} %interleave.1.refs_0_), channel_id=1, source_target_pairs={{0,1},{1,0},{2,3},{3,2},{4,5},{5,4},{6,7},{7,6},{8,9},{9,8},{10,11... | collective-permute-start | bytes 393224 | tf_op jit(solution)/shard_map/ppermute | solution.py:338
  55.6 10.8 %collective-permute-start.11 = (bf16[8,32,1024]{2,1,0:T(8,128)(2,1)S(1)}, bf16[8,32,1024]{2,1,0:T(8,128)(2,1)S(1)}, u32[]{:S(2)}, u32[]{:S(2)}) collective-permute-start(bf16[8,32,1024]{2,1,0:T(8,128)(2,1)S(1)} %column.1.refs_0_.refs_1_), channel_id=1, source_target_pairs={{0,12},{1,13},{2,14},{3,15},{4,8},{5,9},{6,10},{7,11},{8,4},{9,5},... | collective-permute-start | bytes 1572872 | tf_op jit(solution)/shard_map/ppermute | solution.py:346
  57.5 9.6 %collective-permute-start.10 = (bf16[8,32,1024]{2,1,0:T(8,128)(2,1)S(1)}, bf16[8,32,1024]{2,1,0:T(8,128)(2,1)S(1)}, u32[]{:S(2)}, u32[]{:S(2)}) collective-permute-start(bf16[8,32,1024]{2,1,0:T(8,128)(2,1)S(1)} %column.1.refs_0_.refs_1_), channel_id=1, source_target_pairs={{0,4},{1,5},{2,6},{3,7},{4,0},{5,1},{6,2},{7,3},{8,12},{9,13},{10,... | collective-permute-start | bytes 1572872 | tf_op jit(solution)/shard_map/ppermute | solution.py:346
  59.7 9.6 %collective-permute-start.18 = (bf16[4,32,1024]{2,1,0:T(8,128)(2,1)S(1)}, bf16[4,32,1024]{2,1,0:T(8,128)(2,1)S(1)}, u32[]{:S(2)}, u32[]{:S(2)}) collective-permute-start(bf16[4,32,1024]{2,1,0:T(8,128)(2,1)S(1)} %get-tuple-element.92), channel_id=1, source_target_pairs={{0,1},{1,0},{2,3},{3,2},{4,5},{5,4},{6,7},{7,6},{8,9},{9,8},{10,11... | collective-permute-start | bytes 786440 | tf_op jit(solution)/shard_map/ppermute | solution.py:338
  62.3 10.2 %collective-permute-start.19 = (bf16[4,32,1024]{2,1,0:T(8,128)(2,1)S(1)}, bf16[4,32,1024]{2,1,0:T(8,128)(2,1)S(1)}, u32[]{:S(2)}, u32[]{:S(2)}) collective-permute-start(bf16[4,32,1024]{2,1,0:T(8,128)(2,1)S(1)} %get-tuple-element.93), channel_id=1, source_target_pairs={{0,2},{1,3},{2,0},{3,1},{4,6},{5,7},{6,4},{7,5},{8,10},{9,11},{10,... | collective-permute-start | bytes 786440 | tf_op jit(solution)/shard_map/ppermute | solution.py:338
  65.3 7.1 %collective-permute-start.17 = (bf16[128,1024]{1,0:T(8,128)(2,1)S(1)}, bf16[128,1024]{1,0:T(8,128)(2,1)S(1)}, u32[]{:S(2)}, u32[]{:S(2)}) collective-permute-start(bf16[128,1024]{1,0:T(8,128)(2,1)S(1)} %get-tuple-element.119), channel_id=1, source_target_pairs={{0,16},{16,0},{32,48},{48,32},{64,80},{80,64},{96,112},{112,96},{1... | collective-permute-start | bytes 786440 | tf_op jit(solution)/shard_map/ppermute | solution.py:356
  66.4 6.1 %collective-permute-start.16 = (bf16[128,1024]{1,0:T(8,128)(2,1)S(1)}, bf16[128,1024]{1,0:T(8,128)(2,1)S(1)}, u32[]{:S(2)}, u32[]{:S(2)}) collective-permute-start(bf16[128,1024]{1,0:T(8,128)(2,1)S(1)} %get-tuple-element.120), channel_id=1, source_target_pairs={{0,16},{16,0},{32,48},{48,32},{64,80},{80,64},{96,112},{112,96},{1... | collective-permute-start | bytes 786440 | tf_op jit(solution)/shard_map/ppermute | solution.py:356
  67.1 8.0 %collective-permute-start.15 = (bf16[128,1024]{1,0:T(8,128)(2,1)S(1)}, bf16[128,1024]{1,0:T(8,128)(2,1)S(1)}, u32[]{:S(2)}, u32[]{:S(2)}) collective-permute-start(bf16[128,1024]{1,0:T(8,128)(2,1)S(1)} %get-tuple-element.121), channel_id=1, source_target_pairs={{0,16},{16,0},{32,48},{48,32},{64,80},{80,64},{96,112},{112,96},{1... | collective-permute-start | bytes 786440 | tf_op jit(solution)/shard_map/ppermute | solution.py:356
  69.3 5.8 %collective-permute-start.14 = (bf16[128,1024]{1,0:T(8,128)(2,1)S(1)}, bf16[128,1024]{1,0:T(8,128)(2,1)S(1)}, u32[]{:S(2)}, u32[]{:S(2)}) collective-permute-start(bf16[128,1024]{1,0:T(8,128)(2,1)S(1)} %get-tuple-element.122), channel_id=1, source_target_pairs={{0,16},{16,0},{32,48},{48,32},{64,80},{80,64},{96,112},{112,96},{1... | collective-permute-start | bytes 786440 | tf_op jit(solution)/shard_map/ppermute | solution.py:356
  72.5 6.4 %collective-permute-start.13 = (bf16[4,32,1024]{2,1,0:T(8,128)(2,1)S(1)}, bf16[4,32,1024]{2,1,0:T(8,128)(2,1)S(1)}, u32[]{:S(2)}, u32[]{:S(2)}) collective-permute-start(bf16[4,32,1024]{2,1,0:T(8,128)(2,1)S(1)} %slice.91), channel_id=1, source_target_pairs={{0,4},{1,5},{2,6},{3,7},{4,0},{5,1},{6,2},{7,3},{8,12},{9,13},{10,... | collective-permute-start | bytes 786440 | tf_op jit(solution)/shard_map/ppermute | solution.py:349
  72.5 6.4 %collective-permute-start.12 = (bf16[4,32,1024]{2,1,0:T(8,128)(2,1)S(1)}, bf16[4,32,1024]{2,1,0:T(8,128)(2,1)S(1)}, u32[]{:S(2)}, u32[]{:S(2)}) collective-permute-start(bf16[4,32,1024]{2,1,0:T(8,128)(2,1)S(1)} %slice.90), channel_id=1, source_target_pairs={{0,12},{1,13},{2,14},{3,15},{4,8},{5,9},{6,10},{7,11},{8,4},{9,5},... | collective-permute-start | bytes 786440 | tf_op jit(solution)/shard_map/ppermute | solution.py:348
  72.5 12.3 %collective-permute-start.20 = (bf16[4,32,1024]{2,1,0:T(8,128)(2,1)S(1)}, bf16[4,32,1024]{2,1,0:T(8,128)(2,1)S(1)}, u32[]{:S(2)}, u32[]{:S(2)}) collective-permute-start(bf16[4,32,1024]{2,1,0:T(8,128)(2,1)S(1)} %get-tuple-element.95), channel_id=1, source_target_pairs={{0,3},{1,2},{2,1},{3,0},{4,7},{5,6},{6,5},{7,4},{8,11},{9,10},{10,... | collective-permute-start | bytes 786440 | tf_op jit(solution)/shard_map/ppermute | solution.py:338
  75.1 10.2 %collective-permute-start.21 = (bf16[4,32,1024]{2,1,0:T(8,128)(2,1)S(1)}, bf16[4,32,1024]{2,1,0:T(8,128)(2,1)S(1)}, u32[]{:S(2)}, u32[]{:S(2)}) collective-permute-start(bf16[4,32,1024]{2,1,0:T(8,128)(2,1)S(1)} %get-tuple-element.99.refs_6_), channel_id=1, source_target_pairs={{0,16},{16,0},{32,48},{48,32},{64,80},{80,64},{96,112},{112,96},{1... | collective-permute-start | bytes 786440 | tf_op jit(solution)/shard_map/ppermute | solution.py:356
  82.2 10.6 %collective-permute-start.25 = (bf16[2,2,128,512]{3,2,1,0:T(8,128)(2,1)S(1)}, bf16[2,2,128,512]{3,2,1,0:T(8,128)(2,1)S(1)}, u32[]{:S(2)}, u32[]{:S(2)}) collective-permute-start(bf16[2,2,128,512]{3,2,1,0:T(8,128)(2,1)S(1)} %get-tuple-element.104), channel_id=1, source_target_pairs={{0,64},{16,80},{32,96},{48,112},{64,0},{80,16},{96,32},{112,48},{1... | collective-permute-start | bytes 1572872 | tf_op jit(solution)/shard_map/ppermute | solution.py:362
  82.2 4.9 %copy-start.8 = (s32[14]{0:T(128)S(1)}, s32[14]{0:T(128)}, u32[]{:S(2)}) copy-start(s32[14]{0:T(128)} %copy-done.7) | copy-start | bytes 172
  82.2 14.1 %collective-permute-start.26 = (bf16[2,2,128,512]{3,2,1,0:T(8,128)(2,1)S(1)}, bf16[2,2,128,512]{3,2,1,0:T(8,128)(2,1)S(1)}, u32[]{:S(2)}, u32[]{:S(2)}) collective-permute-start(bf16[2,2,128,512]{3,2,1,0:T(8,128)(2,1)S(1)} %get-tuple-element.106), channel_id=1, source_target_pairs={{0,192},{16,208},{32,224},{48,240},{64,128},{80,144},{96,160},{112... | collective-permute-start | bytes 1572872 | tf_op jit(solution)/shard_map/ppermute | solution.py:363
  84.8 1.5 %collective-permute-start.22 = (bf16[4,32,1024]{2,1,0:T(8,128)(2,1)S(1)}, bf16[4,32,1024]{2,1,0:T(8,128)(2,1)S(1)}, u32[]{:S(2)}, u32[]{:S(2)}) collective-permute-start(bf16[4,32,1024]{2,1,0:T(8,128)(2,1)S(1)} %collective-permute-done.18.refs_10_.refs_7_), channel_id=1, source_target_pairs={{0,16},{16,0},{32,48},{48,32},{64,80},{80,64},{96,112},{112,96},{1... | collective-permute-start | bytes 786440 | tf_op jit(solution)/shard_map/ppermute | solution.py:356
  84.8 1.9 %collective-permute-start.23 = (bf16[4,32,1024]{2,1,0:T(8,128)(2,1)S(1)}, bf16[4,32,1024]{2,1,0:T(8,128)(2,1)S(1)}, u32[]{:S(2)}, u32[]{:S(2)}) collective-permute-start(bf16[4,32,1024]{2,1,0:T(8,128)(2,1)S(1)} %collective-permute-done.19.refs_11_.refs_8_), channel_id=1, source_target_pairs={{0,16},{16,0},{32,48},{48,32},{64,80},{80,64},{96,112},{112,96},{1... | collective-permute-start | bytes 786440 | tf_op jit(solution)/shard_map/ppermute | solution.py:356
  85.4 1.8 %collective-permute-start.24 = (bf16[4,32,1024]{2,1,0:T(8,128)(2,1)S(1)}, bf16[4,32,1024]{2,1,0:T(8,128)(2,1)S(1)}, u32[]{:S(2)}, u32[]{:S(2)}) collective-permute-start(bf16[4,32,1024]{2,1,0:T(8,128)(2,1)S(1)} %collective-permute-done.20.refs_9_), channel_id=1, source_target_pairs={{0,16},{16,0},{32,48},{48,32},{64,80},{80,64},{96,112},{112,96},{1... | collective-permute-start | bytes 786440 | tf_op jit(solution)/shard_map/ppermute | solution.py:356
  96.4 9.8 %collective-permute-start.27 = (bf16[2,128,512]{2,1,0:T(8,128)(2,1)S(1)}, bf16[2,128,512]{2,1,0:T(8,128)(2,1)S(1)}, u32[]{:S(2)}, u32[]{:S(2)}) collective-permute-start(bf16[2,128,512]{2,1,0:T(8,128)(2,1)S(1)} %fusion.6), channel_id=1, source_target_pairs={{0,192},{16,208},{32,224},{48,240},{64,128},{80,144},{96,160},{112... | collective-permute-start | bytes 786440 | tf_op jit(solution)/shard_map/ppermute | solution.py:369
  99.4 9.2 %collective-permute-start.28 = (bf16[2,128,512]{2,1,0:T(8,128)(2,1)S(1)}, bf16[2,128,512]{2,1,0:T(8,128)(2,1)S(1)}, u32[]{:S(2)}, u32[]{:S(2)}) collective-permute-start(bf16[2,128,512]{2,1,0:T(8,128)(2,1)S(1)} %fusion.7), channel_id=1, source_target_pairs={{0,64},{16,80},{32,96},{48,112},{64,0},{80,16},{96,32},{112,48},{1... | collective-permute-start | bytes 786440 | tf_op jit(solution)/shard_map/ppermute | solution.py:370
  99.4 17.6 %collective-permute-start.30 = (bf16[2,2,128,512]{3,2,1,0:T(8,128)(2,1)S(1)}, bf16[2,2,128,512]{3,2,1,0:T(8,128)(2,1)S(1)}, u32[]{:S(2)}, u32[]{:S(2)}) collective-permute-start(bf16[2,2,128,512]{3,2,1,0:T(8,128)(2,1)S(1)} %get-tuple-element.114), channel_id=1, source_target_pairs={{0,64},{16,80},{32,96},{48,112},{64,0},{80,16},{96,32},{112,48},{1... | collective-permute-start | bytes 1572872 | tf_op jit(solution)/shard_map/ppermute | solution.py:362
  101.5 16.2 %collective-permute-start.32 = (bf16[2,2,128,512]{3,2,1,0:T(8,128)(2,1)S(1)}, bf16[2,2,128,512]{3,2,1,0:T(8,128)(2,1)S(1)}, u32[]{:S(2)}, u32[]{:S(2)}) collective-permute-start(bf16[2,2,128,512]{3,2,1,0:T(8,128)(2,1)S(1)} %get-tuple-element.116), channel_id=1, source_target_pairs={{0,192},{16,208},{32,224},{48,240},{64,128},{80,144},{96,160},{112... | collective-permute-start | bytes 1572872 | tf_op jit(solution)/shard_map/ppermute | solution.py:363
  108.8 11.0 %collective-permute-start.29 = (bf16[128,1024]{1,0:T(8,128)(2,1)S(1)}, bf16[128,1024]{1,0:T(8,128)(2,1)S(1)}, u32[]{:S(2)}, u32[]{:S(2)}) collective-permute-start(bf16[128,1024]{1,0:T(8,128)(2,1)S(1)} %fusion.10), channel_id=1, source_target_pairs={{0,32},{16,48},{32,0},{48,16},{64,96},{80,112},{96,64},{112,80},{1... | collective-permute-start | bytes 786440 | tf_op jit(solution)/shard_map/ppermute | solution.py:375
  117.2 7.7 %collective-permute-start.31 = (bf16[2,128,512]{2,1,0:T(8,128)(2,1)S(1)}, bf16[2,128,512]{2,1,0:T(8,128)(2,1)S(1)}, u32[]{:S(2)}, u32[]{:S(2)}) collective-permute-start(bf16[2,128,512]{2,1,0:T(8,128)(2,1)S(1)} %fusion.8), channel_id=1, source_target_pairs={{0,192},{16,208},{32,224},{48,240},{64,128},{80,144},{96,160},{112... | collective-permute-start | bytes 786440 | tf_op jit(solution)/shard_map/ppermute | solution.py:369
  117.7 7.2 %collective-permute-start.33 = (bf16[2,128,512]{2,1,0:T(8,128)(2,1)S(1)}, bf16[2,128,512]{2,1,0:T(8,128)(2,1)S(1)}, u32[]{:S(2)}, u32[]{:S(2)}) collective-permute-start(bf16[2,128,512]{2,1,0:T(8,128)(2,1)S(1)} %fusion.9), channel_id=1, source_target_pairs={{0,64},{16,80},{32,96},{48,112},{64,0},{80,16},{96,32},{112,48},{1... | collective-permute-start | bytes 786440 | tf_op jit(solution)/shard_map/ppermute | solution.py:370
  125.2 14.0 %collective-permute-start.34 = (bf16[128,1024]{1,0:T(8,128)(2,1)S(1)}, bf16[128,1024]{1,0:T(8,128)(2,1)S(1)}, u32[]{:S(2)}, u32[]{:S(2)}) collective-permute-start(bf16[128,1024]{1,0:T(8,128)(2,1)S(1)} %fusion.11), channel_id=1, source_target_pairs={{0,32},{16,48},{32,0},{48,16},{64,96},{80,112},{96,64},{112,80},{1... | collective-permute-start | bytes 786440 | tf_op jit(solution)/shard_map/ppermute | solution.py:375

commit v5 on v4

--- a/solution.py
+++ b/solution.py
@@ -294,7 +294,7 @@
 
 
 def first_kernel(*refs):
-    row_refs, own_ref, piece_refs = refs[:5], refs[5], refs[6:10]
+    row_refs, own_ref, piece_refs = refs[:5], refs[5], refs[6:-6]
     *term_refs, new_ref, other_ref = refs[-6:]
     new_ref[...] = own_ref[...]
     at = 0
@@ -429,7 +429,7 @@
     column, up_parts, gate_own = lax.optimization_barrier(
         (join_rows(along_z), up_parts, gate_own)
     )
-    gate_other = swap_core(gate_own, (128, 256, 384))
+    gate_other = swap_core(gate_own, (176, 352))
     row_parts = over_y_ring(column)
     up_parts = over_z(regroup(up_parts))
     *gate_terms, gate_new = products(

time: 140 us -> 140 us (level)
  the two profiles are of different devices: /device:TPU:8 before, /device:TPU:32 now
where the time goes in v5:
time: 140 us; the launch traced here: 138 us
  waiting for transfers between devices  59.4 us (42%)
  starting transfers between devices  54.8 us (39%)
  Pallas kernels  19.6 us (14%)
    ppermute x2, starting transfers between devices, last_sum(): lax.ppermute(both[1].astype(jnp.bfloat16), 'dp', dp_swap(0, 1, 0))  11.1 us
    ppermute x2, waiting for transfers between devices, last_sum(): lax.ppermute(both[1].astype(jnp.bfloat16), 'dp', dp_swap(0, 1, 0))  10.3 us
    all_to_all x1, starting transfers between devices, local(): lax.all_to_all(gate_step, 'mp', split_axis=0, concat_axis=0, tiled=True)  8.8 us
    ppermute x6, waiting for transfers between devices, over_z(): lax.ppermute(parts[k], 'mp', mp_swap(0, k))  8.71 us
    ppermute x2, waiting for transfers between devices, second_sums(): got_a = lax.ppermute(sends[0], 'dp', dp_swap(2, 0, 0))  7.86 us
    ppermute x6, starting transfers between devices, over_z(): lax.ppermute(parts[k], 'mp', mp_swap(0, k))  7.46 us
    pallas_call x2, Pallas kernels, products(): pl.pallas_call(lambda *refs: kernel(*refs[:len(arrays)], *refs[-6:]), in_...  7.14 us
    ppermute x2, waiting for transfers between devices, first_sums(): got_a = lax.ppermute(send_a, 'dp', dp_swap(1, 0, 0))  6.12 us
  transfers between devices with their start and end apart: 35, of which 25 were waited for; matrix products, arithmetic and copies ran while one was open for 1% of the time, Pallas kernels for 12%

profile of v5, /device:TPU:32, one launch (start us, length us, event | category | flops | bytes accessed | tf_op | source)
XLA Modules:
  0.0 137.8 jit_solution(11246764299966631358)
XLA Ops:
  0.6 3.7 %adam_places.1 = bf16[16,32,1024]{2,1,0:T(8,128)(2,1)} custom-call(bf16[32,16384]{1,0:T(8,128)(2,1)} %refs_0_.1, bf16[32,16384]{1,0:T(8,128)(2,1)} %refs_1_.1, bf16[32,16384]{1,0:T(8,128)(2,1)} %refs_2_.2, bf16[32,16384]{1,0:T(8,128)(2,1)} %refs_3_.2), custom_call_target="tpu_custom_call" | custom-call | flops 1 | bytes 1 | tf_op jit(solution)/shard_map/adam_places/pallas_call | solution.py:73
  4.4 8.8 %all-to-all-start = ((bf16[16,32,1024]{2,1,0:T(8,128)(2,1)}), bf16[16,32,1024]{2,1,0:T(8,128)(2,1)S(1)}, u32[]{:S(2)}, u32[]{:S(2)}) async-start(bf16[16,32,1024]{2,1,0:T(8,128)(2,1)} %adam_places.1), calls=%async_computation | async-start | bytes 2097152 | tf_op jit(solution)/shard_map/all_to_all | solution.py:414
  13.3 0.1 stack.59.to_ref.refs_0_
  13.4 0.6 copy-done.4
  14.1 3.7 %attend.1 = (bf16[2,8,1024]{2,1,0:T(8,128)(2,1)S(1)}, bf16[2,8,1024]{2,1,0:T(8,128)(2,1)S(1)}, bf16[2,8,1024]{2,1,0:T(8,128)(2,1)S(1)}, bf16[2,8,1024]{2,1,0:T(8,128)(2,1)S(1)}) custom-call(s32[14]{0:T(128)S(1)} %stack.59.to_ref.refs_0_, s32[2]{0:T(128)S(1)} %copy-done.9, bf16[4,2,8192]{2,1,0:T(2,128)(2,1)S(1)} %copy-done.3, ...), custom_call_target="tpu_custom_call" | custom-call | flops 1 | bytes 1 | tf_op jit(solution)/shard_map/attend/pallas_call | solution.py:265
  17.8 5.0 %adam_flips.1 = (bf16[4,32,1024]{2,1,0:T(8,128)(2,1)}, bf16[4,32,1024]{2,1,0:T(8,128)(2,1)}, bf16[4,32,1024]{2,1,0:T(8,128)(2,1)}, bf16[4,32,1024]{2,1,0:T(8,128)(2,1)}) custom-call(s32[14]{0:T(128)} %copy-done.7, bf16[32,16384]{1,0:T(8,128)(2,1)} %refs_1_.2, bf16[32,16384]{1,0:T(8,128)(2,1)} %refs_1_.2, bf16[32,16384]{1,0:T(8,128)(2,1)} %refs_3_.3, ...), custom_call_target="tpu_custom_call" | custom-call | flops 1 | bytes 1 | tf_op jit(solution)/shard_map/adam_flips/pallas_call | solution.py:105
  22.8 1.6 %collective-permute-start = (bf16[2,8,1024]{2,1,0:T(8,128)(2,1)S(1)}, bf16[2,8,1024]{2,1,0:T(8,128)(2,1)S(1)}, u32[]{:S(2)}, u32[]{:S(2)}) collective-permute-start(bf16[2,8,1024]{2,1,0:T(8,128)(2,1)S(1)} %get-tuple-element.76), channel_id=1, source_target_pairs={{0,64},{16,80},{32,96},{48,112},{64,0},{80,16},{96,32},{112,48},{1... | collective-permute-start | bytes 98312 | tf_op jit(solution)/shard_map/ppermute | solution.py:425
  24.4 2.1 %collective-permute-start.1 = (bf16[2,8,1024]{2,1,0:T(8,128)(2,1)S(1)}, bf16[2,8,1024]{2,1,0:T(8,128)(2,1)S(1)}, u32[]{:S(2)}, u32[]{:S(2)}) collective-permute-start(bf16[2,8,1024]{2,1,0:T(8,128)(2,1)S(1)} %get-tuple-element.77), channel_id=1, source_target_pairs={{0,192},{16,208},{32,224},{48,240},{64,128},{80,144},{96,160},{112... | collective-permute-start | bytes 98312 | tf_op jit(solution)/shard_map/ppermute | solution.py:425
  26.5 0.6 collective-permute-start.2
  27.1 2.7 %collective-permute-done.1.refs_2_ = bf16[2,8,1024]{2,1,0:T(8,128)(2,1)S(1)} collective-permute-done((bf16[2,8,1024]{2,1,0:T(8,128)(2,1)S(1)}, bf16[2,8,1024]{2,1,0:T(8,128)(2,1)S(1)}, u32[]{:S(2)}, u32[]{:S(2)}) %collective-permute-start.1) | collective-permute-done | bytes 32800 | tf_op jit(solution)/shard_map/ppermute | solution.py:425
  29.9 2.0 %collective-permute-done.2.refs_3_ = bf16[2,8,1024]{2,1,0:T(8,128)(2,1)S(1)} collective-permute-done((bf16[2,8,1024]{2,1,0:T(8,128)(2,1)S(1)}, bf16[2,8,1024]{2,1,0:T(8,128)(2,1)S(1)}, u32[]{:S(2)}, u32[]{:S(2)}) %collective-permute-start.2) | collective-permute-done | bytes 32800 | tf_op jit(solution)/shard_map/ppermute | solution.py:425
  31.9 4.6 %collective-permute-start.3 = (bf16[4,8,1024]{2,1,0:T(8,128)(2,1)S(1)}, bf16[4,8,1024]{2,1,0:T(8,128)(2,1)S(1)}, u32[]{:S(2)}, u32[]{:S(2)}) collective-permute-start(bf16[4,8,1024]{2,1,0:T(8,128)(2,1)S(1)} %get-tuple-element.80), channel_id=1, source_target_pairs={{0,32},{16,48},{32,0},{48,16},{64,96},{80,112},{96,64},{112,80},{1... | collective-permute-start | bytes 196616 | tf_op jit(solution)/shard_map/ppermute | solution.py:427
  36.5 4.1 %collective-permute-done.3.second_ref = bf16[4,8,1024]{2,1,0:T(8,128)(2,1)S(1)} collective-permute-done((bf16[4,8,1024]{2,1,0:T(8,128)(2,1)S(1)}, bf16[4,8,1024]{2,1,0:T(8,128)(2,1)S(1)}, u32[]{:S(2)}, u32[]{:S(2)}) %collective-permute-start.3) | collective-permute-done | bytes 65568 | tf_op jit(solution)/shard_map/ppermute | solution.py:427
  40.6 3.1 %collective-permute-start.6 = (bf16[8,8,1024]{2,1,0:T(8,128)(2,1)S(1)}, bf16[8,8,1024]{2,1,0:T(8,128)(2,1)S(1)}, u32[]{:S(2)}, u32[]{:S(2)}) collective-permute-start(bf16[8,8,1024]{2,1,0:T(8,128)(2,1)S(1)} %interleave.1.refs_0_), channel_id=1, source_target_pairs={{0,3},{1,2},{2,1},{3,0},{4,7},{5,6},{6,5},{7,4},{8,11},{9,10},{10,... | collective-permute-start | bytes 393224 | tf_op jit(solution)/shard_map/ppermute | solution.py:338
  43.7 1.6 %collective-permute-start.7 = (bf16[4,32,1024]{2,1,0:T(8,128)(2,1)}, bf16[4,32,1024]{2,1,0:T(8,128)(2,1)S(1)}, u32[]{:S(2)}, u32[]{:S(2)}) collective-permute-start(bf16[4,32,1024]{2,1,0:T(8,128)(2,1)} %get-tuple-element.82), channel_id=1, source_target_pairs={{0,4},{1,5},{2,6},{3,7},{4,0},{5,1},{6,2},{7,3},{8,12},{9,13},{10,... | collective-permute-start | bytes 786440 | tf_op jit(solution)/shard_map/ppermute | solution.py:342
  45.3 1.2 collective-permute-start.8
  46.5 1.4 %collective-permute-start.9 = (bf16[4,32,1024]{2,1,0:T(8,128)(2,1)S(1)}, bf16[4,32,1024]{2,1,0:T(8,128)(2,1)S(1)}, u32[]{:S(2)}, u32[]{:S(2)}) collective-permute-start(bf16[4,32,1024]{2,1,0:T(8,128)(2,1)S(1)} %copy-done.11), channel_id=1, source_target_pairs={{0,8},{1,9},{2,10},{3,11},{4,12},{5,13},{6,14},{7,15},{8,0},{9,1},... | collective-permute-start | bytes 786440 | tf_op jit(solution)/shard_map/ppermute | solution.py:342
  48.0 2.0 %collective-permute-done.6.refs_3_ = bf16[8,8,1024]{2,1,0:T(8,128)(2,1)S(1)} collective-permute-done((bf16[8,8,1024]{2,1,0:T(8,128)(2,1)S(1)}, bf16[8,8,1024]{2,1,0:T(8,128)(2,1)S(1)}, u32[]{:S(2)}, u32[]{:S(2)}) %collective-permute-start.6) | collective-permute-done | bytes 131104 | tf_op jit(solution)/shard_map/ppermute | solution.py:338
  50.0 4.0 %collective-permute-done.5.refs_2_ = bf16[8,8,1024]{2,1,0:T(8,128)(2,1)S(1)} collective-permute-done((bf16[8,8,1024]{2,1,0:T(8,128)(2,1)S(1)}, bf16[8,8,1024]{2,1,0:T(8,128)(2,1)S(1)}, u32[]{:S(2)}, u32[]{:S(2)}) %collective-permute-start.5) | collective-permute-done | bytes 131104 | tf_op jit(solution)/shard_map/ppermute | solution.py:338
  53.9 1.0 collective-permute-done.4.refs_1_
  55.0 1.3 collective-permute-done.8.refs_2_
  56.2 3.4 %collective-permute-start.11 = (bf16[8,32,1024]{2,1,0:T(8,128)(2,1)S(1)}, bf16[8,32,1024]{2,1,0:T(8,128)(2,1)S(1)}, u32[]{:S(2)}, u32[]{:S(2)}) collective-permute-start(bf16[8,32,1024]{2,1,0:T(8,128)(2,1)S(1)} %column.1.refs_0_.refs_1_), channel_id=1, source_target_pairs={{0,12},{1,13},{2,14},{3,15},{4,8},{5,9},{6,10},{7,11},{8,4},{9,5},... | collective-permute-start | bytes 1572872 | tf_op jit(solution)/shard_map/ppermute | solution.py:346
  59.7 0.1 regroup.1
  59.7 0.1 collective-permute-start.17
  59.8 3.2 %collective-permute-start.18 = (bf16[4,32,1024]{2,1,0:T(8,128)(2,1)S(1)}, bf16[4,32,1024]{2,1,0:T(8,128)(2,1)S(1)}, u32[]{:S(2)}, u32[]{:S(2)}) collective-permute-start(bf16[4,32,1024]{2,1,0:T(8,128)(2,1)S(1)} %get-tuple-element.93), channel_id=1, source_target_pairs={{0,2},{1,3},{2,0},{3,1},{4,6},{5,7},{6,4},{7,5},{8,10},{9,11},{10,... | collective-permute-start | bytes 786440 | tf_op jit(solution)/shard_map/ppermute | solution.py:338
  63.1 0.3 collective-permute-start.15
  63.4 3.7 %collective-permute-done.11.refs_2_.refs_3_ = bf16[8,32,1024]{2,1,0:T(8,128)(2,1)S(1)} collective-permute-done((bf16[8,32,1024]{2,1,0:T(8,128)(2,1)S(1)}, bf16[8,32,1024]{2,1,0:T(8,128)(2,1)S(1)}, u32[]{:S(2)}, u32[]{:S(2)}) %collective-permute-start.11) | collective-permute-done | bytes 524320 | tf_op jit(solution)/shard_map/ppermute | solution.py:346
  67.1 1.7 %collective-permute-done.10.refs_1_.refs_2_ = bf16[8,32,1024]{2,1,0:T(8,128)(2,1)S(1)} collective-permute-done((bf16[8,32,1024]{2,1,0:T(8,128)(2,1)S(1)}, bf16[8,32,1024]{2,1,0:T(8,128)(2,1)S(1)}, u32[]{:S(2)}, u32[]{:S(2)}) %collective-permute-start.10) | collective-permute-done | bytes 524320 | tf_op jit(solution)/shard_map/ppermute | solution.py:346
  68.9 0.1 collective-permute-start.13
  69.0 1.2 collective-permute-done.18.refs_10_.refs_8_
  70.2 0.7 collective-permute-start.12
  70.9 1.1 collective-permute-start.19
  72.0 5.7 %collective-permute-done.13.refs_4_.refs_5_ = bf16[4,32,1024]{2,1,0:T(8,128)(2,1)S(1)} collective-permute-done((bf16[4,32,1024]{2,1,0:T(8,128)(2,1)S(1)}, bf16[4,32,1024]{2,1,0:T(8,128)(2,1)S(1)}, u32[]{:S(2)}, u32[]{:S(2)}) %collective-permute-start.13) | collective-permute-done | bytes 262176 | tf_op jit(solution)/shard_map/ppermute | solution.py:349
  77.7 1.3 collective-permute-done.12.refs_3_.refs_4_
  79.0 3.3 %products.2 = (bf16[2,2,128,512]{3,2,1,0:T(8,128)(2,1)S(1)}, bf16[2,2,128,512]{3,2,1,0:T(8,128)(2,1)S(1)}, bf16[2,2,128,512]{3,2,1,0:T(8,128)(2,1)S(1)}, bf16[2,...) custom-call(bf16[8,32,1024]{2,1,0:T(8,128)(2,1)S(1)} %column.1.refs_0_.refs_1_, ...), custom_call_target="tpu_custom_call" | custom-call | flops 1 | bytes 1 | tf_op jit(solution)/shard_map/products/pallas_call | solution.py:319
  82.3 1.6 %collective-permute-start.25 = (bf16[2,2,128,512]{3,2,1,0:T(8,128)(2,1)S(1)}, bf16[2,2,128,512]{3,2,1,0:T(8,128)(2,1)S(1)}, u32[]{:S(2)}, u32[]{:S(2)}) collective-permute-start(bf16[2,2,128,512]{3,2,1,0:T(8,128)(2,1)S(1)} %get-tuple-element.106), channel_id=1, source_target_pairs={{0,192},{16,208},{32,224},{48,240},{64,128},{80,144},{96,160},{112... | collective-permute-start | bytes 1572872 | tf_op jit(solution)/shard_map/ppermute | solution.py:363
  84.0 0.5 collective-permute-done.19.refs_9_
  84.5 0.5 collective-permute-start.23
  85.0 0.5 collective-permute-done.21.refs_11_
  85.5 0.5 collective-permute-done.22.refs_12_
  86.0 0.4 collective-permute-done.23.refs_13_
  86.4 3.8 %products.3 = (bf16[2,2,128,512]{3,2,1,0:T(8,128)(2,1)S(1)}, bf16[2,2,128,512]{3,2,1,0:T(8,128)(2,1)S(1)}, bf16[2,2,128,512]{3,2,1,0:T(8,128)(2,1)S(1)}, bf16[2,...) custom-call(s32[14]{0:T(128)S(1)} %copy-done.8, bf16[8,32,1024]{2,1,0:T(8,128)(2,1)S(1)} %column.1.refs_0_.refs_1_, ...), custom_call_target="tpu_custom_call" | custom-call | flops 1 | bytes 1 | tf_op jit(solution)/shard_map/products/pallas_call | solution.py:319
  90.2 4.4 %collective-permute-done.24 = bf16[2,2,128,512]{3,2,1,0:T(8,128)(2,1)S(1)} collective-permute-done((bf16[2,2,128,512]{3,2,1,0:T(8,128)(2,1)S(1)}, bf16[2,2,128,512]{3,2,1,0:T(8,128)(2,1)S(1)}, u32[]{:S(2)}, u32[]{:S(2)}) %collective-permute-start.24) | collective-permute-done | bytes 524320 | tf_op jit(solution)/shard_map/ppermute | solution.py:362
  94.6 0.1 fusion.6
  94.7 1.5 %collective-permute-done.25 = bf16[2,2,128,512]{3,2,1,0:T(8,128)(2,1)S(1)} collective-permute-done((bf16[2,2,128,512]{3,2,1,0:T(8,128)(2,1)S(1)}, bf16[2,2,128,512]{3,2,1,0:T(8,128)(2,1)S(1)}, u32[]{:S(2)}, u32[]{:S(2)}) %collective-permute-start.25) | collective-permute-done | bytes 524320 | tf_op jit(solution)/shard_map/ppermute | solution.py:363
  96.3 1.4 %collective-permute-start.26 = (bf16[2,128,512]{2,1,0:T(8,128)(2,1)S(1)}, bf16[2,128,512]{2,1,0:T(8,128)(2,1)S(1)}, u32[]{:S(2)}, u32[]{:S(2)}) collective-permute-start(bf16[2,128,512]{2,1,0:T(8,128)(2,1)S(1)} %fusion.6), channel_id=1, source_target_pairs={{0,192},{16,208},{32,224},{48,240},{64,128},{80,144},{96,160},{112... | collective-permute-start | bytes 786440 | tf_op jit(solution)/shard_map/ppermute | solution.py:369
  97.7 2.0 %collective-permute-start.29 = (bf16[2,2,128,512]{3,2,1,0:T(8,128)(2,1)S(1)}, bf16[2,2,128,512]{3,2,1,0:T(8,128)(2,1)S(1)}, u32[]{:S(2)}, u32[]{:S(2)}) collective-permute-start(bf16[2,2,128,512]{3,2,1,0:T(8,128)(2,1)S(1)} %get-tuple-element.114), channel_id=1, source_target_pairs={{0,64},{16,80},{32,96},{48,112},{64,0},{80,16},{96,32},{112,48},{1... | collective-permute-start | bytes 1572872 | tf_op jit(solution)/shard_map/ppermute | solution.py:362
  99.7 1.9 %collective-permute-start.31 = (bf16[2,2,128,512]{3,2,1,0:T(8,128)(2,1)S(1)}, bf16[2,2,128,512]{3,2,1,0:T(8,128)(2,1)S(1)}, u32[]{:S(2)}, u32[]{:S(2)}) collective-permute-start(bf16[2,2,128,512]{3,2,1,0:T(8,128)(2,1)S(1)} %get-tuple-element.116), channel_id=1, source_target_pairs={{0,192},{16,208},{32,224},{48,240},{64,128},{80,144},{96,160},{112... | collective-permute-start | bytes 1572872 | tf_op jit(solution)/shard_map/ppermute | solution.py:363
  101.6 5.2 %collective-permute-done.26 = bf16[2,128,512]{2,1,0:T(8,128)(2,1)S(1)} collective-permute-done((bf16[2,128,512]{2,1,0:T(8,128)(2,1)S(1)}, bf16[2,128,512]{2,1,0:T(8,128)(2,1)S(1)}, u32[]{:S(2)}, u32[]{:S(2)}) %collective-permute-start.26) | collective-permute-done | bytes 262176 | tf_op jit(solution)/shard_map/ppermute | solution.py:369
  106.8 0.1 bitcast_add_fusion.4
  106.9 0.1 bitcast_add_fusion.3
  107.1 5.7 %collective-permute-start.28 = (bf16[128,1024]{1,0:T(8,128)(2,1)S(1)}, bf16[128,1024]{1,0:T(8,128)(2,1)S(1)}, u32[]{:S(2)}, u32[]{:S(2)}) collective-permute-start(bf16[128,1024]{1,0:T(8,128)(2,1)S(1)} %fusion.10), channel_id=1, source_target_pairs={{0,32},{16,48},{32,0},{48,16},{64,96},{80,112},{96,64},{112,80},{1... | collective-permute-start | bytes 786440 | tf_op jit(solution)/shard_map/ppermute | solution.py:375
  112.8 1.7 %collective-permute-done.29 = bf16[2,2,128,512]{3,2,1,0:T(8,128)(2,1)S(1)} collective-permute-done((bf16[2,2,128,512]{3,2,1,0:T(8,128)(2,1)S(1)}, bf16[2,2,128,512]{3,2,1,0:T(8,128)(2,1)S(1)}, u32[]{:S(2)}, u32[]{:S(2)}) %collective-permute-start.29) | collective-permute-done | bytes 524320 | tf_op jit(solution)/shard_map/ppermute | solution.py:362
  114.6 2.2 %collective-permute-start.30 = (bf16[2,128,512]{2,1,0:T(8,128)(2,1)S(1)}, bf16[2,128,512]{2,1,0:T(8,128)(2,1)S(1)}, u32[]{:S(2)}, u32[]{:S(2)}) collective-permute-start(bf16[2,128,512]{2,1,0:T(8,128)(2,1)S(1)} %fusion.8), channel_id=1, source_target_pairs={{0,192},{16,208},{32,224},{48,240},{64,128},{80,144},{96,160},{112... | collective-permute-start | bytes 786440 | tf_op jit(solution)/shard_map/ppermute | solution.py:369
  116.9 0.1 collective-permute-start.32
  117.0 2.5 %collective-permute-done.28 = bf16[128,1024]{1,0:T(8,128)(2,1)S(1)} collective-permute-done((bf16[128,1024]{1,0:T(8,128)(2,1)S(1)}, bf16[128,1024]{1,0:T(8,128)(2,1)S(1)}, u32[]{:S(2)}, u32[]{:S(2)}) %collective-permute-start.28) | collective-permute-done | bytes 262176 | tf_op jit(solution)/shard_map/ppermute | solution.py:375
  119.6 2.7 %collective-permute-done.30 = bf16[2,128,512]{2,1,0:T(8,128)(2,1)S(1)} collective-permute-done((bf16[2,128,512]{2,1,0:T(8,128)(2,1)S(1)}, bf16[2,128,512]{2,1,0:T(8,128)(2,1)S(1)}, u32[]{:S(2)}, u32[]{:S(2)}) %collective-permute-start.30) | collective-permute-done | bytes 262176 | tf_op jit(solution)/shard_map/ppermute | solution.py:369
  122.2 0.1 bitcast_add_fusion.2
  122.3 1.0 collective-permute-done.32
  123.3 0.1 bitcast_add_fusion.1
  123.4 0.1 pad_maximum_fusion
  123.5 5.4 %collective-permute-start.33 = (bf16[128,1024]{1,0:T(8,128)(2,1)S(1)}, bf16[128,1024]{1,0:T(8,128)(2,1)S(1)}, u32[]{:S(2)}, u32[]{:S(2)}) collective-permute-start(bf16[128,1024]{1,0:T(8,128)(2,1)S(1)} %fusion.11), channel_id=1, source_target_pairs={{0,32},{16,48},{32,0},{48,16},{64,96},{80,112},{96,64},{112,80},{1... | collective-permute-start | bytes 786440 | tf_op jit(solution)/shard_map/ppermute | solution.py:375
  129.0 7.7 %collective-permute-done.33 = bf16[128,1024]{1,0:T(8,128)(2,1)S(1)} collective-permute-done((bf16[128,1024]{1,0:T(8,128)(2,1)S(1)}, bf16[128,1024]{1,0:T(8,128)(2,1)S(1)}, u32[]{:S(2)}, u32[]{:S(2)}) %collective-permute-start.33) | collective-permute-done | bytes 262176 | tf_op jit(solution)/shard_map/ppermute | solution.py:375
  136.7 1.0 convolution_convert_fusion
  (59 shorter events, 0.7 us)
Async XLA Ops:
  4.3 8.9 %copy-start.10 = (bf16[8192]{0:T(1024)(128)(2,1)S(1)}, bf16[8192]{0:T(1024)(128)(2,1)}, u32[]{:S(2)}) copy-start(bf16[8192]{0:T(1024)(128)(2,1)} %param.31) | copy-start | bytes 49156
  4.3 9.1 %copy-start = (bf16[2,128,1024]{2,1,0:T(8,128)(2,1)S(1)}, bf16[2,128,1024]{2,1,0:T(8,128)(2,1)}, u32[]{:S(2)}) copy-start(bf16[2,128,1024]{2,1,0:T(8,128)(2,1)} %old_k_ref.1) | copy-start | bytes 1572868
  4.3 9.1 %copy-start.1 = (bf16[2,128,1024]{2,1,0:T(8,128)(2,1)S(1)}, bf16[2,128,1024]{2,1,0:T(8,128)(2,1)}, u32[]{:S(2)}) copy-start(bf16[2,128,1024]{2,1,0:T(8,128)(2,1)} %old_v_ref.1) | copy-start | bytes 1572868
  4.3 9.1 %copy-start.5 = (bf16[4,2,1024]{2,1,0:T(2,128)(2,1)S(1)}, bf16[4,2,1024]{2,1,0:T(2,128)(2,1)}, u32[]{:S(2)}) copy-start(bf16[4,2,1024]{2,1,0:T(2,128)(2,1)} %new_k_ref.1) | copy-start | bytes 49156
  4.3 9.1 %copy-start.6 = (bf16[4,2,1024]{2,1,0:T(2,128)(2,1)S(1)}, bf16[4,2,1024]{2,1,0:T(2,128)(2,1)}, u32[]{:S(2)}) copy-start(bf16[4,2,1024]{2,1,0:T(2,128)(2,1)} %new_v_ref.1) | copy-start | bytes 49156
  4.4 51.9 %all-to-all-start = ((bf16[16,32,1024]{2,1,0:T(8,128)(2,1)}), bf16[16,32,1024]{2,1,0:T(8,128)(2,1)S(1)}, u32[]{:S(2)}, u32[]{:S(2)}) async-start(bf16[16,32,1024]{2,1,0:T(8,128)(2,1)} %adam_places.1), calls=%async_computation | async-start | bytes 2097152 | tf_op jit(solution)/shard_map/all_to_all | solution.py:414
  13.2 0.9 copy-start.4
  13.2 1.0 copy-start.3
  13.3 0.8 copy-start.9
  14.1 3.7 %copy-start.7 = (s32[14]{0:T(128)}, s32[14]{0:T(128)S(1)}, u32[]{:S(2)}) copy-start(s32[14]{0:T(128)S(1)} %stack.59.to_ref.refs_0_) | copy-start | bytes 172
  22.8 23.7 %copy-start.11 = (bf16[4,32,1024]{2,1,0:T(8,128)(2,1)S(1)}, bf16[4,32,1024]{2,1,0:T(8,128)(2,1)}, u32[]{:S(2)}) copy-start(bf16[4,32,1024]{2,1,0:T(8,128)(2,1)} %get-tuple-element.84) | copy-start | bytes 786436
  22.8 4.3 %collective-permute-start = (bf16[2,8,1024]{2,1,0:T(8,128)(2,1)S(1)}, bf16[2,8,1024]{2,1,0:T(8,128)(2,1)S(1)}, u32[]{:S(2)}, u32[]{:S(2)}) collective-permute-start(bf16[2,8,1024]{2,1,0:T(8,128)(2,1)S(1)} %get-tuple-element.76), channel_id=1, source_target_pairs={{0,64},{16,80},{32,96},{48,112},{64,0},{80,16},{96,32},{112,48},{1... | collective-permute-start | bytes 98312 | tf_op jit(solution)/shard_map/ppermute | solution.py:425
  24.4 5.5 %collective-permute-start.1 = (bf16[2,8,1024]{2,1,0:T(8,128)(2,1)S(1)}, bf16[2,8,1024]{2,1,0:T(8,128)(2,1)S(1)}, u32[]{:S(2)}, u32[]{:S(2)}) collective-permute-start(bf16[2,8,1024]{2,1,0:T(8,128)(2,1)S(1)} %get-tuple-element.77), channel_id=1, source_target_pairs={{0,192},{16,208},{32,224},{48,240},{64,128},{80,144},{96,160},{112... | collective-permute-start | bytes 98312 | tf_op jit(solution)/shard_map/ppermute | solution.py:425
  26.5 5.4 %collective-permute-start.2 = (bf16[2,8,1024]{2,1,0:T(8,128)(2,1)S(1)}, bf16[2,8,1024]{2,1,0:T(8,128)(2,1)S(1)}, u32[]{:S(2)}, u32[]{:S(2)}) collective-permute-start(bf16[2,8,1024]{2,1,0:T(8,128)(2,1)S(1)} %get-tuple-element.78), channel_id=1, source_target_pairs={{0,128},{16,144},{32,160},{48,176},{64,192},{80,208},{96,224},{112... | collective-permute-start | bytes 98312 | tf_op jit(solution)/shard_map/ppermute | solution.py:425
  31.9 8.6 %collective-permute-start.3 = (bf16[4,8,1024]{2,1,0:T(8,128)(2,1)S(1)}, bf16[4,8,1024]{2,1,0:T(8,128)(2,1)S(1)}, u32[]{:S(2)}, u32[]{:S(2)}) collective-permute-start(bf16[4,8,1024]{2,1,0:T(8,128)(2,1)S(1)} %get-tuple-element.80), channel_id=1, source_target_pairs={{0,32},{16,48},{32,0},{48,16},{64,96},{80,112},{96,64},{112,80},{1... | collective-permute-start | bytes 196616 | tf_op jit(solution)/shard_map/ppermute | solution.py:427
  40.6 19.1 %copy-start.2 = (bf16[4,32,1024]{2,1,0:T(8,128)(2,1)S(1)}, bf16[4,32,1024]{2,1,0:T(8,128)(2,1)}, u32[]{:S(2)}) copy-start(bf16[4,32,1024]{2,1,0:T(8,128)(2,1)} %get-tuple-element.88.refs_0_) | copy-start | bytes 786436
  40.6 9.4 %collective-permute-start.6 = (bf16[8,8,1024]{2,1,0:T(8,128)(2,1)S(1)}, bf16[8,8,1024]{2,1,0:T(8,128)(2,1)S(1)}, u32[]{:S(2)}, u32[]{:S(2)}) collective-permute-start(bf16[8,8,1024]{2,1,0:T(8,128)(2,1)S(1)} %interleave.1.refs_0_), channel_id=1, source_target_pairs={{0,3},{1,2},{2,1},{3,0},{4,7},{5,6},{6,5},{7,4},{8,11},{9,10},{10,... | collective-permute-start | bytes 393224 | tf_op jit(solution)/shard_map/ppermute | solution.py:338
  43.7 11.3 %collective-permute-start.7 = (bf16[4,32,1024]{2,1,0:T(8,128)(2,1)}, bf16[4,32,1024]{2,1,0:T(8,128)(2,1)S(1)}, u32[]{:S(2)}, u32[]{:S(2)}) collective-permute-start(bf16[4,32,1024]{2,1,0:T(8,128)(2,1)} %get-tuple-element.82), channel_id=1, source_target_pairs={{0,4},{1,5},{2,6},{3,7},{4,0},{5,1},{6,2},{7,3},{8,12},{9,13},{10,... | collective-permute-start | bytes 786440 | tf_op jit(solution)/shard_map/ppermute | solution.py:342
  45.3 11.0 %collective-permute-start.8 = (bf16[4,32,1024]{2,1,0:T(8,128)(2,1)}, bf16[4,32,1024]{2,1,0:T(8,128)(2,1)S(1)}, u32[]{:S(2)}, u32[]{:S(2)}) collective-permute-start(bf16[4,32,1024]{2,1,0:T(8,128)(2,1)} %get-tuple-element.83), channel_id=1, source_target_pairs={{0,12},{1,13},{2,14},{3,15},{4,8},{5,9},{6,10},{7,11},{8,4},{9,5},... | collective-permute-start | bytes 786440 | tf_op jit(solution)/shard_map/ppermute | solution.py:342
  46.5 9.7 %collective-permute-start.9 = (bf16[4,32,1024]{2,1,0:T(8,128)(2,1)S(1)}, bf16[4,32,1024]{2,1,0:T(8,128)(2,1)S(1)}, u32[]{:S(2)}, u32[]{:S(2)}) collective-permute-start(bf16[4,32,1024]{2,1,0:T(8,128)(2,1)S(1)} %copy-done.11), channel_id=1, source_target_pairs={{0,8},{1,9},{2,10},{3,11},{4,12},{5,13},{6,14},{7,15},{8,0},{9,1},... | collective-permute-start | bytes 786440 | tf_op jit(solution)/shard_map/ppermute | solution.py:342
  48.0 6.0 %collective-permute-start.5 = (bf16[8,8,1024]{2,1,0:T(8,128)(2,1)S(1)}, bf16[8,8,1024]{2,1,0:T(8,128)(2,1)S(1)}, u32[]{:S(2)}, u32[]{:S(2)}) collective-permute-start(bf16[8,8,1024]{2,1,0:T(8,128)(2,1)S(1)} %interleave.1.refs_0_), channel_id=1, source_target_pairs={{0,2},{1,3},{2,0},{3,1},{4,6},{5,7},{6,4},{7,5},{8,10},{9,11},{10,... | collective-permute-start | bytes 393224 | tf_op jit(solution)/shard_map/ppermute | solution.py:338
  50.0 5.0 %collective-permute-start.4 = (bf16[8,8,1024]{2,1,0:T(8,128)(2,1)S(1)}, bf16[8,8,1024]{2,1,0:T(8,128)(2,1)S(1)}, u32[]{:S(2)}, u32[]{:S(2)}) collective-permute-start(bf16[8,8,1024]{2,1,0:T(8,128)(2,1)S(1)} %interleave.1.refs_0_), channel_id=1, source_target_pairs={{0,1},{1,0},{2,3},{3,2},{4,5},{5,4},{6,7},{7,6},{8,9},{9,8},{10,11... | collective-permute-start | bytes 393224 | tf_op jit(solution)/shard_map/ppermute | solution.py:338
  56.2 10.8 %collective-permute-start.11 = (bf16[8,32,1024]{2,1,0:T(8,128)(2,1)S(1)}, bf16[8,32,1024]{2,1,0:T(8,128)(2,1)S(1)}, u32[]{:S(2)}, u32[]{:S(2)}) collective-permute-start(bf16[8,32,1024]{2,1,0:T(8,128)(2,1)S(1)} %column.1.refs_0_.refs_1_), channel_id=1, source_target_pairs={{0,12},{1,13},{2,14},{3,15},{4,8},{5,9},{6,10},{7,11},{8,4},{9,5},... | collective-permute-start | bytes 1572872 | tf_op jit(solution)/shard_map/ppermute | solution.py:346
  59.6 9.2 %collective-permute-start.10 = (bf16[8,32,1024]{2,1,0:T(8,128)(2,1)S(1)}, bf16[8,32,1024]{2,1,0:T(8,128)(2,1)S(1)}, u32[]{:S(2)}, u32[]{:S(2)}) collective-permute-start(bf16[8,32,1024]{2,1,0:T(8,128)(2,1)S(1)} %column.1.refs_0_.refs_1_), channel_id=1, source_target_pairs={{0,4},{1,5},{2,6},{3,7},{4,0},{5,1},{6,2},{7,3},{8,12},{9,13},{10,... | collective-permute-start | bytes 1572872 | tf_op jit(solution)/shard_map/ppermute | solution.py:346
  59.7 9.2 %collective-permute-start.17 = (bf16[4,32,1024]{2,1,0:T(8,128)(2,1)S(1)}, bf16[4,32,1024]{2,1,0:T(8,128)(2,1)S(1)}, u32[]{:S(2)}, u32[]{:S(2)}) collective-permute-start(bf16[4,32,1024]{2,1,0:T(8,128)(2,1)S(1)} %get-tuple-element.92), channel_id=1, source_target_pairs={{0,1},{1,0},{2,3},{3,2},{4,5},{5,4},{6,7},{7,6},{8,9},{9,8},{10,11... | collective-permute-start | bytes 786440 | tf_op jit(solution)/shard_map/ppermute | solution.py:338
  59.8 10.4 %collective-permute-start.18 = (bf16[4,32,1024]{2,1,0:T(8,128)(2,1)S(1)}, bf16[4,32,1024]{2,1,0:T(8,128)(2,1)S(1)}, u32[]{:S(2)}, u32[]{:S(2)}) collective-permute-start(bf16[4,32,1024]{2,1,0:T(8,128)(2,1)S(1)} %get-tuple-element.93), channel_id=1, source_target_pairs={{0,2},{1,3},{2,0},{3,1},{4,6},{5,7},{6,4},{7,5},{8,10},{9,11},{10,... | collective-permute-start | bytes 786440 | tf_op jit(solution)/shard_map/ppermute | solution.py:338
  63.1 8.9 %collective-permute-start.15 = (bf16[176,1024]{1,0:T(8,128)(2,1)S(1)}, bf16[176,1024]{1,0:T(8,128)(2,1)S(1)}, u32[]{:S(2)}, u32[]{:S(2)}) collective-permute-start(bf16[176,1024]{1,0:T(8,128)(2,1)S(1)} %get-tuple-element.119), channel_id=1, source_target_pairs={{0,16},{16,0},{32,48},{48,32},{64,80},{80,64},{96,112},{112,96},{1... | collective-permute-start | bytes 1081352 | tf_op jit(solution)/shard_map/ppermute | solution.py:356
  67.1 4.9 %collective-permute-start.14 = (bf16[176,1024]{1,0:T(8,128)(2,1)S(1)}, bf16[176,1024]{1,0:T(8,128)(2,1)S(1)}, u32[]{:S(2)}, u32[]{:S(2)}) collective-permute-start(bf16[176,1024]{1,0:T(8,128)(2,1)S(1)} %get-tuple-element.120), channel_id=1, source_target_pairs={{0,16},{16,0},{32,48},{48,32},{64,80},{80,64},{96,112},{112,96},{1... | collective-permute-start | bytes 1081352 | tf_op jit(solution)/shard_map/ppermute | solution.py:356
  68.8 2.1 %collective-permute-start.16 = (bf16[160,1024]{1,0:T(8,128)(2,1)S(1)}, bf16[160,1024]{1,0:T(8,128)(2,1)S(1)}, u32[]{:S(2)}, u32[]{:S(2)}) collective-permute-start(bf16[160,1024]{1,0:T(8,128)(2,1)S(1)} %split.11), channel_id=1, source_target_pairs={{0,16},{16,0},{32,48},{48,32},{64,80},{80,64},{96,112},{112,96},{1... | collective-permute-start | bytes 983048 | tf_op jit(solution)/shard_map/ppermute | solution.py:356
  68.9 8.8 %collective-permute-start.13 = (bf16[4,32,1024]{2,1,0:T(8,128)(2,1)S(1)}, bf16[4,32,1024]{2,1,0:T(8,128)(2,1)S(1)}, u32[]{:S(2)}, u32[]{:S(2)}) collective-permute-start(bf16[4,32,1024]{2,1,0:T(8,128)(2,1)S(1)} %slice.91), channel_id=1, source_target_pairs={{0,4},{1,5},{2,6},{3,7},{4,0},{5,1},{6,2},{7,3},{8,12},{9,13},{10,... | collective-permute-start | bytes 786440 | tf_op jit(solution)/shard_map/ppermute | solution.py:349
  70.2 8.8 %collective-permute-start.12 = (bf16[4,32,1024]{2,1,0:T(8,128)(2,1)S(1)}, bf16[4,32,1024]{2,1,0:T(8,128)(2,1)S(1)}, u32[]{:S(2)}, u32[]{:S(2)}) collective-permute-start(bf16[4,32,1024]{2,1,0:T(8,128)(2,1)S(1)} %slice.90), channel_id=1, source_target_pairs={{0,12},{1,13},{2,14},{3,15},{4,8},{5,9},{6,10},{7,11},{8,4},{9,5},... | collective-permute-start | bytes 786440 | tf_op jit(solution)/shard_map/ppermute | solution.py:348
  70.9 13.6 %collective-permute-start.19 = (bf16[4,32,1024]{2,1,0:T(8,128)(2,1)S(1)}, bf16[4,32,1024]{2,1,0:T(8,128)(2,1)S(1)}, u32[]{:S(2)}, u32[]{:S(2)}) collective-permute-start(bf16[4,32,1024]{2,1,0:T(8,128)(2,1)S(1)} %get-tuple-element.95), channel_id=1, source_target_pairs={{0,3},{1,2},{2,1},{3,0},{4,7},{5,6},{6,5},{7,4},{8,11},{9,10},{10,... | collective-permute-start | bytes 786440 | tf_op jit(solution)/shard_map/ppermute | solution.py:338
  72.0 12.5 %collective-permute-start.20 = (bf16[4,32,1024]{2,1,0:T(8,128)(2,1)S(1)}, bf16[4,32,1024]{2,1,0:T(8,128)(2,1)S(1)}, u32[]{:S(2)}, u32[]{:S(2)}) collective-permute-start(bf16[4,32,1024]{2,1,0:T(8,128)(2,1)S(1)} %get-tuple-element.99.refs_6_), channel_id=1, source_target_pairs={{0,16},{16,0},{32,48},{48,32},{64,80},{80,64},{96,112},{112,96},{1... | collective-permute-start | bytes 786440 | tf_op jit(solution)/shard_map/ppermute | solution.py:356
  82.3 12.3 %collective-permute-start.24 = (bf16[2,2,128,512]{3,2,1,0:T(8,128)(2,1)S(1)}, bf16[2,2,128,512]{3,2,1,0:T(8,128)(2,1)S(1)}, u32[]{:S(2)}, u32[]{:S(2)}) collective-permute-start(bf16[2,2,128,512]{3,2,1,0:T(8,128)(2,1)S(1)} %get-tuple-element.104), channel_id=1, source_target_pairs={{0,64},{16,80},{32,96},{48,112},{64,0},{80,16},{96,32},{112,48},{1... | collective-permute-start | bytes 1572872 | tf_op jit(solution)/shard_map/ppermute | solution.py:362
  82.3 4.1 %copy-start.8 = (s32[14]{0:T(128)S(1)}, s32[14]{0:T(128)}, u32[]{:S(2)}) copy-start(s32[14]{0:T(128)} %copy-done.7) | copy-start | bytes 172
  82.3 13.8 %collective-permute-start.25 = (bf16[2,2,128,512]{3,2,1,0:T(8,128)(2,1)S(1)}, bf16[2,2,128,512]{3,2,1,0:T(8,128)(2,1)S(1)}, u32[]{:S(2)}, u32[]{:S(2)}) collective-permute-start(bf16[2,2,128,512]{3,2,1,0:T(8,128)(2,1)S(1)} %get-tuple-element.106), channel_id=1, source_target_pairs={{0,192},{16,208},{32,224},{48,240},{64,128},{80,144},{96,160},{112... | collective-permute-start | bytes 1572872 | tf_op jit(solution)/shard_map/ppermute | solution.py:363
  84.0 1.5 %collective-permute-start.21 = (bf16[4,32,1024]{2,1,0:T(8,128)(2,1)S(1)}, bf16[4,32,1024]{2,1,0:T(8,128)(2,1)S(1)}, u32[]{:S(2)}, u32[]{:S(2)}) collective-permute-start(bf16[4,32,1024]{2,1,0:T(8,128)(2,1)S(1)} %collective-permute-done.17.refs_9_.refs_7_), channel_id=1, source_target_pairs={{0,16},{16,0},{32,48},{48,32},{64,80},{80,64},{96,112},{112,96},{1... | collective-permute-start | bytes 786440 | tf_op jit(solution)/shard_map/ppermute | solution.py:356
  84.5 1.5 %collective-permute-start.22 = (bf16[4,32,1024]{2,1,0:T(8,128)(2,1)S(1)}, bf16[4,32,1024]{2,1,0:T(8,128)(2,1)S(1)}, u32[]{:S(2)}, u32[]{:S(2)}) collective-permute-start(bf16[4,32,1024]{2,1,0:T(8,128)(2,1)S(1)} %collective-permute-done.18.refs_10_.refs_8_), channel_id=1, source_target_pairs={{0,16},{16,0},{32,48},{48,32},{64,80},{80,64},{96,112},{112,96},{1... | collective-permute-start | bytes 786440 | tf_op jit(solution)/shard_map/ppermute | solution.py:356
  84.5 1.9 %collective-permute-start.23 = (bf16[4,32,1024]{2,1,0:T(8,128)(2,1)S(1)}, bf16[4,32,1024]{2,1,0:T(8,128)(2,1)S(1)}, u32[]{:S(2)}, u32[]{:S(2)}) collective-permute-start(bf16[4,32,1024]{2,1,0:T(8,128)(2,1)S(1)} %collective-permute-done.19.refs_9_), channel_id=1, source_target_pairs={{0,16},{16,0},{32,48},{48,32},{64,80},{80,64},{96,112},{112,96},{1... | collective-permute-start | bytes 786440 | tf_op jit(solution)/shard_map/ppermute | solution.py:356
  96.3 10.5 %collective-permute-start.26 = (bf16[2,128,512]{2,1,0:T(8,128)(2,1)S(1)}, bf16[2,128,512]{2,1,0:T(8,128)(2,1)S(1)}, u32[]{:S(2)}, u32[]{:S(2)}) collective-permute-start(bf16[2,128,512]{2,1,0:T(8,128)(2,1)S(1)} %fusion.6), channel_id=1, source_target_pairs={{0,192},{16,208},{32,224},{48,240},{64,128},{80,144},{96,160},{112... | collective-permute-start | bytes 786440 | tf_op jit(solution)/shard_map/ppermute | solution.py:369
  97.7 9.2 %collective-permute-start.27 = (bf16[2,128,512]{2,1,0:T(8,128)(2,1)S(1)}, bf16[2,128,512]{2,1,0:T(8,128)(2,1)S(1)}, u32[]{:S(2)}, u32[]{:S(2)}) collective-permute-start(bf16[2,128,512]{2,1,0:T(8,128)(2,1)S(1)} %fusion.7), channel_id=1, source_target_pairs={{0,64},{16,80},{32,96},{48,112},{64,0},{80,16},{96,32},{112,48},{1... | collective-permute-start | bytes 786440 | tf_op jit(solution)/shard_map/ppermute | solution.py:370
  97.7 16.8 %collective-permute-start.29 = (bf16[2,2,128,512]{3,2,1,0:T(8,128)(2,1)S(1)}, bf16[2,2,128,512]{3,2,1,0:T(8,128)(2,1)S(1)}, u32[]{:S(2)}, u32[]{:S(2)}) collective-permute-start(bf16[2,2,128,512]{3,2,1,0:T(8,128)(2,1)S(1)} %get-tuple-element.114), channel_id=1, source_target_pairs={{0,64},{16,80},{32,96},{48,112},{64,0},{80,16},{96,32},{112,48},{1... | collective-permute-start | bytes 1572872 | tf_op jit(solution)/shard_map/ppermute | solution.py:362
  99.7 17.1 %collective-permute-start.31 = (bf16[2,2,128,512]{3,2,1,0:T(8,128)(2,1)S(1)}, bf16[2,2,128,512]{3,2,1,0:T(8,128)(2,1)S(1)}, u32[]{:S(2)}, u32[]{:S(2)}) collective-permute-start(bf16[2,2,128,512]{3,2,1,0:T(8,128)(2,1)S(1)} %get-tuple-element.116), channel_id=1, source_target_pairs={{0,192},{16,208},{32,224},{48,240},{64,128},{80,144},{96,160},{112... | collective-permute-start | bytes 1572872 | tf_op jit(solution)/shard_map/ppermute | solution.py:363
  107.1 12.4 %collective-permute-start.28 = (bf16[128,1024]{1,0:T(8,128)(2,1)S(1)}, bf16[128,1024]{1,0:T(8,128)(2,1)S(1)}, u32[]{:S(2)}, u32[]{:S(2)}) collective-permute-start(bf16[128,1024]{1,0:T(8,128)(2,1)S(1)} %fusion.10), channel_id=1, source_target_pairs={{0,32},{16,48},{32,0},{48,16},{64,96},{80,112},{96,64},{112,80},{1... | collective-permute-start | bytes 786440 | tf_op jit(solution)/shard_map/ppermute | solution.py:375
  114.6 7.7 %collective-permute-start.30 = (bf16[2,128,512]{2,1,0:T(8,128)(2,1)S(1)}, bf16[2,128,512]{2,1,0:T(8,128)(2,1)S(1)}, u32[]{:S(2)}, u32[]{:S(2)}) collective-permute-start(bf16[2,128,512]{2,1,0:T(8,128)(2,1)S(1)} %fusion.8), channel_id=1, source_target_pairs={{0,192},{16,208},{32,224},{48,240},{64,128},{80,144},{96,160},{112... | collective-permute-start | bytes 786440 | tf_op jit(solution)/shard_map/ppermute | solution.py:369
  116.9 6.5 %collective-permute-start.32 = (bf16[2,128,512]{2,1,0:T(8,128)(2,1)S(1)}, bf16[2,128,512]{2,1,0:T(8,128)(2,1)S(1)}, u32[]{:S(2)}, u32[]{:S(2)}) collective-permute-start(bf16[2,128,512]{2,1,0:T(8,128)(2,1)S(1)} %fusion.9), channel_id=1, source_target_pairs={{0,64},{16,80},{32,96},{48,112},{64,0},{80,16},{96,32},{112,48},{1... | collective-permute-start | bytes 786440 | tf_op jit(solution)/shard_map/ppermute | solution.py:370
  123.5 13.2 %collective-permute-start.33 = (bf16[128,1024]{1,0:T(8,128)(2,1)S(1)}, bf16[128,1024]{1,0:T(8,128)(2,1)S(1)}, u32[]{:S(2)}, u32[]{:S(2)}) collective-permute-start(bf16[128,1024]{1,0:T(8,128)(2,1)S(1)} %fusion.11), channel_id=1, source_target_pairs={{0,32},{16,48},{32,0},{48,16},{64,96},{80,112},{96,64},{112,80},{1... | collective-permute-start | bytes 786440 | tf_op jit(solution)/shard_map/ppermute | solution.py:375
